TPU v7x, 32 devices: a whole 2x2x4 slice. The times are simulated.
32 devices in a mesh: rep: 16 (over z, x, core), shard: 2 (over y).
Axes of the slice: x: 2, y: 2, z: 4, core: 2. Of those that a mesh axis runs over, the one named last changes fastest.
Arguments:
- hidden_in: bfloat16 [16384, 1536], P(('rep', 'shard')), may hold values from -6 to 6
- segment_ids: int32 [32, 512], P(('rep', 'shard')), may hold values from 0 to 7, never falling along the last dimension, each value on 1 to 256 neighbouring positions
- routes: int32 [16384, 4], P(('rep', 'shard')), may hold values from 0 to 7, all different within a row; in each aligned block of 512 rows (0 to 511, 512 to 1023, ...) at most 384 rows name the same one
- out_grad: bfloat16 [16384, 1536], P(('rep', 'shard')), may hold values from -6 to 6
- norm1_gain: bfloat16 [1536], P('shard'), may hold values from 0.25 to 1.75
- w_query: bfloat16 [1536, 1536], P('shard'), may hold values from -0.15625 to 0.15625
- key_weight: bfloat16 [1536, 256], P('shard'), may hold values from -0.15625 to 0.15625
- value_weight: bfloat16 [1536, 256], P('shard'), may hold values from -0.15625 to 0.15625
- w_out: bfloat16 [1536, 1536], P('shard'), may hold values from -0.625 to 0.625
- norm2_gain: bfloat16 [1536], P('shard'), may hold values from 0.25 to 1.75
- w_router: bfloat16 [1536, 8], P('shard'), may hold values from -0.078125 to 0.078125
- w_gate: bfloat16 [8, 1536, 768], P(None, 'shard'), may hold values from -0.15625 to 0.15625
- w_up: bfloat16 [8, 1536, 768], P(None, 'shard'), may hold values from -0.15625 to 0.15625
- w_down: bfloat16 [8, 1536, 768], P(None, 'shard'), may hold values from -0.625 to 0.625
Outputs:
- hidden_out: bfloat16 [16384, 1536], P(('rep', 'shard'))
- hidden_grad: bfloat16 [16384, 1536], P(('rep', 'shard'))
- norm1_gain_grad: float32 [1536], P('shard')
- query_grad: float32 [1536, 1536], P('shard')
- key_grad: float32 [1536, 256], P('shard')
- value_grad: float32 [1536, 256], P('shard')
- out_proj_grad: float32 [1536, 1536], P('shard')
- norm2_gain_grad: float32 [1536], P('shard')
- router_grad: float32 [1536, 8], P('shard')
- gate_grad: float32 [8, 1536, 768], P(None, 'shard')
- up_grad: float32 [8, 1536, 768], P(None, 'shard')
- down_grad: float32 [8, 1536, 768], P(None, 'shard')
Inputs may be any that keep to these rules, and one draw needn't show every extreme that they name: `routes`: each row names 4 different experts; in the rows of one device no expert is named more than 384 times, and some expert reaches that count. `segment_ids`: along each sequence the ids never fall, every id appears, each document has 1 to 256 tokens and some document has exactly 256.
All inputs are finite; a program needn't handle non-finite values.
Results may differ from a plain program's by a relative error of at most 0.022.
Values may be sent and summed in bfloat16 or wider, within the bound.
A program may use at most 320 MiB of HBM per device.

v0:
```python
import jax
import jax.numpy as jnp
from jax import lax
from jax.sharding import PartitionSpec as P

MODEL_WIDTH = 1536
QUERY_HEADS = 12
KEY_VALUE_HEADS = 2
HEAD_SIZE = 128
TOPK = 4
CAP = 384


epsilon = 1e-06
rope_base = 1000000.0


def tables(sequence_length, row_width):
    frequency = rope_base ** (-2.0 * jnp.arange(row_width // 2, dtype=jnp.float32) / row_width)
    angles = jnp.arange(sequence_length, dtype=jnp.float32)[:, None] * frequency[None, :]
    angles = jnp.concatenate([angles, angles], axis=-1)
    return (jnp.cos(angles)[:, None, :], jnp.sin(angles)[:, None, :])


def apply_rotary(values, rotary_cosine, rotary_sine):
    half_width = values.shape[-1] // 2
    turned = jnp.concatenate([-values[..., half_width:], values[..., :half_width]], axis=-1)
    return values * rotary_cosine + turned * rotary_sine


def contract(left_side, right_side, left_dim, right_dim):
    return lax.dot_general(
        left_side,
        right_side,
        (((left_dim,), (right_dim,)), ((), ())),
        preferred_element_type=jnp.float32,
    )


def normalize(values, gain_vector):
    scale_rows = lax.rsqrt(jnp.mean(values * values, axis=-1, keepdims=True) + epsilon)
    return (values * scale_rows * gain_vector, scale_rows)


def norm_back(values, scale_rows, gain_vector, upstream):
    scaled = upstream * gain_vector
    gain_grad = jnp.sum(upstream * values * scale_rows, axis=0)
    inner_sum = jnp.sum(scaled * values, axis=-1, keepdims=True)
    return (scaled * scale_rows - values * scale_rows**3 * inner_sum / values.shape[-1], gain_grad)


def softmax_rows(values):
    top_value = jnp.max(values, axis=-1, keepdims=True)
    exp_values = jnp.exp(values - top_value)
    return exp_values / jnp.sum(exp_values, axis=-1, keepdims=True)


def expert_pass(row_block, gate_weight, up_weight, down_weight):
    gate_pre = jnp.einsum(
        "ecd,edf->ecf", row_block, gate_weight, preferred_element_type=jnp.float32
    )
    lift_pre = jnp.einsum("ecd,edf->ecf", row_block, up_weight, preferred_element_type=jnp.float32)
    inner_act = (gate_pre * jax.nn.sigmoid(gate_pre) * lift_pre).astype(jnp.bfloat16)
    output = jnp.einsum(
        "ecf,edf->ecd", inner_act, down_weight, preferred_element_type=jnp.float32
    ).astype(jnp.bfloat16)
    return (output, gate_pre, lift_pre, inner_act)


def expert_back(
    row_block, gate_pre, lift_pre, inner_act, gate_weight, up_weight, down_weight, upstream
):
    inner_grad = jnp.einsum(
        "ecd,edf->ecf", upstream, down_weight, preferred_element_type=jnp.float32
    )
    sigma = jax.nn.sigmoid(gate_pre)
    gate_back = (inner_grad * lift_pre * sigma * (1.0 + gate_pre * (1.0 - sigma))).astype(
        jnp.bfloat16
    )
    lift_back = (inner_grad * gate_pre * sigma).astype(jnp.bfloat16)
    down_sum = jnp.einsum("ecd,ecf->edf", upstream, inner_act, preferred_element_type=jnp.float32)
    gate_sum = jnp.einsum("ecd,ecf->edf", row_block, gate_back, preferred_element_type=jnp.float32)
    up_sum = jnp.einsum("ecd,ecf->edf", row_block, lift_back, preferred_element_type=jnp.float32)
    row_grad = jnp.einsum(
        "ecf,edf->ecd", gate_back, gate_weight, preferred_element_type=jnp.float32
    )
    row_grad = row_grad + jnp.einsum(
        "ecf,edf->ecd", lift_back, up_weight, preferred_element_type=jnp.float32
    )
    return (row_grad.astype(jnp.bfloat16), gate_sum, up_sum, down_sum)


def local(
    hidden_in,
    segment_ids,
    routes,
    out_grad,
    norm1_gain,
    w_query,
    key_weight,
    value_weight,
    w_out,
    norm2_gain,
    w_router,
    w_gate,
    w_up,
    w_down,
):
    sequence_length = hidden_in.shape[0]
    experts = w_gate.shape[0]
    shard_group_width = QUERY_HEADS // KEY_VALUE_HEADS
    head_scale = HEAD_SIZE ** (-0.5)
    gathered = (
        lax.all_gather(norm1_gain, "shard", axis=0, tiled=True),
        lax.all_gather(w_query, "shard", axis=0, tiled=True),
        lax.all_gather(key_weight, "shard", axis=0, tiled=True),
        lax.all_gather(value_weight, "shard", axis=0, tiled=True),
        lax.all_gather(w_out, "shard", axis=0, tiled=True),
        lax.all_gather(norm2_gain, "shard", axis=0, tiled=True),
        lax.all_gather(w_router, "shard", axis=0, tiled=True),
    )
    hidden = hidden_in.astype(jnp.float32)
    segments = segment_ids[0]
    rotary_cosine, rotary_sine = tables(sequence_length, HEAD_SIZE)
    normed_f, scale_one = normalize(hidden, gathered[0].astype(jnp.float32))
    normalized_rows = normed_f.astype(jnp.bfloat16)
    unrotated_query = jnp.dot(
        normalized_rows, gathered[1], preferred_element_type=jnp.float32
    ).reshape(sequence_length, QUERY_HEADS, HEAD_SIZE)
    unrotated_key = jnp.dot(
        normalized_rows, gathered[2], preferred_element_type=jnp.float32
    ).reshape(sequence_length, KEY_VALUE_HEADS, HEAD_SIZE)
    value_matrix = (
        jnp.dot(normalized_rows, gathered[3], preferred_element_type=jnp.float32)
        .astype(jnp.bfloat16)
        .reshape(sequence_length, KEY_VALUE_HEADS, HEAD_SIZE)
    )
    query_matrix = (
        apply_rotary(unrotated_query, rotary_cosine, rotary_sine)
        .astype(jnp.bfloat16)
        .reshape(sequence_length, KEY_VALUE_HEADS, shard_group_width, HEAD_SIZE)
    )
    key_rows = apply_rotary(unrotated_key, rotary_cosine, rotary_sine).astype(jnp.bfloat16)
    position = jnp.arange(sequence_length)
    allowed = (position[None, :] <= position[:, None]) & (segments[:, None] == segments[None, :])
    scores = (
        jnp.einsum("qkgd,skd->kgqs", query_matrix, key_rows, preferred_element_type=jnp.float32)
        * head_scale
    )
    scores = jnp.where(allowed, scores, -1e30)
    top_score = jnp.max(scores, axis=-1, keepdims=True)
    exp_scores = jnp.exp(scores - top_score)
    sum_exp = jnp.sum(exp_scores, axis=-1, keepdims=True)
    log_total = top_score + jnp.log(sum_exp)
    attn_probs = (exp_scores / sum_exp).astype(jnp.bfloat16)
    mixed_heads = jnp.einsum(
        "kgqs,skd->qkgd", attn_probs, value_matrix, preferred_element_type=jnp.float32
    )
    mixed_heads = mixed_heads.reshape(sequence_length, QUERY_HEADS * HEAD_SIZE).astype(jnp.bfloat16)
    middle = hidden + jnp.dot(mixed_heads, gathered[4], preferred_element_type=jnp.float32)
    gain_two = gathered[5].astype(jnp.float32)
    normed_two_f, scale_two = normalize(middle, gain_two)
    normed_two = normed_two_f.astype(jnp.bfloat16)
    logits = jnp.dot(normed_two, gathered[6], preferred_element_type=jnp.float32)
    router_probs = softmax_rows(logits)
    onehot = routes[:, :, None] == jnp.arange(experts, dtype=jnp.int32)[None, None, :]
    picked_probs = jnp.sum(jnp.where(onehot, router_probs[:, None, :], 0.0), axis=-1)
    picked_total = jnp.sum(picked_probs, axis=-1, keepdims=True)
    gate_weights = picked_probs / picked_total
    flat_routes = routes.reshape(-1)
    flat_hot = (flat_routes[:, None] == jnp.arange(experts, dtype=jnp.int32)[None, :]).astype(
        jnp.int32
    )
    before = jnp.cumsum(flat_hot, axis=0) - flat_hot
    slot_index = jnp.sum(before * flat_hot, axis=1)
    place_index = flat_routes * CAP + slot_index
    token_index = jnp.arange(sequence_length * TOPK, dtype=jnp.int32) // TOPK
    owner_token = (
        jnp.full((experts * CAP,), sequence_length, jnp.int32).at[place_index].set(token_index)
    )
    padded_rows = jnp.concatenate([normed_two, jnp.zeros((1, MODEL_WIDTH), jnp.bfloat16)], axis=0)
    buffer = padded_rows[owner_token].reshape(experts, CAP, MODEL_WIDTH)
    full_weights = (
        lax.all_gather(w_gate, "shard", axis=1, tiled=True),
        lax.all_gather(w_up, "shard", axis=1, tiled=True),
        lax.all_gather(w_down, "shard", axis=1, tiled=True),
    )
    expert_out, gate_pre, lift_pre, inner_act = expert_pass(
        buffer, full_weights[0], full_weights[1], full_weights[2]
    )
    picked_out = (
        expert_out.reshape(experts * CAP, MODEL_WIDTH)[place_index]
        .reshape(sequence_length, TOPK, MODEL_WIDTH)
        .astype(jnp.float32)
    )
    hidden_out = (middle + jnp.sum(gate_weights[:, :, None] * picked_out, axis=1)).astype(
        jnp.bfloat16
    )
    upstream = out_grad.astype(jnp.float32)
    again = (
        lax.all_gather(norm1_gain, "shard", axis=0, tiled=True),
        lax.all_gather(w_query, "shard", axis=0, tiled=True),
        lax.all_gather(key_weight, "shard", axis=0, tiled=True),
        lax.all_gather(value_weight, "shard", axis=0, tiled=True),
        lax.all_gather(w_out, "shard", axis=0, tiled=True),
        lax.all_gather(norm2_gain, "shard", axis=0, tiled=True),
        lax.all_gather(w_router, "shard", axis=0, tiled=True),
    )
    gate_grads = jnp.sum(upstream[:, None, :] * picked_out, axis=-1)
    slot_weight = (
        jnp.zeros((experts * CAP,), jnp.float32).at[place_index].set(gate_weights.reshape(-1))
    )
    padded_up = jnp.concatenate([upstream, jnp.zeros((1, MODEL_WIDTH), jnp.float32)], axis=0)
    out_grads = (
        (slot_weight[:, None] * padded_up[owner_token])
        .astype(jnp.bfloat16)
        .reshape(experts, CAP, MODEL_WIDTH)
    )
    weights_again = (
        lax.all_gather(w_gate, "shard", axis=1, tiled=True),
        lax.all_gather(w_up, "shard", axis=1, tiled=True),
        lax.all_gather(w_down, "shard", axis=1, tiled=True),
    )
    row_grads, gate_sum, up_sum, down_sum = expert_back(
        buffer,
        gate_pre,
        lift_pre,
        inner_act,
        weights_again[0],
        weights_again[1],
        weights_again[2],
        out_grads,
    )
    expert_grads = (
        lax.psum_scatter(
            gate_sum.astype(jnp.bfloat16), "shard", scatter_dimension=1, tiled=True
        ).astype(jnp.float32),
        lax.psum_scatter(
            up_sum.astype(jnp.bfloat16), "shard", scatter_dimension=1, tiled=True
        ).astype(jnp.float32),
        lax.psum_scatter(
            down_sum.astype(jnp.bfloat16), "shard", scatter_dimension=1, tiled=True
        ).astype(jnp.float32),
    )
    expert_grads = (
        lax.psum(expert_grads[0].astype(jnp.bfloat16), "rep").astype(jnp.float32),
        lax.psum(expert_grads[1].astype(jnp.bfloat16), "rep").astype(jnp.float32),
        lax.psum(expert_grads[2].astype(jnp.bfloat16), "rep").astype(jnp.float32),
    )
    expert_row_grad = jnp.sum(
        row_grads.reshape(experts * CAP, MODEL_WIDTH)[place_index]
        .reshape(sequence_length, TOPK, MODEL_WIDTH)
        .astype(jnp.float32),
        axis=1,
    )
    weighted = jnp.sum(gate_grads * gate_weights, axis=-1, keepdims=True)
    picked_grad = (gate_grads - weighted) / picked_total
    prob_grad = jnp.sum(jnp.where(onehot, picked_grad[:, :, None], 0.0), axis=1)
    logit_grad = router_probs * (
        prob_grad - jnp.sum(prob_grad * router_probs, axis=-1, keepdims=True)
    )
    logit_grad = logit_grad.astype(jnp.bfloat16)
    router_sum = contract(normed_two, logit_grad, 0, 0)
    normed_two_grad = contract(logit_grad, again[6], 1, 1) + expert_row_grad
    middle_norm_grad, gain_two_grad = norm_back(middle, scale_two, gain_two, normed_two_grad)
    middle_grad = upstream + middle_norm_grad
    branch_grad = middle_grad.astype(jnp.bfloat16)
    out_proj_sum = contract(mixed_heads, branch_grad, 0, 0)
    mixed_grad = (
        contract(branch_grad, again[4], 1, 1)
        .astype(jnp.bfloat16)
        .reshape(sequence_length, KEY_VALUE_HEADS, shard_group_width, HEAD_SIZE)
    )
    probs_again = jnp.exp(
        jnp.einsum("qkgd,skd->kgqs", query_matrix, key_rows, preferred_element_type=jnp.float32)
        * head_scale
        - log_total
    )
    probs_again = jnp.where(allowed, probs_again, 0.0)
    prob_back = jnp.einsum(
        "qkgd,skd->kgqs", mixed_grad, value_matrix, preferred_element_type=jnp.float32
    )
    score_grad = probs_again * (
        prob_back - jnp.sum(prob_back * probs_again, axis=-1, keepdims=True)
    )
    score_grad = score_grad.astype(jnp.bfloat16)
    query_back = (
        jnp.einsum("kgqs,skd->qkgd", score_grad, key_rows, preferred_element_type=jnp.float32)
        * head_scale
    )
    query_back = (
        apply_rotary(
            query_back.reshape(sequence_length, QUERY_HEADS, HEAD_SIZE), rotary_cosine, -rotary_sine
        )
        .astype(jnp.bfloat16)
        .reshape(sequence_length, QUERY_HEADS * HEAD_SIZE)
    )
    key_pullback = (
        jnp.einsum("kgqs,qkgd->skd", score_grad, query_matrix, preferred_element_type=jnp.float32)
        * head_scale
    )
    key_pullback = (
        apply_rotary(key_pullback, rotary_cosine, -rotary_sine)
        .astype(jnp.bfloat16)
        .reshape(sequence_length, KEY_VALUE_HEADS * HEAD_SIZE)
    )
    value_pullback = jnp.einsum(
        "kgqs,qkgd->skd",
        probs_again.astype(jnp.bfloat16),
        mixed_grad,
        preferred_element_type=jnp.float32,
    )
    value_pullback = value_pullback.astype(jnp.bfloat16).reshape(
        sequence_length, KEY_VALUE_HEADS * HEAD_SIZE
    )
    query_sum = contract(normalized_rows, query_back, 0, 0)
    key_sum = contract(normalized_rows, key_pullback, 0, 0)
    value_sum = contract(normalized_rows, value_pullback, 0, 0)
    normed_grad = (
        contract(query_back, again[1], 1, 1)
        + contract(key_pullback, again[2], 1, 1)
        + contract(value_pullback, again[3], 1, 1)
    )
    hidden_norm_grad, gain_one_grad = norm_back(
        hidden, scale_one, again[0].astype(jnp.float32), normed_grad
    )
    hidden_grad = (middle_grad + hidden_norm_grad).astype(jnp.bfloat16)
    attn_grads = (
        lax.psum_scatter(
            gain_one_grad.astype(jnp.bfloat16), "shard", scatter_dimension=0, tiled=True
        ).astype(jnp.float32),
        lax.psum_scatter(
            query_sum.astype(jnp.bfloat16), "shard", scatter_dimension=0, tiled=True
        ).astype(jnp.float32),
        lax.psum_scatter(
            key_sum.astype(jnp.bfloat16), "shard", scatter_dimension=0, tiled=True
        ).astype(jnp.float32),
        lax.psum_scatter(
            value_sum.astype(jnp.bfloat16), "shard", scatter_dimension=0, tiled=True
        ).astype(jnp.float32),
        lax.psum_scatter(
            out_proj_sum.astype(jnp.bfloat16), "shard", scatter_dimension=0, tiled=True
        ).astype(jnp.float32),
        lax.psum_scatter(
            gain_two_grad.astype(jnp.bfloat16), "shard", scatter_dimension=0, tiled=True
        ).astype(jnp.float32),
        lax.psum_scatter(
            router_sum.astype(jnp.bfloat16), "shard", scatter_dimension=0, tiled=True
        ).astype(jnp.float32),
    )
    attn_grads = (
        lax.psum(attn_grads[0].astype(jnp.bfloat16), "rep").astype(jnp.float32),
        lax.psum(attn_grads[1].astype(jnp.bfloat16), "rep").astype(jnp.float32),
        lax.psum(attn_grads[2].astype(jnp.bfloat16), "rep").astype(jnp.float32),
        lax.psum(attn_grads[3].astype(jnp.bfloat16), "rep").astype(jnp.float32),
        lax.psum(attn_grads[4].astype(jnp.bfloat16), "rep").astype(jnp.float32),
        lax.psum(attn_grads[5].astype(jnp.bfloat16), "rep").astype(jnp.float32),
        lax.psum(attn_grads[6].astype(jnp.bfloat16), "rep").astype(jnp.float32),
    )
    return (
        hidden_out,
        hidden_grad,
        attn_grads[0],
        attn_grads[1],
        attn_grads[2],
        attn_grads[3],
        attn_grads[4],
        attn_grads[5],
        attn_grads[6],
        expert_grads[0],
        expert_grads[1],
        expert_grads[2],
    )


def solution(mesh):
    in_specs = (
        P(("rep", "shard"), None),
        P(("rep", "shard"), None),
        P(("rep", "shard"), None),
        P(("rep", "shard"), None),
        P("shard"),
        P("shard", None),
        P("shard", None),
        P("shard", None),
        P("shard", None),
        P("shard"),
        P("shard", None),
        P(None, "shard", None),
        P(None, "shard", None),
        P(None, "shard", None),
    )
    out_specs = (
        P(("rep", "shard"), None),
        P(("rep", "shard"), None),
        P("shard"),
        P("shard", None),
        P("shard", None),
        P("shard", None),
        P("shard", None),
        P("shard"),
        P("shard", None),
        P(None, "shard", None),
        P(None, "shard", None),
        P(None, "shard", None),
    )
    return jax.shard_map(local, mesh=mesh, in_specs=in_specs, out_specs=out_specs, check_vma=False)
```

profile of v0, /device:TPU:0, one launch (start us, length us, event | category | flops | bytes accessed | tf_op | source)
XLA Modules:
  0.0 2481.7 jit_solution(4652554535373318668)
XLA Ops:
  36.2 15.5 gather_fusion.2
  51.7 18.7 copy.116
  86.1 18.2 all_gather.40
  126.6 18.6 all-gather.10.cloned.1.call-done
  161.3 14.7 gather_fusion
  176.6 194.8 %all-gather.12.cloned.1.call-done = bf16[8,1536,768]{2,1,0:T(8,128)(2,1)} async-done(((bf16[8,768,768]{2,1,0:T(8,128)(2,1)}), bf16[8,1536,768]{2,1,0:T(8,128)(2,1)}) %all-gather.12.cloned.1.call-update) | async-done | bytes 18874384 | tf_op jit(solution)/shard_map/all_gather | solution.py:184
  371.4 18.6 fusion.73
  390.0 206.0 %all-gather.14.cloned.1.call-done = bf16[8,1536,768]{2,1,0:T(8,128)(2,1)} async-done(((bf16[8,768,768]{2,1,0:T(8,128)(2,1)}), bf16[8,1536,768]{2,1,0:T(8,128)(2,1)}) %all-gather.14.cloned.1.call-update) | async-done | bytes 18874384 | tf_op jit(solution)/shard_map/all_gather | solution.py:185
  596.0 18.6 fusion.74
  614.6 206.0 %all-gather.16.cloned.1.call-done = bf16[8,1536,768]{2,1,0:T(8,128)(2,1)} async-done(((bf16[8,768,768]{2,1,0:T(8,128)(2,1)}), bf16[8,1536,768]{2,1,0:T(8,128)(2,1)}) %all-gather.16.cloned.1.call-update) | async-done | bytes 18874384 | tf_op jit(solution)/shard_map/all_gather | solution.py:186
  820.6 28.1 %multiply_convert_fusion.1 = (bf16[8,384,768]{2,1,0:T(8,128)(2,1)}, bf16[8,384,768]{2,1,0:T(8,128)(2,1)}, bf16[8,384,768]{2,1,0:T(8,128)(2,1)}) fusion(f32[8,384,768]{2,1,0:T(8,128)} %fusion.73, f32[8,384,768]{2,1,0:T(8,128)} %fusion.74, bf16[8,1536,768]{2,1,0:T(8,128)(2,1)} %all-gather.16.cloned.1.call-done, f32[8,384,1536]{1,2,0:T(8,128)} %copy.116, ...), kind=kOutput, calls=%fused_computation.26 | convolution fusion | flops 7294943232 | bytes 70791168 | tf_op jit(solution)/shard_map/ecd,edf->ecf/dot_general | solution.py:73
  848.6 16.1 convolution_convert_fusion.5
  864.7 18.2 gather_fusion.1
  882.9 12.3 reshape.313
  895.2 17.5 multiply_reduce_fusion
  913.9 19.4 fusion.75
  933.3 20.6 add_convert_fusion
  954.0 18.2 gather_fusion.3
  972.2 12.1 reshape.314
  984.3 12.9 reduce_sum.177
  1063.7 21.1 convolution_convert_fusion
  1084.8 17.7 convolution_convert_fusion.2
  1102.7 18.1 convolution_convert_fusion.1
  1128.2 62.4 %reduce-scatter.15.cloned.1.call-done = bf16[768,1536]{1,0:T(8,128)(2,1)} async-done(((bf16[1536,1536]{1,0:T(8,128)(2,1)}), bf16[768,1536]{1,0:T(8,128)(2,1)}) %reduce-scatter.15.cloned.1.call-update) | async-done | bytes 2359312 | tf_op jit(solution)/shard_map/reduce_scatter | solution.py:341
  1190.7 214.4 %reduce-scatter.23.cloned.1.call-done = bf16[8,768,768]{2,1,0:T(8,128)(2,1)} async-done(((bf16[8,1536,768]{2,1,0:T(8,128)(2,1)}), bf16[8,768,768]{2,1,0:T(8,128)(2,1)}) %reduce-scatter.23.cloned.1.call-update) | async-done | bytes 9437200 | tf_op jit(solution)/shard_map/reduce_scatter | solution.py:241
  1405.1 214.6 %reduce-scatter.19.cloned.1.call-done = bf16[8,768,768]{2,1,0:T(8,128)(2,1)} async-done(((bf16[8,1536,768]{2,1,0:T(8,128)(2,1)}), bf16[8,768,768]{2,1,0:T(8,128)(2,1)}) %reduce-scatter.19.cloned.1.call-update) | async-done | bytes 9437200 | tf_op jit(solution)/shard_map/reduce_scatter | solution.py:235
  1619.7 214.4 %reduce-scatter.21.cloned.1.call-done = bf16[8,768,768]{2,1,0:T(8,128)(2,1)} async-done(((bf16[8,1536,768]{2,1,0:T(8,128)(2,1)}), bf16[8,768,768]{2,1,0:T(8,128)(2,1)}) %reduce-scatter.21.cloned.1.call-update) | async-done | bytes 9437200 | tf_op jit(solution)/shard_map/reduce_scatter | solution.py:238
  1854.8 64.1 %all-reduce.4 = (bf16[768]{0:T(1024)(128)(2,1)S(1)}, bf16[768]{0:T(1024)(128)(2,1)S(1)}, bf16[768,8]{0,1:T(8,128)(2,1)S(1)}) all-reduce(bf16[768]{0:T(1024)(128)(2,1)S(1)} %dynamic-slice.1, bf16[768]{0:T(1024)(128)(2,1)S(1)} %dynamic-slice.3, ...), channel_id=1, replica_groups=mesh['rep'=16,'shard'=2] {'rep'}, use_global_device_ids=true, to_apply=%region_24.25 | all-reduce | flops 7680 | bytes 30720 | tf_op jit(solution)/shard_map/psum | solution.py:352
  1920.7 509.5 %all-reduce.9.cloned.1.call-done = (bf16[768,1536]{1,0:T(8,128)(2,1)}, bf16[768,256]{1,0:T(8,128)(2,1)}, bf16[768,256]{1,0:T(8,128)(2,1)}, bf16[768,1536]{1,0:T(...) async-done(((bf16[768,1536]{1,0:T(8,128)(2,1)}, bf16[768,256]{1,0:T(8,128)(2,1)}, bf16[768,256]{1,0:T(8,128)(2,1)}, ...) | async-done | bytes 33816592 | tf_op jit(solution)/shard_map/psum | solution.py:353
  2430.3 12.2 convert_element_type.248
  2442.5 12.2 convert_element_type.250
  2454.7 12.4 convert_element_type.252
  (277 shorter events, 187.3 us)
Async XLA Ops:
  7.2 100.8 %all-gather.8.cloned.1.call-start = ((), (), s32[]{:S(2)}) async-start(), calls=%async_computation.8 | async-start | bytes 7077888 | tf_op jit(solution)/shard_map/all_gather | solution.py:115
  7.9 137.3 %all-gather.10.cloned.1.call-start = ((), (), s32[]{:S(2)}) async-start(), calls=%async_computation.9 | async-start | bytes 7077888 | tf_op jit(solution)/shard_map/all_gather | solution.py:118
  8.7 362.7 %all-gather.12.cloned.1.call-start = ((), (), s32[]{:S(2)}) async-start(), calls=%async_computation.10 | async-start | bytes 28311552 | tf_op jit(solution)/shard_map/all_gather | solution.py:184
  9.4 586.6 %all-gather.14.cloned.1.call-start = ((), (), s32[]{:S(2)}) async-start(), calls=%async_computation.11 | async-start | bytes 28311552 | tf_op jit(solution)/shard_map/all_gather | solution.py:185
  10.0 14.0 copy-start.6
  10.0 810.5 %all-gather.16.cloned.1.call-start = ((), (), s32[]{:S(2)}) async-start(), calls=%async_computation.12 | async-start | bytes 28311552 | tf_op jit(solution)/shard_map/all_gather | solution.py:186
  10.6 1112.6 %reduce-scatter.13.cloned.1.call-start = ((), (), s32[]{:S(2)}) async-start(), calls=%async_computation.15 | async-start | bytes 1179648 | tf_op jit(solution)/shard_map/reduce_scatter | solution.py:338
  16.5 91.5 %copy-start.48 = (f32[1536]{0:T(1024)}, f32[1536]{0:T(1024)S(1)}, u32[]{:S(2)}) copy-start(f32[1536]{0:T(1024)S(1)} %reshape.369) | copy-start | bytes 18436
  20.9 130.2 %copy-start.45 = (f32[1536]{0:T(1024)}, f32[1536]{0:T(1024)S(1)}, u32[]{:S(2)}) copy-start(f32[1536]{0:T(1024)S(1)} %reshape.370) | copy-start | bytes 18436
  28.1 77.3 %copy-start.59 = (s32[2048,1]{0,1:T(1,128)}, s32[2048,1]{0,1:T(1,128)S(1)}, u32[]{:S(2)}) copy-start(s32[2048,1]{0,1:T(1,128)S(1)} %compare_select_fusion) | copy-start | bytes 24580
  51.7 18.7 copy-start.62
  51.7 25.1 %copy-start.34 = (bf16[768,256]{1,0:T(8,128)(2,1)S(1)}, bf16[768,256]{1,0:T(8,128)(2,1)}, u32[]{:S(2)}) copy-start(bf16[768,256]{1,0:T(8,128)(2,1)} %param.20) | copy-start | bytes 1179652
  51.7 34.4 %copy-start.35 = (bf16[768,256]{1,0:T(8,128)(2,1)S(1)}, bf16[768,256]{1,0:T(8,128)(2,1)}, u32[]{:S(2)}) copy-start(bf16[768,256]{1,0:T(8,128)(2,1)} %param.21) | copy-start | bytes 1179652
  70.4 33.9 %copy-start.10 = (bf16[512,1536]{1,0:T(8,128)(2,1)S(1)}, bf16[512,1536]{1,0:T(8,128)(2,1)}, u32[]{:S(2)}) copy-start(bf16[512,1536]{1,0:T(8,128)(2,1)} %param.14) | copy-start | bytes 4718596
  70.4 35.5 %copy-start.63 = (s32[1,512]{1,0:T(1,128)S(1)}, s32[1,512]{1,0:T(1,128)}, u32[]{:S(2)}) copy-start(s32[1,512]{1,0:T(1,128)} %param.15) | copy-start | bytes 6148
  75.0 76.4 %copy-start.43 = (bf16[1536,8]{0,1:T(8,128)(2,1)}, bf16[1536,8]{0,1:T(8,128)(2,1)S(1)}, u32[]{:S(2)}) copy-start(bf16[1536,8]{0,1:T(8,128)(2,1)S(1)} %all_gather.45) | copy-start | bytes 73732
  76.8 37.0 %copy-start.18 = (f32[512,128]{0,1:T(8,128)}, f32[512,128]{0,1:T(8,128)S(1)}, u32[]{:S(2)}) copy-start(f32[512,128]{0,1:T(8,128)S(1)} %get-tuple-element.48) | copy-start | bytes 786436
  86.1 20.8 copy-start.22
  151.4 24.6 copy-start.4
  161.2 659.4 %copy-start.32 = (f32[8,384]{1,0:T(8,128)}, f32[8,384]{1,0:T(8,128)S(1)}, u32[]{:S(2)}) copy-start(f32[8,384]{1,0:T(8,128)S(1)} %mul.369) | copy-start | bytes 36868
  848.6 16.1 copy-start.50
  895.2 18.5 copy-start.58
  895.2 18.6 copy-start.52
  895.2 18.6 copy-start.56
  1028.5 94.7 %reduce-scatter.11.cloned.1.call-start = ((), (), s32[]{:S(2)}) async-start(), calls=%async_computation.14 | async-start | bytes 1179648 | tf_op jit(solution)/shard_map/reduce_scatter | solution.py:335
  1043.5 84.8 %reduce-scatter.9.cloned.1.call-start = ((), (), s32[]{:S(2)}) async-start(), calls=%async_computation.13 | async-start | bytes 7077888 | tf_op jit(solution)/shard_map/reduce_scatter | solution.py:332
  1055.5 135.2 %reduce-scatter.15.cloned.1.call-start = ((), (), s32[]{:S(2)}) async-start(), calls=%async_computation.16 | async-start | bytes 7077888 | tf_op jit(solution)/shard_map/reduce_scatter | solution.py:341
  1063.0 342.1 %reduce-scatter.23.cloned.1.call-start = ((), (), s32[]{:S(2)}) async-start(), calls=%async_computation.20 | async-start | bytes 28311552 | tf_op jit(solution)/shard_map/reduce_scatter | solution.py:241
  1084.8 534.9 %reduce-scatter.19.cloned.1.call-start = ((), (), s32[]{:S(2)}) async-start(), calls=%async_computation.18 | async-start | bytes 28311552 | tf_op jit(solution)/shard_map/reduce_scatter | solution.py:235
  1102.6 731.5 %reduce-scatter.21.cloned.1.call-start = ((), (), s32[]{:S(2)}) async-start(), calls=%async_computation.19 | async-start | bytes 28311552 | tf_op jit(solution)/shard_map/reduce_scatter | solution.py:238
  1120.7 734.1 %reduce-scatter.17.cloned.1.call-start = ((), (), s32[]{:S(2)}) async-start(), calls=%async_computation.17 | async-start | bytes 36864 | tf_op jit(solution)/shard_map/reduce_scatter | solution.py:347
  1123.1 1307.2 %all-reduce.9.cloned.1.call-start = ((), (), s32[]{:S(2)}) async-start(), calls=%async_computation.21 | async-start | bytes 67633152 | tf_op jit(solution)/shard_map/psum | solution.py:353
  (54 other events, 264.3 us)
Sparse Core Ops, SparseCore 0:
  9.6 65.5 all-gather.7
  76.7 68.4 all-gather.9
  146.7 224.6 all-gather.11
  372.8 223.1 all-gather.13
  597.4 223.1 all-gather.15
  1028.6 17.4 reduce-scatter.12
  1048.4 17.4 reduce-scatter.10
  1068.2 59.9 reduce-scatter.8
  1130.6 59.9 reduce-scatter.14
  1193.4 211.6 reduce-scatter.22
  1408.0 211.6 reduce-scatter.18
  1622.4 211.6 reduce-scatter.20
  1836.9 9.8 reduce-scatter.16
  1852.4 577.8 all-reduce.8
where the time goes:
time: 2490 us; the launch traced here: 2480 us
  waiting for transfers between devices  1850 us (74%)
  matrix products  251 us (10%)
  local copies, waits for them, and re-layouts  145 us (6%)
  blocking collectives  111 us (4%)
  other arithmetic  110 us (4%)
    psum x1, waiting for transfers between devices, local(): lax.psum(attn_grads[1].astype(jnp.bfloat16), 'rep').astype(jnp.float32)  510 us
    reduce_scatter x1, waiting for transfers between devices, local(): lax.psum_scatter(gate_sum.astype(jnp.bfloat16), 'shard', scatter_dimensio...  215 us
    reduce_scatter x1, waiting for transfers between devices, local(): lax.psum_scatter(up_sum.astype(jnp.bfloat16), 'shard', scatter_dimension=...  214 us
    reduce_scatter x1, waiting for transfers between devices, local(): lax.psum_scatter(down_sum.astype(jnp.bfloat16), 'shard', scatter_dimensio...  214 us
    all_gather x1, waiting for transfers between devices, local(): lax.all_gather(w_up, 'shard', axis=1, tiled=True)  206 us
    all_gather x1, waiting for transfers between devices, local(): lax.all_gather(w_down, 'shard', axis=1, tiled=True)  206 us
    all_gather x1, waiting for transfers between devices, local(): lax.all_gather(w_gate, 'shard', axis=1, tiled=True)  195 us
    psum x1, blocking collectives, local(): lax.psum(attn_grads[0].astype(jnp.bfloat16), 'rep').astype(jnp.float32)  64.1 us
  transfers between devices with their start and end apart: 14, of which 10 were waited for; matrix products, arithmetic and copies ran while one was open for 10% of the time, Pallas kernels for 0%

commit v1 on v0

v1 whole, which is shorter than its diff:
```python
import functools

import jax
import jax.numpy as jnp
from jax import lax
from jax.experimental import pallas as pl
from jax.experimental.pallas import tpu as pltpu
from jax.sharding import PartitionSpec as P

MODEL_WIDTH = 1536
QUERY_HEADS = 12
KEY_VALUE_HEADS = 2
HEAD_SIZE = 128
TOPK = 4
FF = 768
HALF = 768
ROWS = 512
PAD = 128
WIDE = MODEL_WIDTH + PAD
CHUNK = 192
PER = HALF // CHUNK
CHUNKS = 6 * PER

epsilon = 1e-06
rope_base = 1000000.0
MESH = pl.DeviceIdType.MESH
bf16 = jnp.bfloat16
f32 = jnp.float32


def tables(sequence_length, row_width):
    frequency = rope_base ** (-2.0 * jnp.arange(row_width // 2, dtype=jnp.float32) / row_width)
    angles = jnp.arange(sequence_length, dtype=jnp.float32)[:, None] * frequency[None, :]
    angles = jnp.concatenate([angles, angles], axis=-1)
    return (jnp.cos(angles)[:, None, :], jnp.sin(angles)[:, None, :])


def apply_rotary(values, rotary_cosine, rotary_sine):
    half_width = values.shape[-1] // 2
    turned = jnp.concatenate([-values[..., half_width:], values[..., :half_width]], axis=-1)
    return values * rotary_cosine + turned * rotary_sine


def contract(left_side, right_side, left_dim, right_dim):
    return lax.dot_general(
        left_side,
        right_side,
        (((left_dim,), (right_dim,)), ((), ())),
        preferred_element_type=jnp.float32,
    )


def normalize(values, gain_vector):
    scale_rows = lax.rsqrt(jnp.mean(values * values, axis=-1, keepdims=True) + epsilon)
    return (values * scale_rows * gain_vector, scale_rows)


def norm_back(values, scale_rows, gain_vector, upstream):
    scaled = upstream * gain_vector
    gain_grad = jnp.sum(upstream * values * scale_rows, axis=0)
    inner_sum = jnp.sum(scaled * values, axis=-1, keepdims=True)
    return (scaled * scale_rows - values * scale_rows**3 * inner_sum / values.shape[-1], gain_grad)


def softmax_rows(values):
    top_value = jnp.max(values, axis=-1, keepdims=True)
    exp_values = jnp.exp(values - top_value)
    return exp_values / jnp.sum(exp_values, axis=-1, keepdims=True)


def place():
    rep = lax.axis_index("rep")
    y = lax.axis_index("shard")
    return rep // 4, (rep // 2) % 2, rep % 2, y


def at(z, x, c, y):
    return ((z * 2 + x) * 2 + c, y)


def remote(src, dst, send, recv, device):
    return pltpu.make_async_remote_copy(
        src_ref=src,
        dst_ref=dst,
        send_sem=send,
        recv_sem=recv,
        device_id=device,
        device_id_type=MESH,
    )


def greet(partners):
    barrier = pltpu.get_barrier_semaphore()
    for device in partners:
        pl.semaphore_signal(barrier, inc=1, device_id=device, device_id_type=MESH)
    pl.semaphore_wait(barrier, len(partners))


def gather_kernel(
    wq, wk, wv, wo, sm, g, wg, wu, wd,
    wqf, wkf, wvf, wof, smf, g4, w0,
    loc, y_s, y_r, x_s, x_r, c_s, c_r, d_s, d_r, z_s, z_r,
):
    z, x, c, y = place()
    ydev, xdev, cdev = at(z, x, c, 1 - y), at(z, 1 - x, c, y), at(z, x, 1 - c, y)
    zdev = at(z + 1 - 2 * (z % 2), x, c, y)
    greet((ydev, xdev, cdev, zdev))
    parts, fulls, experts = (wq, wk, wv, wo), (wqf, wkf, wvf, wof), (wg, wu, wd)
    piece = HALF // 4
    mine = pl.ds((2 * x + c) * piece, piece)
    theirs = pl.ds((2 * (1 - x) + c) * piece, piece)
    expert = 2 * (2 * x + c)
    h = z % 2
    ys, xs, cs, ds, zs = [], [], [], [], []
    for a in range(4):
        ys.append(remote(parts[a].at[mine], fulls[a].at[y, mine], y_s.at[a], y_r.at[a], ydev))
        ys[a].start()
    ys.append(remote(sm, smf.at[y], y_s.at[4], y_r.at[4], ydev))
    ys[4].start()
    xs_g = remote(g, g4.at[2], x_s.at[4], x_r.at[4], xdev)
    cs_g = remote(g, g4.at[1], c_s.at[4], c_r.at[4], cdev)
    cs_g.start()
    for m in range(3):
        ys.append(
            remote(
                experts[m].at[expert, pl.ds(h * 384, 384)],
                w0.at[m, pl.ds(y * HALF + h * 384, 384)],
                y_s.at[5 + m],
                y_r.at[5 + m],
                ydev,
            )
        )
        ys[5 + m].start()
    locs = [pltpu.make_async_copy(parts[a], fulls[a].at[y], loc.at[a]) for a in range(4)]
    locs.append(pltpu.make_async_copy(sm, smf.at[y], loc.at[4]))
    locs.append(pltpu.make_async_copy(g, g4.at[0], loc.at[5]))
    for m in range(3):
        locs.append(
            pltpu.make_async_copy(
                experts[m].at[expert], w0.at[m, pl.ds(y * HALF, HALF)], loc.at[6 + m]
            )
        )
    for copy in locs:
        copy.start()
    for a in range(4):
        ys[a].wait_recv()
        xs.append(
            remote(
                fulls[a].at[1 - y, mine], fulls[a].at[1 - y, mine], x_s.at[a], x_r.at[a], xdev
            )
        )
        cs.append(
            remote(
                fulls[a].at[1 - y, mine], fulls[a].at[1 - y, mine], c_s.at[a], c_r.at[a], cdev
            )
        )
        xs[a].start()
        cs[a].start()
    xs_g.start()
    for a in range(4):
        xs[a].wait_recv()
        ds.append(
            remote(
                fulls[a].at[1 - y, theirs], fulls[a].at[1 - y, theirs], d_s.at[a], d_r.at[a], cdev
            )
        )
        ds[a].start()
    for m in range(3):
        ys[5 + m].wait_recv()
        rows = pl.ds((1 - y) * HALF + h * 384, 384)
        zs.append(remote(w0.at[m, rows], w0.at[m, rows], z_s.at[m], z_r.at[m], zdev))
        zs[m].start()
    xs_g.wait_recv()
    ds_g = remote(g4.at[2], g4.at[3], d_s.at[4], d_r.at[4], cdev)
    ds_g.start()
    ys[4].wait_recv()
    for copy in ys:
        copy.wait_send()
    for copy in xs + [xs_g]:
        copy.wait_send()
    xs_g = None
    for copy in cs + [cs_g] + ds + [ds_g] + zs:
        copy.wait()
    for copy in locs:
        copy.wait()


def gather_call(wq, wk, wv, wo, sm, g, wg, wu, wd):
    anyspace = pl.BlockSpec(memory_space=pl.ANY)
    shapes = [
        (2, HALF, MODEL_WIDTH),
        (2, HALF, 256),
        (2, HALF, 256),
        (2, HALF, MODEL_WIDTH),
        (2, 16, HALF),
        (4, ROWS, MODEL_WIDTH),
        (3, MODEL_WIDTH, FF),
    ]
    dma = pltpu.SemaphoreType.DMA
    return pl.pallas_call(
        gather_kernel,
        out_shape=[jax.ShapeDtypeStruct(s, bf16) for s in shapes],
        in_specs=[anyspace] * 9,
        out_specs=[anyspace] * 7,
        scratch_shapes=[dma((9,)), dma((8,)), dma((8,))] + [dma((5,))] * 6 + [dma((3,))] * 2,
        compiler_params=pltpu.CompilerParams(collective_id=1, has_side_effects=True),
        name="gather_weights",
    )(wq, wk, wv, wo, sm, g, wg, wu, wd)


def expert_kernel(
    hg, g4, w0, wg, wu, wd,
    r_own, r_core, r_x, o_own, o_core, o_x, out, gr, ya, za, zb,
    H, G, W, ACT, DG, RS, OS, CR, CO, STG, VA, VB, VS, VZ, VT, VF, FN,
    loc, h_s, h_r, wy_s, wy_r, wz_s, wz_r, stg_sem, y_s, y_r, ld_a, ld_b,
    z1_s, z1_r, ld_z, z2_s, z2_r, ld_f, z3_s, z3_r, fo, x_s, x_r, c1_s, c1_r, c2_s, c2_r,
    rc_s, rc_r, rx_s, rx_r, rd_s, rd_r, ro,
):
    z, x, c, y = place()
    mid = (z == 1) | (z == 2)
    ydev, xdev, cdev = at(z, x, c, 1 - y), at(z, 1 - x, c, y), at(z, x, 1 - c, y)
    zdev = at(z + 1 - 2 * (z % 2), x, c, y)
    mdev = at(3 - z, x, c, y)
    greet((ydev, xdev, cdev, zdev, mdev))
    shards = (wg, wu, wd)
    e0 = 2 * (2 * x + c)
    h = z % 2

    hx = remote(hg, H.at[pl.ds(2 * ROWS, ROWS)], h_s.at[0], h_r.at[0], xdev)
    hc = remote(hg, H.at[pl.ds(ROWS, ROWS)], h_s.at[1], h_r.at[1], cdev)
    hx.start()
    hc.start()
    own = [
        pltpu.make_async_copy(hg, H.at[pl.ds(0, ROWS)], loc.at[0]),
        pltpu.make_async_copy(g4, G, loc.at[1]),
        pltpu.make_async_copy(w0, W.at[0], loc.at[2]),
    ]
    for m in range(3):
        own.append(
            pltpu.make_async_copy(
                shards[m].at[e0 + 1], W.at[1, m, pl.ds(y * HALF, HALF)], loc.at[3 + m]
            )
        )
    wys = []
    for m in range(3):
        wys.append(
            remote(
                shards[m].at[e0 + 1, pl.ds(h * 384, 384)],
                W.at[1, m, pl.ds(y * HALF + h * 384, 384)],
                wy_s.at[m],
                wy_r.at[m],
                ydev,
            )
        )
        wys[m].start()
    for copy in own:
        copy.start()

    def gate_of(j, rows):
        lane = lax.broadcasted_iota(jnp.int32, (2 * ROWS, PAD), 1)
        packed = H[rows, MODEL_WIDTH:].astype(f32)
        picked = (lane == e0 + j) | (lane == e0 + j + 8)
        return jnp.sum(jnp.where(picked, packed, 0.0), axis=1, keepdims=True), lane

    def forward(j, first):
        rows = pl.ds(first, 2 * ROWS)
        gate, lane = gate_of(j, rows)

        def step(t, total):
            columns = pl.ds(pl.multiple_of(t * 256, 256), 256)
            ug = jnp.dot(
                H[rows, :MODEL_WIDTH], W[j, 0, :, columns], preferred_element_type=f32
            )
            uu = jnp.dot(
                H[rows, :MODEL_WIDTH], W[j, 1, :, columns], preferred_element_type=f32
            )
            dh = jnp.dot(G[rows, :], W[j, 2, :, columns], preferred_element_type=f32)
            sigma = jax.nn.sigmoid(ug)
            silu = ug * sigma
            hid = silu * uu
            ACT[j, 0, rows, columns] = (hid * gate).astype(bf16)
            dhg = dh * gate
            ACT[j, 1, rows, columns] = (dhg * uu * sigma * (1.0 + ug * (1.0 - sigma))).astype(bf16)
            ACT[j, 2, rows, columns] = (dhg * silu).astype(bf16)
            return total + jnp.sum(hid * dh, axis=1, keepdims=True)

        total = lax.fori_loop(0, FF // 256, step, jnp.zeros((2 * ROWS, 1), f32))
        high = total.astype(bf16).astype(f32)
        low = total - high
        here = jnp.where(lane == e0 + j, high, jnp.where(lane == e0 + j + 8, low, 0.0))
        if j == 0:
            DG[rows, :] = here.astype(bf16)
        else:
            DG[rows, :] = (DG[rows, :].astype(f32) + here).astype(bf16)

    def nt(j, k, rows, m, ns):
        return lax.dot_general(
            ACT[j, k, rows, :],
            W[j, m, ns, :],
            (((1,), (1,)), ((), ())),
            preferred_element_type=f32,
        )

    def back_rows(rows, ns):
        o = nt(0, 0, rows, 2, ns) + nt(1, 0, rows, 2, ns)
        d = nt(0, 1, rows, 0, ns) + nt(0, 2, rows, 1, ns)
        d = d + nt(1, 1, rows, 0, ns) + nt(1, 2, rows, 1, ns)
        return o, d

    def weight_tile(j, m, left, half, i, slot):
        at_row = half * HALF + i * 384
        lhs = left[:, pl.ds(pl.multiple_of(at_row, 128), 384)]
        act = (m + 1) % 3
        rhs = ACT[j, act]
        tile = lax.dot_general(lhs, rhs, (((0,), (0,)), ((), ())), preferred_element_type=f32)
        STG[slot] = tile.astype(bf16)
        copy = pltpu.make_async_copy(
            STG.at[slot], gr.at[j, m, pl.ds(at_row, 384)], stg_sem.at[slot]
        )
        copy.start()
        return copy

    def y_copy(k):
        j, m, i = k // (3 * PER), (k // PER) % 3, k % PER
        return remote(
            gr.at[j, m, pl.ds((1 - y) * HALF + i * CHUNK, CHUNK)],
            ya.at[k],
            y_s.at[k],
            y_r.at[k],
            ydev,
        )

    def weight_pair(j, m, left, i):
        away = weight_tile(j, m, left, 1 - y, i, 0)
        here = weight_tile(j, m, left, y, i, 1)
        away.wait()
        first = (j * 3 + m) * PER + i * (384 // CHUNK)
        for n in range(384 // CHUNK):
            y_copy(first + n).start()
        here.wait()

    def weight_grads(j, slots):
        done = 0
        for left, m0, steps in ((H, 0, 4), (G, 2, 2)):

            def step(q, _, left=left, m0=m0):
                weight_pair(j, m0 + q // 2, left, q % 2)
                return 0

            lax.fori_loop(0, steps, step, 0)
        del done, slots

    def spot(k, expert):
        j, m, i = k // (3 * PER), (k // PER) % 3, k % PER
        return out.at[m, expert + j, pl.ds(i * CHUNK, CHUNK)]

    def load_a(k):
        j, m, i = k // (3 * PER), (k // PER) % 3, k % PER
        return pltpu.make_async_copy(
            gr.at[j, m, pl.ds(y * HALF + i * CHUNK, CHUNK)], VA.at[k % 2], ld_a.at[k % 2]
        )

    def load_b(k):
        return pltpu.make_async_copy(ya.at[k], VB.at[k % 2], ld_b.at[k % 2])

    def load_z(k):
        return pltpu.make_async_copy(za.at[k], VZ.at[k % 2], ld_z.at[k % 2])

    def load_f(k):
        return pltpu.make_async_copy(zb.at[k], VF.at[k % 2], ld_f.at[k % 2])

    def z1_copy(k):
        return remote(VS.at[k % 4], za.at[k], z1_s.at[k], z1_r.at[k], zdev)

    def z2_copy(k):
        return remote(VT.at[k % 4], zb.at[k], z2_s.at[k], z2_r.at[k], mdev)

    def z3_copy(k):
        return remote(FN.at[k % 4], spot(k, e0), z3_s.at[k], z3_r.at[k], zdev)

    def store_f(k):
        return pltpu.make_async_copy(FN.at[k % 4], spot(k, e0), fo.at[k % 4])

    def x_copy(k):
        return remote(spot(k, e0), spot(k, e0), x_s.at[k], x_r.at[k], xdev)

    def c1_copy(k):
        return remote(spot(k, e0), spot(k, e0), c1_s.at[k], c1_r.at[k], cdev)

    def c2_copy(k):
        other = 2 * (2 * (1 - x) + c)
        return remote(spot(k, other), spot(k, other), c2_s.at[k], c2_r.at[k], cdev)

    def when(k, cond=None):
        ok = (k >= 0) & (k < CHUNKS)
        return pl.when(ok if cond is None else ok & cond)

    def slot(s):
        k_cx = s - 11

        @when(k_cx)
        def _():
            x_copy(k_cx).wait_recv()
            c2_copy(k_cx).start()

        k_x = s - 9

        @when(k_x, mid)
        def _():
            store_f(k_x).wait()
            z3_copy(k_x).wait_send()

        @when(k_x, jnp.logical_not(mid))
        def _():
            z3_copy(k_x).wait_recv()

        @when(k_x)
        def _():
            x_copy(k_x).start()
            c1_copy(k_x).start()

        k_fa = s - 7

        @when(k_fa, mid)
        def _():
            load_f(k_fa).wait()
            z2_copy(k_fa).wait_send()
            FN[k_fa % 4] = (VT[k_fa % 4].astype(f32) + VF[k_fa % 2].astype(f32)).astype(bf16)
            z3_copy(k_fa).start()
            store_f(k_fa).start()

        k_fl = s - 6

        @when(k_fl, mid)
        def _():
            z2_copy(k_fl).wait_recv()
            load_f(k_fl).start()

        k_za = s - 4

        @when(k_za, mid)
        def _():
            load_z(k_za).wait()
            VT[k_za % 4] = (VS[k_za % 4].astype(f32) + VZ[k_za % 2].astype(f32)).astype(bf16)
            z2_copy(k_za).start()

        k_zl = s - 3

        @when(k_zl, mid)
        def _():
            z1_copy(k_zl).wait_recv()
            load_z(k_zl).start()

        @when(s - 5, jnp.logical_not(mid))
        def _():
            z1_copy(s - 5).wait_send()

        k_a = s - 1

        @when(k_a)
        def _():
            load_a(k_a).wait()
            load_b(k_a).wait()
            VS[k_a % 4] = (VA[k_a % 2].astype(f32) + VB[k_a % 2].astype(f32)).astype(bf16)

        @when(k_a, jnp.logical_not(mid))
        def _():
            z1_copy(k_a).start()

        @when(s)
        def _():
            y_copy(s).wait_recv()
            load_a(s).start()
            load_b(s).start()

    def slots(first, last):
        def step(s, _):
            slot(s)
            return 0

        lax.fori_loop(first, last, step, 0)

    own[1].wait()
    own[2].wait()
    own[0].wait()
    hc.wait_recv()
    forward(0, 0)
    hx.wait_recv()
    hd = remote(
        H.at[pl.ds(2 * ROWS, ROWS)], H.at[pl.ds(3 * ROWS, ROWS)], h_s.at[2], h_r.at[2], cdev
    )
    hd.start()
    wzs = []
    for m in range(3):
        wys[m].wait_recv()
        rows = pl.ds((1 - y) * HALF + h * 384, 384)
        wzs.append(remote(W.at[1, m, rows], W.at[1, m, rows], wz_s.at[m], wz_r.at[m], zdev))
        wzs[m].start()
    hd.wait_recv()
    forward(0, 2 * ROWS)
    weight_grads(0, 0)
    for m in range(3):
        wzs[m].wait_recv()
        own[3 + m].wait()
    forward(1, 0)
    slots(0, 2)
    forward(1, 2 * ROWS)
    slots(2, 4)

    def tail(buffer_r, rows):
        buffer_r[:, MODEL_WIDTH:] = DG[rows, :]

    third, second = pl.ds(3 * ROWS, ROWS), pl.ds(2 * ROWS, ROWS)

    def rc_copy(t, which):
        ns = pl.ds(pl.multiple_of(t * 512, 512), 512)
        src, dst = ((RS, CR), (OS, CO))[which]
        return remote(
            src.at[t % 2], dst.at[:, ns], rc_s.at[which, t], rc_r.at[which, t], cdev
        )

    for t in range(3):
        ns = pl.ds(t * 512, 512)
        if t == 2:
            rc_copy(0, 0).wait_send()
            rc_copy(0, 1).wait_send()
        o, d = back_rows(third, ns)
        RS[t % 2] = d.astype(bf16)
        OS[t % 2] = o.astype(bf16)
        rc_copy(t, 0).start()
        rc_copy(t, 1).start()
    dg_copy = remote(
        DG.at[third], CR.at[:, pl.ds(MODEL_WIDTH, PAD)], rd_s.at[0], rd_r.at[0], cdev
    )
    dg_copy.start()
    slots(4, 6)
    for t in range(3):
        ns = pl.ds(t * 512, 512)
        o, d = back_rows(second, ns)
        rc_copy(t, 0).wait_recv()
        rc_copy(t, 1).wait_recv()
        CR[:, ns] = (CR[:, ns].astype(f32) + d).astype(bf16)
        CO[:, ns] = (CO[:, ns].astype(f32) + o).astype(bf16)
    dg_copy.wait_recv()
    CR[:, MODEL_WIDTH:] = CR[:, MODEL_WIDTH:] + DG[second, :]
    rx = remote(CR, r_x, rx_s.at[0], rx_r.at[0], xdev)
    ox = remote(CO, o_x, rx_s.at[1], rx_r.at[1], xdev)
    rx.start()
    ox.start()
    slots(6, 8)
    weight_grads(1, 0)
    slots(8, 10)
    for which, (src, dst) in enumerate(((RS, CR), (OS, CO))):
        for t in (1, 2):
            rc_copy(t, which).wait_send()
    dg_copy.wait_send()

    def rb_copy(t, which):
        src, dst = ((RS, r_core), (OS, o_core))[which]
        return remote(
            src.at[t % 2],
            dst.at[:, pl.ds(t * 512, 512)],
            rd_s.at[1 + which * 3 + t],
            rd_r.at[1 + which * 3 + t],
            cdev,
        )

    def ro_copy(t, which):
        src, dst = ((RS, r_own), (OS, o_own))[which]
        return pltpu.make_async_copy(
            src.at[t % 2], dst.at[:, pl.ds(t * 512, 512)], ro.at[which, t]
        )

    first = pl.ds(ROWS, ROWS)
    tail_b = remote(
        DG.at[first], r_core.at[:, pl.ds(MODEL_WIDTH, PAD)], rd_s.at[7], rd_r.at[7], cdev
    )
    tail_b.start()
    tail_o = pltpu.make_async_copy(
        DG.at[pl.ds(0, ROWS)], r_own.at[:, pl.ds(MODEL_WIDTH, PAD)], ro.at[0, 3]
    )
    tail_o.start()
    for t in range(3):
        if t == 2:
            rb_copy(0, 0).wait_send()
            rb_copy(0, 1).wait_send()
        o, d = back_rows(first, pl.ds(t * 512, 512))
        RS[t % 2] = d.astype(bf16)
        OS[t % 2] = o.astype(bf16)
        rb_copy(t, 0).start()
        rb_copy(t, 1).start()
    slots(10, 12)
    for t in range(3):
        if t < 2:
            rb_copy(2 - t, 0).wait_send()
            rb_copy(2 - t, 1).wait_send()
        else:
            ro_copy(0, 0).wait()
            ro_copy(0, 1).wait()
        o, d = back_rows(pl.ds(0, ROWS), pl.ds(t * 512, 512))
        RS[t % 2] = d.astype(bf16)
        OS[t % 2] = o.astype(bf16)
        ro_copy(t, 0).start()
        ro_copy(t, 1).start()
    slots(12, CHUNKS + 11)
    for which in range(2):
        for t in (1, 2):
            ro_copy(t, which).wait()
        for t in range(3):
            rb_copy(t, which).wait_recv()
    tail_b.wait()
    tail_o.wait()
    rx.wait()
    ox.wait()

    def finish(k, _):
        x_copy(k).wait_send()
        c1_copy(k).wait()
        c2_copy(k).wait()
        y_copy(k).wait_send()
        return 0

    lax.fori_loop(0, CHUNKS, finish, 0)
    for m in range(3):
        wys[m].wait_send()
        wzs[m].wait_send()
    hx.wait_send()
    hc.wait_send()
    hd.wait_send()


def expert_call(hg, g4, w0, wg, wu, wd):
    anyspace = pl.BlockSpec(memory_space=pl.ANY)
    dma = pltpu.SemaphoreType.DMA
    vmem = lambda *s: pltpu.VMEM(s, bf16)
    shapes = [(ROWS, WIDE)] * 3 + [(ROWS, MODEL_WIDTH)] * 3
    shapes += [(3, 8, HALF, FF), (2, 3, MODEL_WIDTH, FF)] + [(CHUNKS, CHUNK, FF)] * 3
    scratch = [
        vmem(4 * ROWS, WIDE),
        vmem(4 * ROWS, MODEL_WIDTH),
        vmem(2, 3, MODEL_WIDTH, FF),
        vmem(2, 3, 4 * ROWS, FF),
        vmem(4 * ROWS, PAD),
        vmem(2, ROWS, 512),
        vmem(2, ROWS, 512),
        vmem(ROWS, WIDE),
        vmem(ROWS, MODEL_WIDTH),
        vmem(2, 384, FF),
        vmem(2, CHUNK, FF),
        vmem(2, CHUNK, FF),
        vmem(4, CHUNK, FF),
        vmem(2, CHUNK, FF),
        vmem(4, CHUNK, FF),
        vmem(2, CHUNK, FF),
        vmem(4, CHUNK, FF),
        dma((6,)), dma((3,)), dma((3,)), dma((3,)), dma((3,)), dma((3,)), dma((3,)),
        dma((2,)), dma((CHUNKS,)), dma((CHUNKS,)), dma((2,)), dma((2,)),
        dma((CHUNKS,)), dma((CHUNKS,)), dma((2,)), dma((CHUNKS,)), dma((CHUNKS,)), dma((2,)),
        dma((CHUNKS,)), dma((CHUNKS,)), dma((4,)), dma((CHUNKS,)), dma((CHUNKS,)),
        dma((CHUNKS,)), dma((CHUNKS,)), dma((CHUNKS,)), dma((CHUNKS,)),
        dma((2, 3)), dma((2, 3)), dma((2,)), dma((2,)), dma((8,)), dma((8,)), dma((2, 4)),
    ]
    return pl.pallas_call(
        expert_kernel,
        out_shape=[jax.ShapeDtypeStruct(s, bf16) for s in shapes],
        in_specs=[anyspace] * 6,
        out_specs=[anyspace] * len(shapes),
        scratch_shapes=scratch,
        compiler_params=pltpu.CompilerParams(
            collective_id=2, has_side_effects=True, vmem_limit_bytes=66 * 1000 * 1000
        ),
        name="experts",
    )(hg, g4, w0, wg, wu, wd)[:7]


def attention_forward(hidden, segments, gain_one, w_q, w_k, w_v, w_o, gain_two):
    sequence_length = hidden.shape[0]
    group = QUERY_HEADS // KEY_VALUE_HEADS
    head_scale = HEAD_SIZE ** (-0.5)
    cosine, sine = tables(sequence_length, HEAD_SIZE)
    normed_f, scale_one = normalize(hidden, gain_one)
    h1 = normed_f.astype(bf16)
    qr = jnp.dot(h1, w_q, preferred_element_type=f32)
    kr = jnp.dot(h1, w_k, preferred_element_type=f32)
    values = jnp.dot(h1, w_v, preferred_element_type=f32).astype(bf16)
    values = values.reshape(sequence_length, KEY_VALUE_HEADS, HEAD_SIZE)
    qr = qr.reshape(sequence_length, QUERY_HEADS, HEAD_SIZE)
    kr = kr.reshape(sequence_length, KEY_VALUE_HEADS, HEAD_SIZE)
    queries = apply_rotary(qr, cosine, sine).astype(bf16)
    queries = queries.reshape(sequence_length, KEY_VALUE_HEADS, group, HEAD_SIZE)
    keys = apply_rotary(kr, cosine, sine).astype(bf16)
    position = jnp.arange(sequence_length)
    allowed = (position[None, :] <= position[:, None]) & (segments[:, None] == segments[None, :])
    scores = jnp.einsum("qkgd,skd->kgqs", queries, keys, preferred_element_type=f32) * head_scale
    scores = jnp.where(allowed, scores, -1e30)
    top_score = jnp.max(scores, axis=-1, keepdims=True)
    exp_scores = jnp.exp(scores - top_score)
    sum_exp = jnp.sum(exp_scores, axis=-1, keepdims=True)
    log_total = top_score + jnp.log(sum_exp)
    probs = (exp_scores / sum_exp).astype(bf16)
    mixed = jnp.einsum("kgqs,skd->qkgd", probs, values, preferred_element_type=f32)
    mixed = mixed.reshape(sequence_length, QUERY_HEADS * HEAD_SIZE).astype(bf16)
    middle = hidden + jnp.dot(mixed, w_o, preferred_element_type=f32)
    normed_two_f, scale_two = normalize(middle, gain_two)
    h2 = normed_two_f.astype(bf16)
    kept = (scale_one, h1, queries, keys, values, allowed, log_total, mixed, middle, scale_two)
    return h2, kept


def router_forward(h2, w_router, routes):
    logits = jnp.dot(h2, w_router, preferred_element_type=f32)
    probs = softmax_rows(logits)
    experts = w_router.shape[1]
    chosen = jnp.any(
        routes[:, :, None] == jnp.arange(experts, dtype=jnp.int32)[None, None, :], axis=1
    )
    picked = jnp.where(chosen, probs, 0.0)
    total = jnp.sum(picked, axis=-1, keepdims=True)
    return probs, chosen, total, picked / total


def router_backward(h2, w_router, probs, chosen, total, gates, gate_grads):
    gate_grads = jnp.where(chosen, gate_grads, 0.0)
    weighted = jnp.sum(gate_grads * gates, axis=-1, keepdims=True)
    prob_grad = jnp.where(chosen, (gate_grads - weighted) / total, 0.0)
    logit_grad = probs * (prob_grad - jnp.sum(prob_grad * probs, axis=-1, keepdims=True))
    logit_grad = logit_grad.astype(bf16)
    return contract(h2, logit_grad, 0, 0), contract(logit_grad, w_router, 1, 1)


def attention_backward(hidden, kept, gain_one, w_q, w_k, w_v, w_o, gain_two, upstream, dh2):
    scale_one, h1, queries, keys, values, allowed, log_total, mixed, middle, scale_two = kept
    sequence_length = hidden.shape[0]
    group = QUERY_HEADS // KEY_VALUE_HEADS
    head_scale = HEAD_SIZE ** (-0.5)
    cosine, sine = tables(sequence_length, HEAD_SIZE)
    middle_norm_grad, gain_two_grad = norm_back(middle, scale_two, gain_two, dh2)
    middle_grad = upstream + middle_norm_grad
    branch_grad = middle_grad.astype(bf16)
    out_proj_sum = contract(mixed, branch_grad, 0, 0)
    mixed_grad = contract(branch_grad, w_o, 1, 1).astype(bf16)
    mixed_grad = mixed_grad.reshape(sequence_length, KEY_VALUE_HEADS, group, HEAD_SIZE)
    probs = jnp.exp(
        jnp.einsum("qkgd,skd->kgqs", queries, keys, preferred_element_type=f32) * head_scale
        - log_total
    )
    probs = jnp.where(allowed, probs, 0.0)
    prob_back = jnp.einsum("qkgd,skd->kgqs", mixed_grad, values, preferred_element_type=f32)
    score_grad = probs * (prob_back - jnp.sum(prob_back * probs, axis=-1, keepdims=True))
    score_grad = score_grad.astype(bf16)
    dq = jnp.einsum("kgqs,skd->qkgd", score_grad, keys, preferred_element_type=f32) * head_scale
    dq = dq.reshape(sequence_length, QUERY_HEADS, HEAD_SIZE)
    dq = apply_rotary(dq, cosine, -sine).astype(bf16)
    dq = dq.reshape(sequence_length, QUERY_HEADS * HEAD_SIZE)
    dk = jnp.einsum("kgqs,qkgd->skd", score_grad, queries, preferred_element_type=f32) * head_scale
    dk = apply_rotary(dk, cosine, -sine).astype(bf16)
    dk = dk.reshape(sequence_length, KEY_VALUE_HEADS * HEAD_SIZE)
    dv = jnp.einsum("kgqs,qkgd->skd", probs.astype(bf16), mixed_grad, preferred_element_type=f32)
    dv = dv.astype(bf16).reshape(sequence_length, KEY_VALUE_HEADS * HEAD_SIZE)
    query_sum = contract(h1, dq, 0, 0)
    key_sum = contract(h1, dk, 0, 0)
    value_sum = contract(h1, dv, 0, 0)
    dh1 = contract(dq, w_q, 1, 1) + contract(dk, w_k, 1, 1) + contract(dv, w_v, 1, 1)
    hidden_norm_grad, gain_one_grad = norm_back(hidden, scale_one, gain_one, dh1)
    hidden_grad = (middle_grad + hidden_norm_grad).astype(bf16)
    return hidden_grad, (
        gain_one_grad,
        query_sum,
        key_sum,
        value_sum,
        out_proj_sum,
        gain_two_grad,
    )


def reduce_over_all(value, dimension):
    value = lax.psum_scatter(
        value.astype(bf16), "shard", scatter_dimension=dimension, tiled=True
    ).astype(f32)
    return lax.psum(value.astype(bf16), "rep").astype(f32)


def local(
    hidden_in,
    segment_ids,
    routes,
    out_grad,
    norm1_gain,
    w_query,
    key_weight,
    value_weight,
    w_out,
    norm2_gain,
    w_router,
    w_gate,
    w_up,
    w_down,
):
    small = jnp.concatenate(
        [norm1_gain[None], norm2_gain[None], w_router.T, jnp.zeros((6, HALF), bf16)], axis=0
    )
    w_q, w_k, w_v, w_o, small, g4, w0 = gather_call(
        w_query, key_weight, value_weight, w_out, small, out_grad, w_gate, w_up, w_down
    )
    whole = lambda w: w.reshape(MODEL_WIDTH, w.shape[-1])
    w_q, w_k, w_v, w_o = whole(w_q), whole(w_k), whole(w_v), whole(w_o)
    small = small.transpose(1, 0, 2).reshape(16, MODEL_WIDTH)
    gain_one, gain_two = small[0].astype(f32), small[1].astype(f32)
    router = small[2:10].T
    hidden = hidden_in.astype(f32)
    h2, kept = attention_forward(
        hidden, segment_ids[0], gain_one, w_q, w_k, w_v, w_o, gain_two
    )
    probs, chosen, total, gates = router_forward(h2, router, routes)
    high = gates.astype(bf16)
    low = (gates - high.astype(f32)).astype(bf16)
    hg = jnp.concatenate([h2, high, low, jnp.zeros((ROWS, PAD - 16), bf16)], axis=1)
    r_own, r_core, r_x, o_own, o_core, o_x, grads = expert_call(
        hg, g4.reshape(4 * ROWS, MODEL_WIDTH), w0, w_gate, w_up, w_down
    )
    add = lambda a, b, c: a.astype(f32) + b.astype(f32) + c.astype(f32)
    middle = kept[8]
    hidden_out = (middle + add(o_own, o_core, o_x)).astype(bf16)
    returned = add(r_own, r_core, r_x)
    gate_grads = returned[:, 1536:1544] + returned[:, 1544:1552]
    router_sum, routed = router_backward(h2, router, probs, chosen, total, gates, gate_grads)
    dh2 = routed + returned[:, :MODEL_WIDTH]
    hidden_grad, sums = attention_backward(
        hidden, kept, gain_one, w_q, w_k, w_v, w_o, gain_two, out_grad.astype(f32), dh2
    )
    attn = [reduce_over_all(value, 0) for value in sums + (router_sum,)]
    grads = [grads[m].astype(f32) for m in range(3)]
    return (hidden_out, hidden_grad, *attn, *grads)


def local_any(
    hidden_in,
    segment_ids,
    routes,
    out_grad,
    norm1_gain,
    w_query,
    key_weight,
    value_weight,
    w_out,
    norm2_gain,
    w_router,
    w_gate,
    w_up,
    w_down,
):
    wide = lambda w, axis: lax.all_gather(w, "shard", axis=axis, tiled=True)
    gain_one, gain_two = wide(norm1_gain, 0).astype(f32), wide(norm2_gain, 0).astype(f32)
    w_q, w_k, w_v, w_o = (wide(w, 0) for w in (w_query, key_weight, value_weight, w_out))
    router = wide(w_router, 0)
    hidden = hidden_in.astype(f32)
    h2, kept = attention_forward(
        hidden, segment_ids[0], gain_one, w_q, w_k, w_v, w_o, gain_two
    )
    probs, chosen, total, gates = router_forward(h2, router, routes)
    full = [wide(w, 1) for w in (w_gate, w_up, w_down)]

    def expert(carry, inputs):
        mixed, dh2 = carry
        gate_weight, up_weight, down_weight, gate = inputs
        gate = gate[:, None]
        ug = jnp.dot(h2, gate_weight, preferred_element_type=f32)
        uu = jnp.dot(h2, up_weight, preferred_element_type=f32)
        dh = jnp.dot(out_grad, down_weight, preferred_element_type=f32)
        sigma = jax.nn.sigmoid(ug)
        silu = ug * sigma
        hid = silu * uu
        gate_grad = jnp.sum(hid * dh, axis=1)
        hidden_rows = (hid * gate).astype(bf16)
        dug = (dh * gate * uu * sigma * (1.0 + ug * (1.0 - sigma))).astype(bf16)
        duu = (dh * gate * silu).astype(bf16)
        mixed = mixed + contract(hidden_rows, down_weight, 1, 1)
        dh2 = dh2 + contract(dug, gate_weight, 1, 1) + contract(duu, up_weight, 1, 1)
        sums = (contract(h2, dug, 0, 0), contract(h2, duu, 0, 0))
        sums = sums + (contract(out_grad, hidden_rows, 0, 0),)
        return (mixed, dh2), (gate_grad, *(s.astype(bf16) for s in sums))

    zeros = jnp.zeros(hidden.shape, f32)
    (mixed, dh2), (gate_grads, *sums) = lax.scan(expert, (zeros, zeros), (*full, gates.T))
    hidden_out = (kept[8] + mixed).astype(bf16)
    router_sum, routed = router_backward(h2, router, probs, chosen, total, gates, gate_grads.T)
    hidden_grad, attn = attention_backward(
        hidden, kept, gain_one, w_q, w_k, w_v, w_o, gain_two, out_grad.astype(f32), routed + dh2
    )
    attn = [reduce_over_all(value, 0) for value in attn + (router_sum,)]
    grads = [reduce_over_all(value, 1) for value in sums]
    return (hidden_out, hidden_grad, *attn, *grads)


def solution(mesh):
    rows, vector, matrix = P(("rep", "shard"), None), P("shard"), P("shard", None)
    stack = P(None, "shard", None)
    in_specs = (
        rows, rows, rows, rows, vector, matrix, matrix, matrix, matrix, vector, matrix,
        stack, stack, stack,
    )
    out_specs = (
        rows, rows, vector, matrix, matrix, matrix, matrix, vector, matrix, stack, stack, stack,
    )
    fits = dict(mesh.shape) == {"rep": 16, "shard": 2}
    body = local if fits else local_any
    return jax.shard_map(body, mesh=mesh, in_specs=in_specs, out_specs=out_specs, check_vma=False)
```

time: 2490 us -> 1090 us (0.44)
  waiting for transfers between devices: 1850 us -> 152 us
  Pallas kernels: 0 us -> 672 us
  matrix products: 251 us -> 74.9 us
  local copies, waits for them, and re-layouts: 145 us -> 22.4 us
  blocking collectives: 111 us -> 66.6 us
  other arithmetic: 110 us -> 77.1 us
    pallas_call x0 -> x2, Pallas kernels: none -> 672 us  [the longest x1 345 us: expert_call(): pl.pallas_call(expert_kernel, out_shape=[jax.ShapeDtypeStruct(s, bf16) fo...]
    all_gather x5 -> x0, waiting for transfers between devices: 625 us -> none  [the longest x1 206 us: local(): lax.all_gather(w_up, 'shard', axis=1, tiled=True)]
    reduce_scatter x8 -> x5, waiting for transfers between devices: 711 us -> 109 us  [reduce_over_all(): lax.psum_scatter(value.astype(bf16), 'shard', scatter_dimension=dimension...]
    psum x1, waiting for transfers between devices: 510 us -> 42.9 us  [reduce_over_all(): return lax.psum(value.astype(bf16), 'rep').astype(f32)]
    dot_general x20 -> x11, matrix products: 222 us -> 43.3 us  [the longest x1 7.85 us: attention_backward(): jnp.einsum('kgqs,qkgd->skd', probs.astype(bf16), mixed_grad, preferred_el...]
    gather x5 -> x0, local copies, waits for them, and re-layouts: 85.3 us -> none  [the longest x2 34.3 us: local(): padded_up[owner_token]]
    all_gather x5 -> x0, blocking collectives: 41.7 us -> none  [the longest x1 18.2 us: local(): lax.all_gather(value_weight, 'shard', axis=0, tiled=True)]
    reduce_sum x8 -> x4, other arithmetic: 33.2 us -> 3.9 us  [the longest x1 2.65 us: attention_forward(): sum_exp = jnp.sum(exp_scores, axis=-1, keepdims=True)]
  transfers between devices with their start and end apart: 14 -> 6, of which waited for: 10 -> 3; matrix products, arithmetic and copies ran while one was open for 10% -> 8% of each run, Pallas kernels for 0% -> 0%
where the time goes in v1:
time: 1090 us; the launch traced here: 1080 us
  Pallas kernels  672 us (62%)
  waiting for transfers between devices  152 us (14%)
  other arithmetic  77.1 us (7%)
  matrix products  74.9 us (7%)
  blocking collectives  66.6 us (6%)
  local copies, waits for them, and re-layouts  22.4 us (2%)
  between operations  15.9 us (1%)
    pallas_call x1, Pallas kernels, expert_call(): pl.pallas_call(expert_kernel, out_shape=[jax.ShapeDtypeStruct(s, bf16) fo...  345 us
    pallas_call x1, Pallas kernels, gather_call(): pl.pallas_call(gather_kernel, out_shape=[jax.ShapeDtypeStruct(s, bf16) fo...  327 us
    reduce_scatter x5, waiting for transfers between devices, reduce_over_all(): lax.psum_scatter(value.astype(bf16), 'shard', scatter_dimension=dimension...  109 us
    psum x1, blocking collectives, reduce_over_all(): return lax.psum(value.astype(bf16), 'rep').astype(f32)  61.6 us
    psum x1, waiting for transfers between devices, reduce_over_all(): return lax.psum(value.astype(bf16), 'rep').astype(f32)  42.9 us
    dot_general x10, matrix products, contract(): lax.dot_general(left_side, right_side, (((left_dim,), (right_dim,)), ((),...  31.7 us
    convert_element_type x1, other arithmetic, local(): grads = [grads[m].astype(f32) for m in range(3)]  27.9 us
  transfers between devices with their start and end apart: 6, of which 3 were waited for; matrix products, arithmetic and copies ran while one was open for 8% of the time, Pallas kernels for 0%

profile of v1, /device:TPU:0, one launch (start us, length us, event | category | flops | bytes accessed | tf_op | source)
XLA Modules:
  0.0 1081.3 jit_solution(2307434466397655853)
XLA Ops:
  10.1 327.0 %gather_weights.1 = (bf16[2,768,1536]{2,1,0:T(8,128)(2,1)}, bf16[2,768,256]{2,1,0:T(8,128)(2,1)}, bf16[2,768,256]{2,1,0:T(8,128)(2,1)}, bf16[2,768,1536]{2,1,0:T...) custom-call(bf16[768,1536]{1,0:T(8,128)(2,1)} %wq.1, ...), custom_call_target="tpu_custom_call" | custom-call | tf_op jit(solution)/shard_map/gather_weights/pallas_call | solution.py:200
  343.2 2.7 convolution_convert_fusion.6
  346.7 6.6 copy.66
  353.3 4.7 fusion.29
  359.7 2.3 fusion.5
  361.9 2.6 fusion.6
  366.7 3.9 fusion.28
  370.6 5.3 multiply_reduce_fusion.2
  380.6 344.8 %experts.1 = (bf16[512,1664]{1,0:T(8,128)(2,1)}, bf16[512,1664]{1,0:T(8,128)(2,1)}, bf16[512,1664]{1,0:T(8,128)(2,1)}, bf16[512,1536]{1,0:T(8,128)(2,1)}, bf16[5...) custom-call(bf16[512,1664]{1,0:T(8,128)(2,1)} %concatenate.39.hg, ...), custom_call_target="tpu_custom_call" | custom-call | tf_op jit(solution)/shard_map/experts/pallas_call | solution.py:663
  725.4 3.2 convert_add_fusion.1
  732.5 3.1 subtract_add_fusion
  735.6 4.5 convolution_convert_fusion.2
  741.7 7.8 fusion.36
  751.4 7.5 fusion
  759.0 7.2 fusion.2
  766.3 2.1 broadcast_multiply_fusion.1
  770.9 7.2 convolution_convert_fusion
  779.1 5.7 bitcast_multiply_fusion.2
  785.3 2.2 broadcast_multiply_fusion
  788.5 4.6 convolution_convert_fusion.1
  796.7 3.8 fusion.27
  800.5 5.2 fusion.69
  806.9 2.9 fusion.22
  809.8 46.0 %reduce-scatter.12.cloned.1.call-done = bf16[768,1536]{1,0:T(8,128)(2,1)} async-done(((bf16[1536,1536]{1,0:T(8,128)(2,1)}), bf16[768,1536]{1,0:T(8,128)(2,1)}) %reduce-scatter.12.cloned.1.call-update) | async-done | bytes 2359312 | tf_op jit(solution)/shard_map/reduce_scatter | solution.py:777
  855.8 62.9 %reduce-scatter.6.cloned.1.call-done = bf16[768,1536]{1,0:T(8,128)(2,1)} async-done(((bf16[1536,1536]{1,0:T(8,128)(2,1)}), bf16[768,1536]{1,0:T(8,128)(2,1)}) %reduce-scatter.6.cloned.1.call-update) | async-done | bytes 2359312 | tf_op jit(solution)/shard_map/reduce_scatter | solution.py:777
  918.7 4.9 fusion.19
  924.9 5.0 all-reduce.4
  930.1 27.9 %bitcast_convert_fusion = (f32[8,768,768]{2,1,0:T(8,128)}, f32[8,768,768]{2,1,0:T(8,128)}, f32[8,768,768]{2,1,0:T(8,128)}) fusion(bf16[3,8,768,768]{3,2,1,0:T(8,128)(2,1)} %get-tuple-element.39), kind=kLoop, calls=%fused_computation.13 | loop fusion | flops 14155776 | bytes 84934656 | tf_op jit(solution)/shard_map/convert_element_type | solution.py:832
  958.0 61.6 %all-reduce.2 = (bf16[768]{0:T(1024)(128)(2,1)S(1)}, bf16[768]{0:T(1024)(128)(2,1)S(1)}, bf16[768,8]{0,1:T(8,128)(2,1)S(1)}) all-reduce(bf16[768]{0:T(1024)(128)(2,1)S(1)} %dynamic-slice.1, bf16[768]{0:T(1024)(128)(2,1)S(1)} %dynamic-slice.3, ...), channel_id=1, replica_groups=mesh['rep'=16,'shard'=2] {'rep'}, use_global_device_ids=true, to_apply=%region_15.16 | all-reduce | flops 7680 | bytes 30720 | tf_op jit(solution)/shard_map/psum | solution.py:780
  1021.4 42.9 %all-reduce.7.cloned.1.call-done = (bf16[768,1536]{1,0:T(8,128)(2,1)}, bf16[768,256]{1,0:T(8,128)(2,1)}, bf16[768,256]{1,0:T(8,128)(2,1)}, bf16[768,1536]{1,0:T(8,128)(2,1)}) async-done(((bf16[768,1536]{1,0:T(8,128)(2,1)}, bf16[768,256]{1,0:T(8,128)(2,1)}, bf16[768,256]{1,0:T(8,128)(2,1)}, bf16[768,1536]{1,0:T(8,128)(2,1)}), (bf16[768,1536]{1,0:T(8,128)(2,1)}, bf16[768,256]{1,0:T(8,128)(2,1)}, ...) | async-done | bytes 5505040 | tf_op jit(solution)/shard_map/psum | solution.py:780
  1068.3 2.8 convert_element_type.235
  1071.1 2.8 convert_element_type.241
  (161 shorter events, 41.3 us)
Async XLA Ops:
  7.2 802.6 %reduce-scatter.10.cloned.1.call-start = ((), (), s32[]{:S(2)}) async-start(), calls=%async_computation.7 | async-start | bytes 1179648 | tf_op jit(solution)/shard_map/reduce_scatter | solution.py:777
  10.1 328.8 %copy-start.8 = (bf16[512,1536]{1,0:T(8,128)(2,1)S(1)}, bf16[512,1536]{1,0:T(8,128)(2,1)}, u32[]{:S(2)}) copy-start(bf16[512,1536]{1,0:T(8,128)(2,1)} %param.14) | copy-start | bytes 4718596
  10.1 329.7 %copy-start.40 = (s32[512,4]{0,1:T(4,128)S(1)}, s32[512,4]{0,1:T(4,128)}, u32[]{:S(2)}) copy-start(s32[512,4]{0,1:T(4,128)} %param.16) | copy-start | bytes 24580
  10.1 330.0 %copy-start.37 = (s32[1,512]{1,0:T(1,128)S(1)}, s32[1,512]{1,0:T(1,128)}, u32[]{:S(2)}) copy-start(s32[1,512]{1,0:T(1,128)} %param.15) | copy-start | bytes 6148
  337.1 4.9 copy-start.16
  339.8 13.5 %copy-start.35 = (f32[512]{0:T(512)}, f32[512]{0:T(512)S(1)}, u32[]{:S(2)}) copy-start(f32[512]{0:T(512)S(1)} %get-tuple-element.79) | copy-start | bytes 6148
  340.3 24.3 %copy-start.10 = (pred[512,512]{0,1:T(8,128)(4,1)}, pred[512,512]{0,1:T(8,128)(4,1)S(1)}, u32[]{:S(2)}) copy-start(pred[512,512]{0,1:T(8,128)(4,1)S(1)} %fusion.39) | copy-start | bytes 786436
  342.0 16.7 %copy-start.14 = (f32[512,128]{0,1:T(8,128)}, f32[512,128]{0,1:T(8,128)S(1)}, u32[]{:S(2)}) copy-start(f32[512,128]{0,1:T(8,128)S(1)} %get-tuple-element.77) | copy-start | bytes 786436
  361.9 4.8 copy-start
  361.9 4.8 copy-start.31
  370.6 5.4 copy-start.42
  376.3 4.3 copy-start.4
  725.4 4.2 copy-start.3
  729.6 2.9 copy-start.25
  729.6 6.0 slice-start
  732.5 3.1 slice-start.1
  741.7 7.9 copy-start.9
  741.7 7.9 copy-start.36
  749.6 9.3 copy-start.33
  751.3 58.5 %reduce-scatter.8.cloned.1.call-start = ((), (), s32[]{:S(2)}) async-start(), calls=%async_computation.6 | async-start | bytes 1179648 | tf_op jit(solution)/shard_map/reduce_scatter | solution.py:777
  758.9 7.3 copy-start.7
  769.2 9.0 copy-start.27
  770.9 84.9 %reduce-scatter.12.cloned.1.call-start = ((), (), s32[]{:S(2)}) async-start(), calls=%async_computation.8 | async-start | bytes 7077888 | tf_op jit(solution)/shard_map/reduce_scatter | solution.py:777
  778.2 140.5 %reduce-scatter.6.cloned.1.call-start = ((), (), s32[]{:S(2)}) async-start(), calls=%async_computation.5 | async-start | bytes 7077888 | tf_op jit(solution)/shard_map/reduce_scatter | solution.py:777
  793.1 164.9 %reduce-scatter.14.cloned.1.call-start = ((), (), s32[]{:S(2)}) async-start(), calls=%async_computation.9 | async-start | bytes 36864 | tf_op jit(solution)/shard_map/reduce_scatter | solution.py:777
  796.6 267.7 %all-reduce.7.cloned.1.call-start = ((), (), s32[]{:S(2)}) async-start(), calls=%async_computation.10 | async-start | bytes 11010048 | tf_op jit(solution)/shard_map/psum | solution.py:780
  800.4 5.2 copy-start.17
  800.5 5.2 copy-start.28
  809.8 108.9 %copy-start.41 = (f32[512]{0:T(512)S(1)}, f32[512]{0:T(512)}, u32[]{:S(2)}) copy-start(f32[512]{0:T(512)} %get-tuple-element.78) | copy-start | bytes 6148
  918.7 5.0 copy-start.43
  1064.3 4.0 copy-start.21
  1068.3 2.8 copy-start.20
  (20 other events, 35.8 us)
Sparse Core Ops, SparseCore 0:
  751.5 21.0 reduce-scatter.9
  775.4 17.4 reduce-scatter.7
  795.8 59.9 reduce-scatter.11
  858.6 59.9 reduce-scatter.5
  921.3 9.8 reduce-scatter.13
  934.9 129.3 all-reduce.6

commit v2 on v1

--- a/solution.py
+++ b/solution.py
@@ -99,7 +99,7 @@
 def gather_kernel(
     wq, wk, wv, wo, sm, g, wg, wu, wd,
     wqf, wkf, wvf, wof, smf, g4, w0,
-    loc, y_s, y_r, x_s, x_r, c_s, c_r, d_s, d_r, z_s, z_r,
+    bq, bk, bv, bo, bs, bg, loc, y_s, y_r, x_s, x_r, c_s, c_r, d_s, d_r, z_s, z_r,
 ):
     z, x, c, y = place()
     ydev, xdev, cdev = at(z, x, c, 1 - y), at(z, 1 - x, c, y), at(z, x, 1 - c, y)
@@ -124,24 +124,22 @@
         ys.append(
             remote(
                 experts[m].at[expert, pl.ds(h * 384, 384)],
-                w0.at[m, pl.ds(y * HALF + h * 384, 384)],
+                w0.at[m, pl.ds(h * 384, 384)],
                 y_s.at[5 + m],
                 y_r.at[5 + m],
                 ydev,
             )
         )
         ys[5 + m].start()
-    locs = [pltpu.make_async_copy(parts[a], fulls[a].at[y], loc.at[a]) for a in range(4)]
-    locs.append(pltpu.make_async_copy(sm, smf.at[y], loc.at[4]))
-    locs.append(pltpu.make_async_copy(g, g4.at[0], loc.at[5]))
-    for m in range(3):
-        locs.append(
-            pltpu.make_async_copy(
-                experts[m].at[expert], w0.at[m, pl.ds(y * HALF, HALF)], loc.at[6 + m]
-            )
-        )
-    for copy in locs:
+    pairs = [(parts[a], (bq, bk, bv, bo)[a], fulls[a].at[y]) for a in range(4)]
+    pairs += [(sm, bs, smf.at[y]), (g, bg, g4.at[0])]
+    loads = [pltpu.make_async_copy(p[0], p[1], loc.at[i]) for i, p in enumerate(pairs)]
+    locs = [pltpu.make_async_copy(p[1], p[2], loc.at[6 + i]) for i, p in enumerate(pairs)]
+    for copy in loads:
         copy.start()
+    for i in range(6):
+        loads[i].wait()
+        locs[i].start()
     for a in range(4):
         ys[a].wait_recv()
         xs.append(
@@ -167,7 +165,7 @@
         ds[a].start()
     for m in range(3):
         ys[5 + m].wait_recv()
-        rows = pl.ds((1 - y) * HALF + h * 384, 384)
+        rows = pl.ds(h * 384, 384)
         zs.append(remote(w0.at[m, rows], w0.at[m, rows], z_s.at[m], z_r.at[m], zdev))
         zs[m].start()
     xs_g.wait_recv()
@@ -194,7 +192,7 @@
         (2, HALF, MODEL_WIDTH),
         (2, 16, HALF),
         (4, ROWS, MODEL_WIDTH),
-        (3, MODEL_WIDTH, FF),
+        (3, HALF, FF),
     ]
     dma = pltpu.SemaphoreType.DMA
     return pl.pallas_call(
@@ -202,7 +200,14 @@
         out_shape=[jax.ShapeDtypeStruct(s, bf16) for s in shapes],
         in_specs=[anyspace] * 9,
         out_specs=[anyspace] * 7,
-        scratch_shapes=[dma((9,)), dma((8,)), dma((8,))] + [dma((5,))] * 6 + [dma((3,))] * 2,
+        scratch_shapes=[
+            pltpu.VMEM(s, bf16)
+            for s in (
+                (HALF, MODEL_WIDTH), (HALF, 256), (HALF, 256), (HALF, MODEL_WIDTH), (16, HALF),
+                (ROWS, MODEL_WIDTH),
+            )
+        ]
+        + [dma((12,)), dma((8,)), dma((8,))] + [dma((5,))] * 6 + [dma((3,))] * 2,
         compiler_params=pltpu.CompilerParams(collective_id=1, has_side_effects=True),
         name="gather_weights",
     )(wq, wk, wv, wo, sm, g, wg, wu, wd)
@@ -233,12 +238,18 @@
     own = [
         pltpu.make_async_copy(hg, H.at[pl.ds(0, ROWS)], loc.at[0]),
         pltpu.make_async_copy(g4, G, loc.at[1]),
-        pltpu.make_async_copy(w0, W.at[0], loc.at[2]),
+        pltpu.make_async_copy(w0, W.at[0, :, pl.ds((1 - y) * HALF, HALF)], loc.at[2]),
     ]
     for m in range(3):
         own.append(
             pltpu.make_async_copy(
                 shards[m].at[e0 + 1], W.at[1, m, pl.ds(y * HALF, HALF)], loc.at[3 + m]
+            )
+        )
+    for m in range(3):
+        own.append(
+            pltpu.make_async_copy(
+                shards[m].at[e0], W.at[0, m, pl.ds(y * HALF, HALF)], loc.at[6 + m]
             )
         )
     wys = []
@@ -483,6 +494,8 @@
     own[1].wait()
     own[2].wait()
     own[0].wait()
+    for m in range(3):
+        own[6 + m].wait()
     hc.wait_recv()
     forward(0, 0)
     hx.wait_recv()
@@ -653,7 +666,7 @@
         vmem(4, CHUNK, FF),
         vmem(2, CHUNK, FF),
         vmem(4, CHUNK, FF),
-        dma((6,)), dma((3,)), dma((3,)), dma((3,)), dma((3,)), dma((3,)), dma((3,)),
+        dma((9,)), dma((3,)), dma((3,)), dma((3,)), dma((3,)), dma((3,)), dma((3,)),
         dma((2,)), dma((CHUNKS,)), dma((CHUNKS,)), dma((2,)), dma((2,)),
         dma((CHUNKS,)), dma((CHUNKS,)), dma((2,)), dma((CHUNKS,)), dma((CHUNKS,)), dma((2,)),
         dma((CHUNKS,)), dma((CHUNKS,)), dma((4,)), dma((CHUNKS,)), dma((CHUNKS,)),
@@ -671,6 +684,258 @@
         ),
         name="experts",
     )(hg, g4, w0, wg, wu, wd)[:7]
+
+
+BLOCKS = 7
+WIDTH = 512
+SIXTH = 192
+
+
+def attention_kernel(
+    d, sm, out, smo, ca, ya, xa, za, zb, sa, VA, VB, PP, VY, QQ, VX, VS, VZ, VT, VF, FN, SA, SB, SC,
+    loc, c_s, c_r, ld, y_s, y_r, ldy, x_s, x_r, ldx, z1_s, z1_r, ldz, z2_s, z2_r, ldf, z3_s, z3_r,
+    fo, xg_s, xg_r, c1_s, c1_r, c2_s, c2_r, s_s, s_r, sl,
+):
+    z, x, c, y = place()
+    mid = (z == 1) | (z == 2)
+    ydev, xdev, cdev = at(z, x, c, 1 - y), at(z, 1 - x, c, y), at(z, x, 1 - c, y)
+    zdev = at(z + 1 - 2 * (z % 2), x, c, y)
+    mdev = at(3 - z, x, c, y)
+    greet((ydev, xdev, cdev, zdev, mdev))
+
+    def c_copy(k):
+        return remote(
+            d.at[k, :, pl.ds((1 - c) * 384, 384)], ca.at[k], c_s.at[k], c_r.at[k], cdev
+        )
+
+    def load_a(k):
+        return pltpu.make_async_copy(
+            d.at[k, :, pl.ds(c * 384, 384)], VA.at[k % 2], ld.at[0, k % 2]
+        )
+
+    def load_b(k):
+        return pltpu.make_async_copy(ca.at[k], VB.at[k % 2], ld.at[1, k % 2])
+
+    def y_copy(k):
+        return remote(PP.at[k % 4, 1 - y], ya.at[k], y_s.at[k], y_r.at[k], ydev)
+
+    def load_y(k):
+        return pltpu.make_async_copy(ya.at[k], VY.at[k % 2], ldy.at[k % 2])
+
+    def x_copy(k):
+        return remote(
+            QQ.at[k % 4, pl.ds((1 - x) * SIXTH, SIXTH)], xa.at[k], x_s.at[k], x_r.at[k], xdev
+        )
+
+    def load_x(k):
+        return pltpu.make_async_copy(xa.at[k], VX.at[k % 2], ldx.at[k % 2])
+
+    def z1_copy(k):
+        return remote(VS.at[k % 8], za.at[k], z1_s.at[k], z1_r.at[k], zdev)
+
+    def load_z(k):
+        return pltpu.make_async_copy(za.at[k], VZ.at[k % 2], ldz.at[k % 2])
+
+    def z2_copy(k):
+        return remote(VT.at[k % 4], zb.at[k], z2_s.at[k], z2_r.at[k], mdev)
+
+    def load_f(k):
+        return pltpu.make_async_copy(zb.at[k], VF.at[k % 2], ldf.at[k % 2])
+
+    def spot(k, xx, cc):
+        return out.at[k, pl.ds(cc * 384 + xx * SIXTH, SIXTH)]
+
+    def z3_copy(k):
+        return remote(FN.at[k % 4], spot(k, x, c), z3_s.at[k], z3_r.at[k], zdev)
+
+    def store_f(k):
+        return pltpu.make_async_copy(FN.at[k % 4], spot(k, x, c), fo.at[k % 4])
+
+    def xg_copy(k):
+        return remote(spot(k, x, c), spot(k, x, c), xg_s.at[k], xg_r.at[k], xdev)
+
+    def c1_copy(k):
+        return remote(spot(k, x, c), spot(k, x, c), c1_s.at[k], c1_r.at[k], cdev)
+
+    def c2_copy(k):
+        return remote(spot(k, 1 - x, c), spot(k, 1 - x, c), c2_s.at[k], c2_r.at[k], cdev)
+
+    def when(k, cond=None):
+        ok = (k >= 0) & (k < BLOCKS)
+        return pl.when(ok if cond is None else ok & cond)
+
+    def slot(s):
+        @when(s - 13)
+        def _():
+            xg_copy(s - 13).wait_recv()
+            c2_copy(s - 13).start()
+
+        @when(s - 12, mid)
+        def _():
+            store_f(s - 12).wait()
+            z3_copy(s - 12).wait_send()
+
+        @when(s - 12, jnp.logical_not(mid))
+        def _():
+            z3_copy(s - 12).wait_recv()
+            z1_copy(s - 12).wait_send()
+
+        @when(s - 12)
+        def _():
+            xg_copy(s - 12).start()
+            c1_copy(s - 12).start()
+
+        @when(s - 10, mid)
+        def _():
+            k = s - 10
+            load_f(k).wait()
+            z2_copy(k).wait_send()
+            FN[k % 4] = (VT[k % 4].astype(f32) + VF[k % 2].astype(f32)).astype(bf16)
+            z3_copy(k).start()
+            store_f(k).start()
+
+        @when(s - 9, mid)
+        def _():
+            z2_copy(s - 9).wait_recv()
+            load_f(s - 9).start()
+
+        @when(s - 8, mid)
+        def _():
+            k = s - 8
+            load_z(k).wait()
+            VT[k % 4] = (VS[k % 8].astype(f32) + VZ[k % 2].astype(f32)).astype(bf16)
+            z2_copy(k).start()
+
+        @when(s - 7, mid)
+        def _():
+            z1_copy(s - 7).wait_recv()
+            load_z(s - 7).start()
+
+        @when(s - 6)
+        def _():
+            k = s - 6
+            load_x(k).wait()
+            x_copy(k).wait_send()
+            mine = pl.ds(pl.multiple_of(x * SIXTH, SIXTH), SIXTH)
+            VS[k % 8] = (QQ[k % 4, mine, :].astype(f32) + VX[k % 2].astype(f32)).astype(bf16)
+
+        @when(s - 6, jnp.logical_not(mid))
+        def _():
+            z1_copy(s - 6).start()
+
+        @when(s - 5)
+        def _():
+            x_copy(s - 5).wait_recv()
+            load_x(s - 5).start()
+
+        @when(s - 4)
+        def _():
+            k = s - 4
+            load_y(k).wait()
+            y_copy(k).wait_send()
+            QQ[k % 4] = (PP[k % 4, y].astype(f32) + VY[k % 2].astype(f32)).astype(bf16)
+            x_copy(k).start()
+
+        @when(s - 3)
+        def _():
+            y_copy(s - 3).wait_recv()
+            load_y(s - 3).start()
+
+        @when(s - 1)
+        def _():
+            k = s - 1
+            load_a(k).wait()
+            load_b(k).wait()
+            PP[k % 4] = (VA[k % 2].astype(f32) + VB[k % 2].astype(f32)).astype(bf16)
+            y_copy(k).start()
+
+        @when(s)
+        def _():
+            c_copy(s).wait_recv()
+            load_a(s).start()
+            load_b(s).start()
+
+    for k in range(BLOCKS):
+        c_copy(k).start()
+
+    first = pltpu.make_async_copy(sm, SA, sl.at[0])
+    first.start()
+    first.wait()
+
+    def swap(i, device):
+        copy = remote(SC, sa.at[i], s_s.at[i], s_r.at[i], device)
+        copy.start()
+        return copy
+
+    def arrive(i):
+        load = pltpu.make_async_copy(sa.at[i], SB, sl.at[0])
+        load.start()
+        load.wait()
+        return SB[...].astype(f32)
+
+    SC[...] = SA[...]
+    hop = swap(0, cdev)
+    hop.wait()
+    SC[...] = (SC[...].astype(f32) + arrive(0)).astype(bf16)
+    lax.fori_loop(0, 3, lambda s, _: (slot(s), 0)[1], 0)
+    hop = swap(1, xdev)
+    hop.wait()
+    SC[...] = (SC[...].astype(f32) + arrive(1)).astype(bf16)
+    lax.fori_loop(3, 5, lambda s, _: (slot(s), 0)[1], 0)
+    hop = swap(2, ydev)
+    hop.wait()
+    SC[...] = (SC[...].astype(f32) + arrive(2)).astype(bf16)
+    lax.fori_loop(5, 7, lambda s, _: (slot(s), 0)[1], 0)
+    hop = swap(3, zdev)
+    hop.wait()
+    SC[...] = (SC[...].astype(f32) + arrive(3)).astype(bf16)
+    lax.fori_loop(7, 9, lambda s, _: (slot(s), 0)[1], 0)
+    hop = swap(4, mdev)
+    hop.wait()
+    SA[...] = (SC[...].astype(f32) + arrive(4)).astype(bf16)
+    last = pltpu.make_async_copy(SA, smo, sl.at[1])
+    last.start()
+    lax.fori_loop(9, BLOCKS + 13, lambda s, _: (slot(s), 0)[1], 0)
+    last.wait()
+
+    def finish(k, _):
+        c_copy(k).wait_send()
+        xg_copy(k).wait_send()
+        c1_copy(k).wait()
+        c2_copy(k).wait()
+        return 0
+
+    lax.fori_loop(0, BLOCKS, finish, 0)
+
+
+def attention_call(d, sm):
+    anyspace = pl.BlockSpec(memory_space=pl.ANY)
+    dma = pltpu.SemaphoreType.DMA
+    vmem = lambda *s: pltpu.VMEM(s, bf16)
+    n = BLOCKS
+    shapes = [(n, HALF, WIDTH), (2, 16, HALF), (n, 2, 384, WIDTH), (n, 384, WIDTH)]
+    shapes += [(n, SIXTH, WIDTH)] * 3 + [(5, 2, 16, HALF)]
+    scratch = [
+        vmem(2, 2, 384, WIDTH), vmem(2, 2, 384, WIDTH), vmem(4, 2, 384, WIDTH),
+        vmem(2, 384, WIDTH), vmem(4, 384, WIDTH), vmem(2, SIXTH, WIDTH), vmem(8, SIXTH, WIDTH),
+        vmem(2, SIXTH, WIDTH), vmem(4, SIXTH, WIDTH), vmem(2, SIXTH, WIDTH), vmem(4, SIXTH, WIDTH),
+        vmem(2, 16, HALF), vmem(2, 16, HALF), vmem(2, 16, HALF),
+        dma((1,)), dma((n,)), dma((n,)), dma((2, 2)), dma((n,)), dma((n,)), dma((2,)),
+        dma((n,)), dma((n,)), dma((2,)), dma((n,)), dma((n,)), dma((2,)), dma((n,)), dma((n,)),
+        dma((2,)), dma((n,)), dma((n,)), dma((4,)), dma((n,)), dma((n,)), dma((n,)), dma((n,)),
+        dma((n,)), dma((n,)), dma((5,)), dma((5,)), dma((2,)),
+    ]
+    return pl.pallas_call(
+        attention_kernel,
+        out_shape=[jax.ShapeDtypeStruct(s, bf16) for s in shapes],
+        in_specs=[anyspace] * 2,
+        out_specs=[anyspace] * len(shapes),
+        scratch_shapes=scratch,
+        compiler_params=pltpu.CompilerParams(
+            collective_id=3, has_side_effects=True, vmem_limit_bytes=40 * 1000 * 1000
+        ),
+        name="attention_sums",
+    )(d, sm)[:2]
 
 
 def attention_forward(hidden, segments, gain_one, w_q, w_k, w_v, w_o, gain_two):
@@ -828,7 +1093,18 @@
     hidden_grad, sums = attention_backward(
         hidden, kept, gain_one, w_q, w_k, w_v, w_o, gain_two, out_grad.astype(f32), dh2
     )
-    attn = [reduce_over_all(value, 0) for value in sums + (router_sum,)]
+    gain_one_sum, query_sum, key_sum, value_sum, out_sum, gain_two_sum = sums
+    d = jnp.concatenate([query_sum, key_sum, value_sum, out_sum], axis=1).astype(bf16)
+    d = d.reshape(2, HALF, BLOCKS, WIDTH).transpose(2, 0, 1, 3)
+    sm = jnp.concatenate(
+        [gain_one_sum[None], gain_two_sum[None], router_sum.T, jnp.zeros((6, MODEL_WIDTH), f32)],
+        axis=0,
+    )
+    sm = sm.astype(bf16).reshape(16, 2, HALF).transpose(1, 0, 2)
+    d, sm = attention_call(d, sm)
+    d = d.transpose(1, 0, 2).reshape(HALF, BLOCKS * WIDTH).astype(f32)
+    sm = lax.dynamic_index_in_dim(sm, lax.axis_index("shard"), 0, keepdims=False).astype(f32)
+    attn = (sm[0], d[:, :1536], d[:, 1536:1792], d[:, 1792:2048], d[:, 2048:], sm[1], sm[2:10].T)
     grads = [grads[m].astype(f32) for m in range(3)]
     return (hidden_out, hidden_grad, *attn, *grads)
 

time: 1090 us -> 815 us (0.75)
  waiting for transfers between devices: 152 us -> 0 us
  Pallas kernels: 672 us -> 559 us
  local copies, waits for them, and re-layouts: 22.4 us -> 110 us
  blocking collectives: 66.6 us -> 0 us
  matrix products: 74.9 us -> 59.1 us
  between operations: 15.9 us -> 1.71 us
    pallas_call x1, Pallas kernels: 327 us -> 88.3 us  [gather_call(): pl.pallas_call(gather_kernel, out_shape=[jax.ShapeDtypeStruct(s, bf16) fo...]
    pallas_call x0 -> x1, Pallas kernels: none -> 128 us  [attention_call(): pl.pallas_call(attention_kernel, out_shape=[jax.ShapeDtypeStruct(s, bf16)...]
    reduce_scatter x5 -> x0, waiting for transfers between devices: 109 us -> none  [reduce_over_all(): lax.psum_scatter(value.astype(bf16), 'shard', scatter_dimension=dimension...]
    convert_element_type x0 -> x3, local copies, waits for them, and re-layouts: none -> 62 us  [the longest x2 49.9 us: local(): jnp.concatenate([query_sum, key_sum, value_sum, out_sum], axis=1)]
    psum x1 -> x0, blocking collectives: 61.6 us -> none  [reduce_over_all(): return lax.psum(value.astype(bf16), 'rep').astype(f32)]
    psum x1 -> x0, waiting for transfers between devices: 42.9 us -> none  [reduce_over_all(): return lax.psum(value.astype(bf16), 'rep').astype(f32)]
    unnamed x95 -> x86, local copies, waits for them, and re-layouts: 8.54 us -> 23.5 us
    dot_general x10, matrix products: 31.7 us -> 19.7 us  [contract(): lax.dot_general(left_side, right_side, (((left_dim,), (right_dim,)), ((),...]
  transfers between devices with their start and end apart: 6 -> 0, of which waited for: 3 -> 0; matrix products, arithmetic and copies ran while one was open for 8% -> 0% of each run, Pallas kernels for 0% -> 0%
where the time goes in v2:
time: 815 us; the launch traced here: 804 us
  Pallas kernels  559 us (69%)
  local copies, waits for them, and re-layouts  110 us (13%)
  other arithmetic  74.4 us (9%)
  matrix products  59.1 us (7%)
    pallas_call x1, Pallas kernels, expert_call(): pl.pallas_call(expert_kernel, out_shape=[jax.ShapeDtypeStruct(s, bf16) fo...  343 us
    pallas_call x1, Pallas kernels, attention_call(): pl.pallas_call(attention_kernel, out_shape=[jax.ShapeDtypeStruct(s, bf16)...  128 us
    pallas_call x1, Pallas kernels, gather_call(): pl.pallas_call(gather_kernel, out_shape=[jax.ShapeDtypeStruct(s, bf16) fo...  88.3 us
    convert_element_type x2, local copies, waits for them, and re-layouts, local(): jnp.concatenate([query_sum, key_sum, value_sum, out_sum], axis=1)  49.9 us
    convert_element_type x1, other arithmetic, local(): grads = [grads[m].astype(f32) for m in range(3)]  27.6 us
    unnamed x86, local copies, waits for them, and re-layouts  23.5 us
    dot_general x10, matrix products, contract(): lax.dot_general(left_side, right_side, (((left_dim,), (right_dim,)), ((),...  19.7 us

profile of v2, /device:TPU:0, one launch (start us, length us, event | category | flops | bytes accessed | tf_op | source)
XLA Modules:
  0.0 804.3 jit_solution(12896309273969276726)
XLA Ops:
  9.0 88.3 %gather_weights.1 = (bf16[2,768,1536]{2,1,0:T(8,128)(2,1)}, bf16[2,768,256]{2,1,0:T(8,128)(2,1)}, bf16[2,768,256]{2,1,0:T(8,128)(2,1)}, bf16[2,768,1536]{2,1,0:T...) custom-call(bf16[768,1536]{1,0:T(8,128)(2,1)} %wq.1, ...), custom_call_target="tpu_custom_call" | custom-call | tf_op jit(solution)/shard_map/gather_weights/pallas_call | solution.py:198
  99.0 2.6 convolution_convert_fusion.6
  104.8 6.7 copy.61
  111.6 4.7 fusion.29
  117.7 2.3 fusion.5
  120.0 2.6 fusion.6
  122.7 2.1 copy-done
  124.8 4.1 fusion.28
  128.9 5.4 multiply_reduce_fusion.2
  138.9 342.7 %experts.1 = (bf16[512,1664]{1,0:T(8,128)(2,1)}, bf16[512,1664]{1,0:T(8,128)(2,1)}, bf16[512,1664]{1,0:T(8,128)(2,1)}, bf16[512,1536]{1,0:T(8,128)(2,1)}, bf16[5...) custom-call(bf16[512,1664]{1,0:T(8,128)(2,1)} %concatenate.54.hg, ...), custom_call_target="tpu_custom_call" | custom-call | tf_op jit(solution)/shard_map/experts/pallas_call | solution.py:676
  481.7 3.1 convert_add_fusion.1
  489.5 2.7 subtract_add_fusion
  492.2 2.6 convolution_convert_fusion.2
  496.5 7.9 fusion.36
  506.7 4.3 convolution_convert_fusion.1
  512.7 7.0 fusion
  519.6 7.1 fusion.2
  526.8 2.1 broadcast_multiply_fusion.1
  533.1 2.1 fusion.25
  537.4 2.7 fusion.71
  542.6 2.1 fusion.19
  544.9 3.3 convolution_convert_fusion
  548.2 7.3 pad_maximum_fusion
  555.5 22.7 %convert_element_type.196 = bf16[2,768,7,512]{1,0,3,2:T(2,128)(2,1)} reshape(bf16[1536,3584]{0,1:T(8,128)(2,1)} %pad_maximum_fusion) | data formatting | bytes 22020096 | tf_op jit(solution)/shard_map/convert_element_type | solution.py:1097
  578.2 27.2 %copy.75 = bf16[2,768,7,512]{3,1,0,2:T(8,128)(2,1)} copy(bf16[2,768,7,512]{1,0,3,2:T(2,128)(2,1)} %convert_element_type.196) | data formatting | bytes 22020096 | tf_op jit(solution)/shard_map/convert_element_type | solution.py:1097
  605.4 127.8 %attention_sums.1 = (bf16[7,768,512]{2,1,0:T(8,128)(2,1)S(1)}, bf16[2,16,768]{2,1,0:T(8,128)(2,1)S(1)}, bf16[7,2,384,512]{3,2,1,0:T(8,128)(2,1)}, bf16[7,384,512...) custom-call(bf16[7,2,768,512]{3,2,1,0:T(8,128)(2,1)} %bitcast.166, ...), custom_call_target="tpu_custom_call" | custom-call | tf_op jit(solution)/shard_map/attention_sums/pallas_call | solution.py:928
  734.4 5.8 convert_bitcast_fusion
  740.2 12.1 %copy.78 = f32[768,7,512]{0,2,1:T(8,128)} copy(f32[768,7,512]{2,0,1:T(8,128)} %convert_bitcast_fusion) | data formatting | bytes 22020096 | tf_op jit(solution)/shard_map/convert_element_type | solution.py:1105
  753.8 8.1 %fusion.68 = (f32[768,1536]{0,1:T(8,128)}, f32[768,1536]{0,1:T(8,128)}) fusion(f32[768,3584]{0,1:T(8,128)} %bitcast.168), kind=kLoop, calls=%fused_computation.134 | loop fusion | bytes 18874368 | tf_op jit(solution)/shard_map/slice | solution.py:1107
  761.9 6.0 copy.82
  770.3 6.0 copy.79
  776.3 27.6 %bitcast_convert_fusion = (f32[8,768,768]{2,1,0:T(8,128)}, f32[8,768,768]{2,1,0:T(8,128)}, f32[8,768,768]{2,1,0:T(8,128)}) fusion(bf16[3,8,768,768]{3,2,1,0:T(8,128)(2,1)} %get-tuple-element.43), kind=kLoop, calls=%fused_computation.15 | loop fusion | flops 14155776 | bytes 84934656 | tf_op jit(solution)/shard_map/convert_element_type | solution.py:1108
  (141 shorter events, 43.4 us)
Async XLA Ops:
  9.0 107.8 %copy-start.13 = (f32[512,128]{0,1:T(8,128)}, f32[512,128]{0,1:T(8,128)S(1)}, u32[]{:S(2)}) copy-start(f32[512,128]{0,1:T(8,128)S(1)} %get-tuple-element.102) | copy-start | bytes 786436
  9.0 90.0 %copy-start.7 = (bf16[512,1536]{1,0:T(8,128)(2,1)S(1)}, bf16[512,1536]{1,0:T(8,128)(2,1)}, u32[]{:S(2)}) copy-start(bf16[512,1536]{1,0:T(8,128)(2,1)} %param.14) | copy-start | bytes 4718596
  97.2 4.3 copy-start.15
  104.8 12.9 %copy-start.17 = (bf16[512,2,128,1]{0,2,3,1:T(8,128)(2,1)}, bf16[512,2,128,1]{0,2,3,1:T(8,128)(2,1)S(1)}, u32[]{:S(2)}) copy-start(bf16[512,2,128,1]{0,2,3,1:T(8,128)(2,1)S(1)} %fusion.46) | copy-start | bytes 786436
  117.7 2.3 copy-start.5
  120.0 4.8 copy-start
  120.0 4.8 copy-start.28
  128.8 5.4 copy-start.32
  134.6 2.3 copy-start.3
  481.6 4.1 copy-start.4
  486.7 2.4 copy-start.22
  486.7 2.8 copy-start.23
  486.7 5.5 slice-start.5
  489.5 2.7 slice-start.6
  492.2 2.7 copy-start.9
  496.5 7.9 copy-start.8
  496.5 9.5 %copy-start.33 = (bf16[2,128,6,512]{3,1,2,0:T(8,128)(2,1)S(1)}, bf16[2,128,6,512]{3,1,2,0:T(8,128)(2,1)}, u32[]{:S(2)}) copy-start(bf16[2,128,6,512]{3,1,2,0:T(8,128)(2,1)} %copy-done.32) | copy-start | bytes 4718596
  504.4 6.6 copy-start.30
  504.4 2.3 copy-start.10
  504.4 6.6 slice-start
  506.7 4.3 slice-start.1
  506.7 5.6 slice-start.2
  506.7 6.0 copy-start.12
  506.7 6.0 copy-start.29
  519.6 7.1 copy-start.6
  526.8 2.2 copy-start.18
  533.1 3.0 slice-start.3
  535.2 2.2 slice-start.4
  537.4 2.7 copy-start.16
  542.6 2.2 copy-start.24
  544.8 3.4 copy-start.25
  544.8 3.4 copy-start.26
  (9 other events, 13.1 us)

commit v3 on v1

v3 whole, which is shorter than its diff:
```python
import functools

import jax
import jax.numpy as jnp
from jax import lax
from jax.experimental import pallas as pl
from jax.experimental.pallas import tpu as pltpu
from jax.sharding import PartitionSpec as P

MODEL_WIDTH = 1536
QUERY_HEADS = 12
KEY_VALUE_HEADS = 2
HEAD_SIZE = 128
TOPK = 4
FF = 768
HALF = 768
ROWS = 512
PAD = 128
WIDE = MODEL_WIDTH + PAD
CHUNK = 96
PER = HALF // CHUNK
CHUNKS = 6 * PER

epsilon = 1e-06
rope_base = 1000000.0
MESH = pl.DeviceIdType.MESH
bf16 = jnp.bfloat16
f32 = jnp.float32


def tables(sequence_length, row_width):
    frequency = rope_base ** (-2.0 * jnp.arange(row_width // 2, dtype=jnp.float32) / row_width)
    angles = jnp.arange(sequence_length, dtype=jnp.float32)[:, None] * frequency[None, :]
    angles = jnp.concatenate([angles, angles], axis=-1)
    return (jnp.cos(angles)[:, None, :], jnp.sin(angles)[:, None, :])


def apply_rotary(values, rotary_cosine, rotary_sine):
    half_width = values.shape[-1] // 2
    turned = jnp.concatenate([-values[..., half_width:], values[..., :half_width]], axis=-1)
    return values * rotary_cosine + turned * rotary_sine


def contract(left_side, right_side, left_dim, right_dim):
    return lax.dot_general(
        left_side,
        right_side,
        (((left_dim,), (right_dim,)), ((), ())),
        preferred_element_type=jnp.float32,
    )


def normalize(values, gain_vector):
    scale_rows = lax.rsqrt(jnp.mean(values * values, axis=-1, keepdims=True) + epsilon)
    return (values * scale_rows * gain_vector, scale_rows)


def norm_back(values, scale_rows, gain_vector, upstream):
    scaled = upstream * gain_vector
    gain_grad = jnp.sum(upstream * values * scale_rows, axis=0)
    inner_sum = jnp.sum(scaled * values, axis=-1, keepdims=True)
    return (scaled * scale_rows - values * scale_rows**3 * inner_sum / values.shape[-1], gain_grad)


def softmax_rows(values):
    top_value = jnp.max(values, axis=-1, keepdims=True)
    exp_values = jnp.exp(values - top_value)
    return exp_values / jnp.sum(exp_values, axis=-1, keepdims=True)


def place():
    rep = lax.axis_index("rep")
    y = lax.axis_index("shard")
    return rep // 4, (rep // 2) % 2, rep % 2, y


def at(z, x, c, y):
    return ((z * 2 + x) * 2 + c, y)


def remote(src, dst, send, recv, device):
    return pltpu.make_async_remote_copy(
        src_ref=src,
        dst_ref=dst,
        send_sem=send,
        recv_sem=recv,
        device_id=device,
        device_id_type=MESH,
    )


def greet(partners):
    barrier = pltpu.get_barrier_semaphore()
    for device in partners:
        pl.semaphore_signal(barrier, inc=1, device_id=device, device_id_type=MESH)
    pl.semaphore_wait(barrier, len(partners))


def gather_kernel(
    wq, wk, wv, wo, sm, g, wg, wu, wd,
    wqf, wkf, wvf, wof, smf, g4, w0,
    bq, bk, bv, bo, bs, bg, loc, y_s, y_r, x_s, x_r, c_s, c_r, d_s, d_r, z_s, z_r,
):
    z, x, c, y = place()
    ydev, xdev, cdev = at(z, x, c, 1 - y), at(z, 1 - x, c, y), at(z, x, 1 - c, y)
    zdev = at(z + 1 - 2 * (z % 2), x, c, y)
    greet((ydev, xdev, cdev, zdev))
    parts, fulls, experts = (wq, wk, wv, wo), (wqf, wkf, wvf, wof), (wg, wu, wd)
    piece = HALF // 4
    mine = pl.ds((2 * x + c) * piece, piece)
    theirs = pl.ds((2 * (1 - x) + c) * piece, piece)
    expert = 2 * (2 * x + c)
    h = z % 2
    ys, xs, cs, ds, zs = [], [], [], [], []
    for a in range(4):
        ys.append(remote(parts[a].at[mine], fulls[a].at[y, mine], y_s.at[a], y_r.at[a], ydev))
        ys[a].start()
    ys.append(remote(sm, smf.at[y], y_s.at[4], y_r.at[4], ydev))
    ys[4].start()
    xs_g = remote(g, g4.at[2], x_s.at[4], x_r.at[4], xdev)
    cs_g = remote(g, g4.at[1], c_s.at[4], c_r.at[4], cdev)
    cs_g.start()
    for m in range(3):
        ys.append(
            remote(
                experts[m].at[expert, pl.ds(h * 384, 384)],
                w0.at[m, pl.ds(h * 384, 384)],
                y_s.at[5 + m],
                y_r.at[5 + m],
                ydev,
            )
        )
        ys[5 + m].start()
    pairs = [(parts[a], (bq, bk, bv, bo)[a], fulls[a].at[y]) for a in range(4)]
    pairs += [(sm, bs, smf.at[y]), (g, bg, g4.at[0])]
    loads = [pltpu.make_async_copy(p[0], p[1], loc.at[i]) for i, p in enumerate(pairs)]
    locs = [pltpu.make_async_copy(p[1], p[2], loc.at[6 + i]) for i, p in enumerate(pairs)]
    for copy in loads:
        copy.start()
    for i in range(6):
        loads[i].wait()
        locs[i].start()
    for a in range(4):
        ys[a].wait_recv()
        xs.append(
            remote(
                fulls[a].at[1 - y, mine], fulls[a].at[1 - y, mine], x_s.at[a], x_r.at[a], xdev
            )
        )
        cs.append(
            remote(
                fulls[a].at[1 - y, mine], fulls[a].at[1 - y, mine], c_s.at[a], c_r.at[a], cdev
            )
        )
        xs[a].start()
        cs[a].start()
    xs_g.start()
    for a in range(4):
        xs[a].wait_recv()
        ds.append(
            remote(
                fulls[a].at[1 - y, theirs], fulls[a].at[1 - y, theirs], d_s.at[a], d_r.at[a], cdev
            )
        )
        ds[a].start()
    for m in range(3):
        ys[5 + m].wait_recv()
        rows = pl.ds(h * 384, 384)
        zs.append(remote(w0.at[m, rows], w0.at[m, rows], z_s.at[m], z_r.at[m], zdev))
        zs[m].start()
    xs_g.wait_recv()
    ds_g = remote(g4.at[2], g4.at[3], d_s.at[4], d_r.at[4], cdev)
    ds_g.start()
    ys[4].wait_recv()
    for copy in ys:
        copy.wait_send()
    for copy in xs + [xs_g]:
        copy.wait_send()
    xs_g = None
    for copy in cs + [cs_g] + ds + [ds_g] + zs:
        copy.wait()
    for copy in locs:
        copy.wait()


def gather_call(wq, wk, wv, wo, sm, g, wg, wu, wd):
    anyspace = pl.BlockSpec(memory_space=pl.ANY)
    shapes = [
        (2, HALF, MODEL_WIDTH),
        (2, HALF, 256),
        (2, HALF, 256),
        (2, HALF, MODEL_WIDTH),
        (2, 16, HALF),
        (4, ROWS, MODEL_WIDTH),
        (3, HALF, FF),
    ]
    dma = pltpu.SemaphoreType.DMA
    return pl.pallas_call(
        gather_kernel,
        out_shape=[jax.ShapeDtypeStruct(s, bf16) for s in shapes],
        in_specs=[anyspace] * 9,
        out_specs=[anyspace] * 7,
        scratch_shapes=[
            pltpu.VMEM(s, bf16)
            for s in (
                (HALF, MODEL_WIDTH), (HALF, 256), (HALF, 256), (HALF, MODEL_WIDTH), (16, HALF),
                (ROWS, MODEL_WIDTH),
            )
        ]
        + [dma((12,)), dma((8,)), dma((8,))] + [dma((5,))] * 6 + [dma((3,))] * 2,
        compiler_params=pltpu.CompilerParams(collective_id=1, has_side_effects=True),
        name="gather_weights",
    )(wq, wk, wv, wo, sm, g, wg, wu, wd)


def nt_dot(a, b):
    return lax.dot_general(a, b, (((1,), (1,)), ((), ())), preferred_element_type=f32)


def tn_dot(a, b):
    return lax.dot_general(a, b, (((0,), (0,)), ((), ())), preferred_element_type=f32)


def turn_table(sine):
    sign = jnp.where(jnp.arange(HEAD_SIZE) < HEAD_SIZE // 2, -1.0, 1.0)
    return sine[:, 0, :] * sign[None, :]


def router_rows(h2, router_rows_t, routes):
    logits = nt_dot(h2, router_rows_t)
    lane = lax.broadcasted_iota(jnp.int32, logits.shape, 1)
    real = lane < 8
    logits = jnp.where(real, logits, -1e30)
    top = jnp.max(logits, axis=1, keepdims=True)
    exp_values = jnp.where(real, jnp.exp(logits - top), 0.0)
    probs = exp_values / jnp.sum(exp_values, axis=1, keepdims=True)
    chosen = lane == routes[:, 0:1]
    for k in range(1, 4):
        chosen = chosen | (lane == routes[:, k : k + 1])
    picked = jnp.where(chosen, probs, 0.0)
    total = jnp.sum(picked, axis=1, keepdims=True)
    return probs, chosen, total, picked / total


def middle_backward(returned, h2, rt, routes, y1, g, gain_two, DL, DY, DA, GS):
    GS[...] = jnp.zeros_like(GS)

    def step(b, _):
        rows = pl.ds(pl.multiple_of(b * 128, 128), 128)
        probs, chosen, total, gates = router_rows(h2(rows), rt[...], routes[rows, :])
        back = returned(rows)
        packed = back[:, MODEL_WIDTH:]
        gate_grads = jnp.where(chosen, packed + pltpu.roll(packed, PAD - 8, 1), 0.0)
        weighted = jnp.sum(gate_grads * gates, axis=1, keepdims=True)
        prob_grad = jnp.where(chosen, (gate_grads - weighted) / total, 0.0)
        inner = jnp.sum(prob_grad * probs, axis=1, keepdims=True)
        logit_grad = (probs * (prob_grad - inner)).astype(bf16)
        DL[rows, :] = logit_grad
        dh2 = back[:, :MODEL_WIDTH] + jnp.dot(logit_grad, rt[...], preferred_element_type=f32)
        v = y1[rows, :]
        r = lax.rsqrt(jnp.mean(v * v, axis=1, keepdims=True) + epsilon)
        GS[...] = GS[...] + jnp.sum(dh2 * v * r, axis=0, keepdims=True)
        scaled = dh2 * gain_two[...]
        along = jnp.sum(scaled * v, axis=1, keepdims=True)
        dy = g[rows, :].astype(f32) + (scaled * r - v * (r * r * r * along / MODEL_WIDTH))
        DY[rows, :] = dy
        DA[rows, :] = dy.astype(bf16)
        return 0

    lax.fori_loop(0, ROWS // 128, step, 0)


def heads_backward(Q, K, V, DOB, BIAS, LSE, COS, SIN, DQKV, DK, DV, tick):
    scale = HEAD_SIZE ** (-0.5)
    DK[...] = jnp.zeros_like(DK)
    DV[...] = jnp.zeros_like(DV)
    for group in range(2):
        shared = pl.ds(group * HEAD_SIZE, HEAD_SIZE)

        def head(n, _, group=group, shared=shared):
            columns = pl.ds(pl.multiple_of((group * 6 + n) * HEAD_SIZE, HEAD_SIZE), HEAD_SIZE)
            lane = lax.broadcasted_iota(jnp.int32, (ROWS, PAD), 1)
            lse = jnp.sum(
                jnp.where(lane == group * 6 + n, LSE[...], 0.0), axis=1, keepdims=True
            )
            for block in range(2):
                rows, keys = pl.ds(block * 256, 256), pl.ds(0, 256 * (block + 1))
                q, dob = Q[rows, columns], DOB[rows, columns]
                k, v = K[keys, shared], V[keys, shared]
                logits = nt_dot(q, k) * scale + BIAS[rows, keys]
                p = jnp.exp(logits - lse[block * 256 : block * 256 + 256])
                dp = nt_dot(dob, v)
                inner = jnp.sum(dp * p, axis=1, keepdims=True)
                ds = (p * (dp - inner)).astype(bf16)
                dq = jnp.dot(ds, k, preferred_element_type=f32) * scale
                dq = dq * COS[rows, :] - pltpu.roll(dq, 64, 1) * SIN[rows, :]
                DQKV[rows, columns] = dq.astype(bf16)
                DK[group, keys, :] = DK[group, keys, :] + tn_dot(ds, q)
                DV[group, keys, :] = DV[group, keys, :] + tn_dot(p.astype(bf16), dob)
            return 0

        for n in range(0, 6, 3):
            lax.fori_loop(n, n + 3, head, 0)
            tick()
        dk = DK[group] * scale
        dk = dk * COS[...] - pltpu.roll(dk, 64, 1) * SIN[...]
        DQKV[:, pl.ds(1536 + group * HEAD_SIZE, HEAD_SIZE)] = dk.astype(bf16)
        DQKV[:, pl.ds(1792 + group * HEAD_SIZE, HEAD_SIZE)] = DV[group].astype(bf16)


def first_backward(DH1, X, DY, gain_one, HG, GS):
    GS[...] = jnp.zeros_like(GS)

    def step(b, _):
        rows = pl.ds(pl.multiple_of(b * 128, 128), 128)
        v, up = X[rows, :].astype(f32), DH1[rows, :]
        r = lax.rsqrt(jnp.mean(v * v, axis=1, keepdims=True) + epsilon)
        GS[...] = GS[...] + jnp.sum(up * v * r, axis=0, keepdims=True)
        scaled = up * gain_one[...]
        along = jnp.sum(scaled * v, axis=1, keepdims=True)
        back = scaled * r - v * (r * r * r * along / MODEL_WIDTH)
        HG[rows, :] = (DY[rows, :] + back).astype(bf16)
        return 0

    lax.fori_loop(0, ROWS // 128, step, 0)


def mask_bias(seg_column, seg_row, BIAS):
    row = lax.broadcasted_iota(jnp.int32, (ROWS, ROWS), 0)
    column = lax.broadcasted_iota(jnp.int32, (ROWS, ROWS), 1)
    same = seg_column[:, 0:1] == seg_row[0:1, :]
    BIAS[...] = jnp.where((column <= row) & same, 0.0, -1e30)


BLOCKS = 7
PARTS = 2 * BLOCKS
WIDTH = 512
QUARTER = 96
EXPERT_SLOTS = CHUNKS + 14
PART_SLOTS = PARTS + 13


def layer_kernel(
    hg, g4, w0, wg, wu, wd, y1, xin, h1, q, k, v, ob, lse, cos, sin, rt, routes, gain1, gain2,
    segc, segr, wq, wk, wv, wo,
    o_own, o_core, o_x, out, aout, smo, hgrad,
    r_core, r_x, gr, ya, za, zb, d, ca, yb, xb, zc, zd, sa,
    H, W, DG, CR, CO, VA, VB, VS, VZ, VT, VF, FN, SM, SB,
    loc, h_s, h_r, wy_s, wy_r, wz_s, wz_r, stg_sem, y_s, y_r, ld_a, ld_b,
    z1_s, z1_r, ld_z, z2_s, z2_r, ld_f, z3_s, z3_r, fo, x_s, x_r, c1_s, c1_r, c2_s, c2_r,
    z4_s, z4_r, rc_s, rc_r, rx_s, rx_r, rd_s, rd_r, ro,
    ac_s, ac_r, ald, ay_s, ay_r, aldy, ax_s, ax_r, aldx, az1_s, az1_r, aldz, az2_s, az2_r, aldf,
    az3_s, az3_r, afo, axg_s, axg_r, ac1_s, ac1_r, ac2_s, ac2_r, s_s, s_r, sl, att,
):
    z, x, c, y = place()
    mid = (z == 1) | (z == 2)
    end = jnp.logical_not(mid)
    ydev, xdev, cdev = at(z, x, c, 1 - y), at(z, 1 - x, c, y), at(z, x, 1 - c, y)
    zdev = at(z + 1 - 2 * (z % 2), x, c, y)
    mdev = at(3 - z, x, c, y)
    greet((ydev, xdev, cdev, zdev, mdev))
    shards = (wg, wu, wd)
    e0 = 2 * (2 * x + c)
    other = 2 * (2 * (1 - x) + c)
    h = z % 2
    local_copy = pltpu.make_async_copy

    hx = remote(hg, H.at[pl.ds(2 * ROWS, ROWS)], h_s.at[0], h_r.at[0], xdev)
    hc = remote(hg, H.at[pl.ds(ROWS, ROWS)], h_s.at[1], h_r.at[1], cdev)
    hx.start()
    hc.start()

    def parts_of(n):
        return n // (3 * PER), (n // PER) % 3, n % PER

    def y_copy(n):
        j, m, i = parts_of(n)
        src = gr.at[j, m, pl.ds((1 - y) * HALF + i * CHUNK, CHUNK)]
        return remote(src, ya.at[n], y_s.at[n], y_r.at[n], ydev)

    def spot(n, expert):
        j, m, i = parts_of(n)
        return out.at[m, expert + j, pl.ds(i * CHUNK, CHUNK)]

    def load_a(n):
        j, m, i = parts_of(n)
        src = gr.at[j, m, pl.ds(y * HALF + i * CHUNK, CHUNK)]
        return local_copy(src, VA.at[n % 2], ld_a.at[n % 2])

    def load_b(n):
        return local_copy(ya.at[n], VB.at[n % 2], ld_b.at[n % 2])

    def load_z(n):
        return local_copy(za.at[n], VZ.at[n % 2], ld_z.at[n % 2])

    def load_f(n):
        return local_copy(zb.at[n], VF.at[n % 2], ld_f.at[n % 2])

    def z1_copy(n):
        return remote(VS.at[n % 4], za.at[n], z1_s.at[n], z1_r.at[n], zdev)

    def z2_copy(n):
        return remote(VT.at[n % 4], zb.at[n], z2_s.at[n], z2_r.at[n], mdev)

    def z3_copy(n):
        return remote(FN.at[n % 4], spot(n, e0), z3_s.at[n], z3_r.at[n], zdev)

    def z4_copy(n):
        return remote(spot(n, other), spot(n, other), z4_s.at[n], z4_r.at[n], zdev)

    def store_f(n):
        return local_copy(FN.at[n % 4], spot(n, e0), fo.at[n % 4])

    def x_copy(n):
        return remote(spot(n, e0), spot(n, e0), x_s.at[n], x_r.at[n], xdev)

    def c1_copy(n):
        return remote(spot(n, e0), spot(n, e0), c1_s.at[n], c1_r.at[n], cdev)

    def c2_copy(n):
        return remote(spot(n, other), spot(n, other), c2_s.at[n], c2_r.at[n], cdev)

    def crosses(n):
        return (n % 2 == 0) | ((n % 4 == 1) & mid) | ((n % 4 == 3) & end)

    def when(n, cond=None):
        ok = (n >= 0) & (n < CHUNKS)
        return pl.when(ok if cond is None else ok & cond)

    def slot(s):
        @when(s - 13, jnp.logical_not(crosses(s - 13 + 4 * CHUNKS)))
        def _():
            z4_copy(s - 13).wait_recv()
            c2_copy(s - 13).start()

        crossed = crosses(s - 11 + 4 * CHUNKS)

        @when(s - 11, crossed)
        def _():
            x_copy(s - 11).wait_recv()
            c2_copy(s - 11).start()

        @when(s - 11, crossed & ((s + 1) % 2 == 1))
        def _():
            z4_copy(s - 11).start()

        @when(s - 9, mid)
        def _():
            store_f(s - 9).wait()
            z3_copy(s - 9).wait_send()

        @when(s - 9, end)
        def _():
            z3_copy(s - 9).wait_recv()

        @when(s - 9, crosses(s - 9 + 4 * CHUNKS))
        def _():
            x_copy(s - 9).start()

        @when(s - 9)
        def _():
            c1_copy(s - 9).start()

        @when(s - 7, mid)
        def _():
            n = s - 7
            load_f(n).wait()
            z2_copy(n).wait_send()
            FN[n % 4] = (VT[n % 4].astype(f32) + VF[n % 2].astype(f32)).astype(bf16)
            z3_copy(n).start()
            store_f(n).start()

        @when(s - 6, mid)
        def _():
            z2_copy(s - 6).wait_recv()
            load_f(s - 6).start()

        @when(s - 4, mid)
        def _():
            n = s - 4
            load_z(n).wait()
            VT[n % 4] = (VS[n % 4].astype(f32) + VZ[n % 2].astype(f32)).astype(bf16)
            z2_copy(n).start()

        @when(s - 3, mid)
        def _():
            z1_copy(s - 3).wait_recv()
            load_z(s - 3).start()

        @when(s - 5, end)
        def _():
            z1_copy(s - 5).wait_send()

        @when(s - 1)
        def _():
            n = s - 1
            load_a(n).wait()
            load_b(n).wait()
            VS[n % 4] = (VA[n % 2].astype(f32) + VB[n % 2].astype(f32)).astype(bf16)

        @when(s - 1, end)
        def _():
            z1_copy(s - 1).start()

        @when(s)
        def _():
            y_copy(s).wait_recv()
            load_a(s).start()
            load_b(s).start()

    def slots(first, last):
        def step(s, _):
            slot(s)
            return 0

        lax.fori_loop(first, last, step, 0)

    third, second = pl.ds(3 * ROWS, ROWS), pl.ds(2 * ROWS, ROWS)
    first, zeroth = pl.ds(ROWS, ROWS), pl.ds(0, ROWS)

    def experts(G, ACT, STG, RS, OS):
        own = [
            local_copy(hg, H.at[pl.ds(0, ROWS)], loc.at[0]),
            local_copy(g4, G, loc.at[1]),
            local_copy(w0, W.at[0, :, pl.ds((1 - y) * HALF, HALF)], loc.at[2]),
        ]
        for m in range(3):
            own.append(
                local_copy(shards[m].at[e0 + 1], W.at[1, m, pl.ds(y * HALF, HALF)], loc.at[3 + m])
            )
        for m in range(3):
            own.append(
                local_copy(shards[m].at[e0], W.at[0, m, pl.ds(y * HALF, HALF)], loc.at[6 + m])
            )
        wys = []
        for m in range(3):
            wys.append(
                remote(
                    shards[m].at[e0 + 1, pl.ds(h * 384, 384)],
                    W.at[1, m, pl.ds(y * HALF + h * 384, 384)],
                    wy_s.at[m],
                    wy_r.at[m],
                    ydev,
                )
            )
            wys[m].start()
        for copy in own:
            copy.start()

        def gate_of(j, rows):
            lane = lax.broadcasted_iota(jnp.int32, (2 * ROWS, PAD), 1)
            packed = H[rows, MODEL_WIDTH:].astype(f32)
            picked = (lane == e0 + j) | (lane == e0 + j + 8)
            return jnp.sum(jnp.where(picked, packed, 0.0), axis=1, keepdims=True), lane

        def forward(j, begin, base=None):
            rows = pl.ds(begin, 2 * ROWS)
            gate, lane = gate_of(j, rows)

            def step(t, total):
                columns = pl.ds(pl.multiple_of(t * 256, 256), 256)
                ug = jnp.dot(
                    H[rows, :MODEL_WIDTH], W[j, 0, :, columns], preferred_element_type=f32
                )
                uu = jnp.dot(
                    H[rows, :MODEL_WIDTH], W[j, 1, :, columns], preferred_element_type=f32
                )
                dh = jnp.dot(G[rows, :], W[j, 2, :, columns], preferred_element_type=f32)
                sigma = jax.nn.sigmoid(ug)
                silu = ug * sigma
                hid = silu * uu
                ACT[j, 0, rows, columns] = (hid * gate).astype(bf16)
                dhg = dh * gate
                ACT[j, 1, rows, columns] = (
                    dhg * uu * sigma * (1.0 + ug * (1.0 - sigma))
                ).astype(bf16)
                ACT[j, 2, rows, columns] = (dhg * silu).astype(bf16)
                if base is not None:
                    slot(base + t)
                return total + jnp.sum(hid * dh, axis=1, keepdims=True)

            total = lax.fori_loop(0, FF // 256, step, jnp.zeros((2 * ROWS, 1), f32))
            high = total.astype(bf16).astype(f32)
            low = total - high
            here = jnp.where(lane == e0 + j, high, jnp.where(lane == e0 + j + 8, low, 0.0))
            if j == 0:
                DG[rows, :] = here.astype(bf16)
            else:
                DG[rows, :] = (DG[rows, :].astype(f32) + here).astype(bf16)

        def back_rows(rows, ns):
            o = nt_dot(ACT[0, 0, rows, :], W[0, 2, ns, :])
            o = o + nt_dot(ACT[1, 0, rows, :], W[1, 2, ns, :])
            e = nt_dot(ACT[0, 1, rows, :], W[0, 0, ns, :])
            e = e + nt_dot(ACT[0, 2, rows, :], W[0, 1, ns, :])
            e = e + nt_dot(ACT[1, 1, rows, :], W[1, 0, ns, :])
            e = e + nt_dot(ACT[1, 2, rows, :], W[1, 1, ns, :])
            return o, e

        def weight_tile(j, m, left, half, i, place_in):
            begin = half * HALF + i * 384
            lhs = left[:, pl.ds(pl.multiple_of(begin, 128), 384)]
            STG[place_in] = tn_dot(lhs, ACT[j, (m + 1) % 3]).astype(bf16)
            copy = local_copy(
                STG.at[place_in], gr.at[j, m, pl.ds(begin, 384)], stg_sem.at[place_in]
            )
            copy.start()
            return copy

        def weight_grads(j, base=None):
            done = 0
            for left, m0, steps in ((H, 0, 4), (G, 2, 2)):

                def step(n, _, left=left, m0=m0, done=done):
                    m, i = m0 + n // 2, n % 2
                    away = weight_tile(j, m, left, 1 - y, i, 0)
                    here = weight_tile(j, m, left, y, i, 1)
                    away.wait()
                    begin = (j * 3 + m) * PER + i * (384 // CHUNK)
                    for p in range(384 // CHUNK):
                        y_copy(begin + p).start()
                    if base is not None:
                        slot(base + done + n)
                    here.wait()
                    return 0

                lax.fori_loop(0, steps, step, 0)
                done += steps

        def rc_copy(t, which):
            ns = pl.ds(pl.multiple_of(t * 512, 512), 512)
            src, dst = ((RS, CR), (OS, CO))[which]
            return remote(
                src.at[t % 2], dst.at[:, ns], rc_s.at[which, t], rc_r.at[which, t], cdev
            )

        def rb_copy(t, which):
            ns = pl.ds(pl.multiple_of(t * 512, 512), 512)
            src, dst = ((RS, r_core), (OS, o_core))[which]
            return remote(
                src.at[t % 2], dst.at[:, ns], rd_s.at[1 + which * 3 + t],
                rd_r.at[1 + which * 3 + t], cdev,
            )

        def ro_copy(t):
            ns = pl.ds(pl.multiple_of(t * 512, 512), 512)
            return local_copy(OS.at[t % 2], o_own.at[:, ns], ro.at[t])

        own[1].wait()
        own[2].wait()
        own[0].wait()
        for m in range(3):
            own[6 + m].wait()
        hc.wait_recv()
        forward(0, 0)
        hx.wait_recv()
        hd = remote(H.at[second], H.at[third], h_s.at[2], h_r.at[2], cdev)
        hd.start()
        wzs = []
        for m in range(3):
            wys[m].wait_recv()
            rows = pl.ds((1 - y) * HALF + h * 384, 384)
            wzs.append(remote(W.at[1, m, rows], W.at[1, m, rows], wz_s.at[m], wz_r.at[m], zdev))
            wzs[m].start()
        hd.wait_recv()
        forward(0, 2 * ROWS)
        weight_grads(0)
        for m in range(3):
            wzs[m].wait_recv()
            own[3 + m].wait()
        forward(1, 0, 0)
        forward(1, 2 * ROWS, 3)

        def third_step(t, _):
            ns = pl.ds(pl.multiple_of(t * 512, 512), 512)

            @pl.when(t == 2)
            def _():
                rc_copy(0, 0).wait_send()
                rc_copy(0, 1).wait_send()

            o, e = back_rows(third, ns)
            RS[t % 2] = e.astype(bf16)
            OS[t % 2] = o.astype(bf16)
            rc_copy(t, 0).start()
            rc_copy(t, 1).start()
            slot(6 + t)
            return 0

        lax.fori_loop(0, 3, third_step, 0)
        dg_copy = remote(
            DG.at[third], CR.at[:, pl.ds(MODEL_WIDTH, PAD)], rd_s.at[0], rd_r.at[0], cdev
        )
        dg_copy.start()

        def second_step(t, _):
            ns = pl.ds(pl.multiple_of(t * 512, 512), 512)
            o, e = back_rows(second, ns)
            rc_copy(t, 0).wait_recv()
            rc_copy(t, 1).wait_recv()
            CR[:, ns] = (CR[:, ns].astype(f32) + e).astype(bf16)
            CO[:, ns] = (CO[:, ns].astype(f32) + o).astype(bf16)
            slot(9 + t)
            return 0

        lax.fori_loop(0, 3, second_step, 0)
        dg_copy.wait_recv()
        CR[:, MODEL_WIDTH:] = CR[:, MODEL_WIDTH:] + DG[second, :]
        rx.start()
        weight_grads(1, 12)
        for which in range(2):
            for t in (1, 2):
                rc_copy(t, which).wait_send()
        dg_copy.wait_send()
        tail_b.start()

        def first_step(t, _):
            ns = pl.ds(pl.multiple_of(t * 512, 512), 512)

            @pl.when(t == 2)
            def _():
                rb_copy(0, 0).wait_send()
                rb_copy(0, 1).wait_send()

            o, e = back_rows(first, ns)
            RS[t % 2] = e.astype(bf16)
            OS[t % 2] = o.astype(bf16)
            rb_copy(t, 0).start()
            rb_copy(t, 1).start()
            slot(18 + t)
            return 0

        lax.fori_loop(0, 3, first_step, 0)
        for t in (1, 2):
            rb_copy(t, 0).wait_send()
            rb_copy(t, 1).wait_send()

        def zeroth_step(t, _):
            ns = pl.ds(pl.multiple_of(t * 512, 512), 512)
            o, e = back_rows(zeroth, ns)

            @pl.when(t == 2)
            def _():
                ro_copy(0).wait()

            H[first, ns] = e.astype(bf16)
            OS[t % 2] = o.astype(bf16)
            ro_copy(t).start()
            slot(21 + t)
            return 0

        lax.fori_loop(0, 3, zeroth_step, 0)
        H[first, MODEL_WIDTH:] = DG[zeroth, :]
        for t in range(3):
            rb_copy(t, 0).wait_recv()
            rb_copy(t, 1).wait_recv()
        for t in (1, 2):
            ro_copy(t).wait()
        for m in range(3):
            wys[m].wait_send()
            wzs[m].wait_send()
        hx.wait_send()
        hc.wait_send()
        hd.wait_send()
        rx.wait_send()

    rx = remote(CR, r_x, rx_s.at[0], rx_r.at[0], xdev)
    ox = remote(CO, o_x, rx_s.at[1], rx_r.at[1], xdev)
    tail_b = remote(
        DG.at[first], r_core.at[:, pl.ds(MODEL_WIDTH, PAD)], rd_s.at[7], rd_r.at[7], cdev
    )
    vm = pltpu.VMEM
    pl.run_scoped(
        experts,
        vm((4 * ROWS, MODEL_WIDTH), bf16),
        vm((2, 3, 4 * ROWS, FF), bf16),
        vm((2, 384, FF), bf16),
        vm((2, ROWS, 512), bf16),
        vm((2, ROWS, 512), bf16),
    )
    ox.start()
    tail_b.wait()

    def attention(
        Y1, DY, GB, XB, H1, OB, QB, KB, VV, DA, DOB, DQKV, BIAS, LSE, COS, SIN, RT, RO, G1, G2,
        SC, SR, DL, GS, DK, DV, HG, STG,
        AA, AB, PP, VY, QQ, VX, AS, AZ, AT, AF, AN,
    ):
        pairs = [
            (y1, Y1), (g4.at[pl.ds(0, ROWS)], GB), (xin, XB), (h1, H1), (ob, OB), (q, QB), (k, KB),
            (v, VV), (lse, LSE), (cos, COS), (sin, SIN), (rt, RT), (routes, RO), (gain1, G1),
            (gain2, G2), (segc, SC), (segr, SR), (r_core, H.at[second]),
        ]
        for half in range(2):
            rows = pl.ds(half * HALF, HALF)
            for n, w in ((0, wq), (1, wo)):
                for part in range(2):
                    columns = pl.ds(part * HALF, HALF)
                    pairs.append((w.at[half, :, columns], W.at[n, part, rows]))
            pairs.append((wk.at[half], W.at[0, 2, rows, pl.ds(0, 256)]))
            pairs.append((wv.at[half], W.at[0, 2, rows, pl.ds(256, 256)]))
        loads = [local_copy(p[0], p[1], att.at[n]) for n, p in enumerate(pairs)]
        for copy in loads:
            copy.start()
        slots(24, 26)
        for copy in loads:
            copy.wait()
        mask_bias(SC, SR, BIAS)
        slots(26, 28)
        rx.wait_recv()
        last = local_copy(r_x, H.at[third], att.at[len(pairs)])
        last.start()
        last.wait()

        def rows_of(n):
            q_, i = n // 2, n % 2
            return q_, i * 384

        def ac_copy(n):
            b, begin = rows_of(n)
            src = d.at[b, :, pl.ds(begin + (1 - c) * 192, 192)]
            return remote(src, ca.at[n], ac_s.at[n], ac_r.at[n], cdev)

        def aload_a(n):
            b, begin = rows_of(n)
            return local_copy(d.at[b, :, pl.ds(begin + c * 192, 192)], AA.at[n % 2], ald.at[0, n % 2])

        def aload_b(n):
            return local_copy(ca.at[n], AB.at[n % 2], ald.at[1, n % 2])

        def ay_copy(n):
            return remote(PP.at[n % 4, 1 - y], yb.at[n], ay_s.at[n], ay_r.at[n], ydev)

        def aload_y(n):
            return local_copy(yb.at[n], VY.at[n % 2], aldy.at[n % 2])

        def ax_copy(n):
            src = QQ.at[n % 4, pl.ds((1 - x) * QUARTER, QUARTER)]
            return remote(src, xb.at[n], ax_s.at[n], ax_r.at[n], xdev)

        def aload_x(n):
            return local_copy(xb.at[n], VX.at[n % 2], aldx.at[n % 2])

        def az1_copy(n):
            return remote(AS.at[n % 8], zc.at[n], az1_s.at[n], az1_r.at[n], zdev)

        def aload_z(n):
            return local_copy(zc.at[n], AZ.at[n % 2], aldz.at[n % 2])

        def az2_copy(n):
            return remote(AT.at[n % 4], zd.at[n], az2_s.at[n], az2_r.at[n], mdev)

        def aload_f(n):
            return local_copy(zd.at[n], AF.at[n % 2], aldf.at[n % 2])

        def aspot(n, xx, cc):
            b, begin = rows_of(n)
            columns = pl.ds(pl.multiple_of(b * WIDTH, WIDTH), WIDTH)
            return aout.at[pl.ds(begin + cc * 192 + xx * QUARTER, QUARTER), columns]

        def az3_copy(n):
            return remote(AN.at[n % 4], aspot(n, x, c), az3_s.at[n], az3_r.at[n], zdev)

        def astore(n):
            return local_copy(AN.at[n % 4], aspot(n, x, c), afo.at[n % 4])

        def axg_copy(n):
            return remote(aspot(n, x, c), aspot(n, x, c), axg_s.at[n], axg_r.at[n], xdev)

        def ac1_copy(n):
            return remote(aspot(n, x, c), aspot(n, x, c), ac1_s.at[n], ac1_r.at[n], cdev)

        def ac2_copy(n):
            return remote(aspot(n, 1 - x, c), aspot(n, 1 - x, c), ac2_s.at[n], ac2_r.at[n], cdev)

        def awhen(n, cond=None):
            ok = (n >= 0) & (n < PARTS)
            return pl.when(ok if cond is None else ok & cond)

        def aslot(s):
            @awhen(s - 13)
            def _():
                axg_copy(s - 13).wait_recv()
                ac2_copy(s - 13).start()

            @awhen(s - 12, mid)
            def _():
                astore(s - 12).wait()
                az3_copy(s - 12).wait_send()

            @awhen(s - 12, end)
            def _():
                az3_copy(s - 12).wait_recv()
                az1_copy(s - 12).wait_send()

            @awhen(s - 12)
            def _():
                axg_copy(s - 12).start()
                ac1_copy(s - 12).start()

            @awhen(s - 10, mid)
            def _():
                n = s - 10
                aload_f(n).wait()
                az2_copy(n).wait_send()
                AN[n % 4] = (AT[n % 4].astype(f32) + AF[n % 2].astype(f32)).astype(bf16)
                az3_copy(n).start()
                astore(n).start()

            @awhen(s - 9, mid)
            def _():
                az2_copy(s - 9).wait_recv()
                aload_f(s - 9).start()

            @awhen(s - 8, mid)
            def _():
                n = s - 8
                aload_z(n).wait()
                AT[n % 4] = (AS[n % 8].astype(f32) + AZ[n % 2].astype(f32)).astype(bf16)
                az2_copy(n).start()

            @awhen(s - 7, mid)
            def _():
                az1_copy(s - 7).wait_recv()
                aload_z(s - 7).start()

            @awhen(s - 6)
            def _():
                n = s - 6
                aload_x(n).wait()
                ax_copy(n).wait_send()
                mine = pl.ds(pl.multiple_of(x * QUARTER, 16), QUARTER)
                AS[n % 8] = (QQ[n % 4, mine, :].astype(f32) + VX[n % 2].astype(f32)).astype(bf16)

            @awhen(s - 6, end)
            def _():
                az1_copy(s - 6).start()

            @awhen(s - 5)
            def _():
                ax_copy(s - 5).wait_recv()
                aload_x(s - 5).start()

            @awhen(s - 4)
            def _():
                n = s - 4
                aload_y(n).wait()
                ay_copy(n).wait_send()
                QQ[n % 4] = (PP[n % 4, y].astype(f32) + VY[n % 2].astype(f32)).astype(bf16)
                ax_copy(n).start()

            @awhen(s - 3)
            def _():
                ay_copy(s - 3).wait_recv()
                aload_y(s - 3).start()

            @awhen(s - 1)
            def _():
                n = s - 1
                aload_a(n).wait()
                aload_b(n).wait()
                PP[n % 4] = (AA[n % 2].astype(f32) + AB[n % 2].astype(f32)).astype(bf16)
                ay_copy(n).start()

            @awhen(s)
            def _():
                ac_copy(s).wait_recv()
                aload_a(s).start()
                aload_b(s).start()

        def emit(b, left, right):
            copies = []
            for half in range(2):
                STG[half] = tn_dot(left[:, pl.ds(half * HALF, HALF)], right).astype(bf16)
                copies.append(local_copy(STG.at[half], d.at[b, half], stg_sem.at[half]))
                copies[half].start()
            for copy in copies:
                copy.wait()
            ac_copy(2 * b).start()
            ac_copy(2 * b + 1).start()

        def returned(rows):
            begin = rows.start
            one = H[pl.ds(pl.multiple_of(begin + ROWS, 128), 128), :].astype(f32)
            two = H[pl.ds(pl.multiple_of(begin + 2 * ROWS, 128), 128), :].astype(f32)
            three = H[pl.ds(pl.multiple_of(begin + 3 * ROWS, 128), 128), :].astype(f32)
            return one + two + three

        middle_backward(
            returned, lambda rows: H[rows, :MODEL_WIDTH], RT, RO, Y1, GB, G2, DL, DY, DA, GS
        )
        for half in range(2):
            columns = pl.ds(half * HALF, HALF)
            SM[half, 1:2, :] = GS[:, columns].astype(bf16)
            router = tn_dot(DL[...], H[zeroth, columns])
            SM[half, 2:10, :] = router[0:8].astype(bf16)
            SM[half, 10:16, :] = jnp.zeros((6, HALF), bf16)

        def out_block(b, _):
            emit(b, OB, DA[:, pl.ds(pl.multiple_of(b * WIDTH, WIDTH), WIDTH)])
            slot(28 + b)
            return 0

        lax.fori_loop(0, 3, out_block, 0)

        def dob_tile(t, _):
            ns = pl.ds(pl.multiple_of(t * 512, 512), 512)
            tile = nt_dot(DA[:, :HALF], W[1, 0, ns, :]) + nt_dot(DA[:, HALF:], W[1, 1, ns, :])
            DOB[:, ns] = tile.astype(bf16)
            slot(31 + t)
            return 0

        lax.fori_loop(0, 3, dob_tile, 0)
        state = [34, 0]

        def tick():
            first_slot, first_part = state

            def step(n, _):
                slot(first_slot + n)
                return 0

            lax.fori_loop(0, 2, step, 0)
            if first_part < 6:
                lax.fori_loop(0, 2, lambda n, _: (aslot(first_part + n), 0)[1], 0)
            state[0] += 2
            state[1] = min(state[1] + 2, 6)

        heads_backward(QB, KB, VV, DOB, BIAS, LSE, COS, SIN, DQKV, DK, DV, tick)
        done, parts_done = state

        def qkv_block(b, _):
            emit(3 + b, H1, DQKV[:, pl.ds(pl.multiple_of(b * WIDTH, WIDTH), WIDTH)])
            slot(done + b)
            return 0

        lax.fori_loop(0, 4, qkv_block, 0)
        done += 4

        def dh1_tile(t, _):
            ns = pl.ds(pl.multiple_of(t * 512, 512), 512)
            tile = nt_dot(DQKV[:, :HALF], W[0, 0, ns, :])
            tile = tile + nt_dot(DQKV[:, HALF:MODEL_WIDTH], W[0, 1, ns, :])
            Y1[:, ns] = tile + nt_dot(DQKV[:, MODEL_WIDTH:], W[0, 2, ns, :512])
            slot(done + t)
            aslot(parts_done + t)
            return 0

        lax.fori_loop(0, 3, dh1_tile, 0)
        done, parts_done = done + 3, parts_done + 3
        first_backward(Y1, XB, DY, G1, HG, GS)
        for half in range(2):
            SM[half, 0:1, :] = GS[:, pl.ds(half * HALF, HALF)].astype(bf16)
        result = local_copy(HG, hgrad, att.at[len(pairs) + 1])
        result.start()

        for i, device in enumerate((cdev, xdev, ydev, zdev, mdev)):
            hop = remote(SM, sa.at[i], s_s.at[i], s_r.at[i], device)
            hop.start()
            slot(done)
            aslot(parts_done)
            done, parts_done = done + 1, parts_done + 1
            hop.wait()
            load = local_copy(sa.at[i], SB, sl.at[0])
            load.start()
            load.wait()
            SM[...] = (SM[...].astype(f32) + SB[...].astype(f32)).astype(bf16)
        small = local_copy(SM, smo, sl.at[1])
        small.start()

        last_slot = max(EXPERT_SLOTS - done, PART_SLOTS - parts_done)

        def drain(n, _):
            slot(done + n)
            aslot(parts_done + n)
            return 0

        lax.fori_loop(0, last_slot, drain, 0)
        small.wait()
        result.wait()

        def finish_part(n, _):
            ac_copy(n).wait_send()
            axg_copy(n).wait_send()
            ac1_copy(n).wait()
            ac2_copy(n).wait()
            return 0

        lax.fori_loop(0, PARTS, finish_part, 0)

    part = lambda *shape: vm(shape, bf16)
    pl.run_scoped(
        attention,
        vm((ROWS, MODEL_WIDTH), f32), vm((ROWS, MODEL_WIDTH), f32),
        part(ROWS, MODEL_WIDTH), part(ROWS, MODEL_WIDTH), part(ROWS, MODEL_WIDTH),
        part(ROWS, MODEL_WIDTH), part(ROWS, MODEL_WIDTH), part(ROWS, 256), part(ROWS, 256),
        part(ROWS, MODEL_WIDTH), part(ROWS, MODEL_WIDTH), part(ROWS, 2048),
        vm((ROWS, ROWS), f32), vm((ROWS, PAD), f32), vm((ROWS, PAD), f32), vm((ROWS, PAD), f32),
        part(PAD, MODEL_WIDTH), vm((ROWS, PAD), jnp.int32), vm((1, MODEL_WIDTH), f32),
        vm((1, MODEL_WIDTH), f32), vm((ROWS, PAD), jnp.int32), vm((8, ROWS), jnp.int32),
        part(ROWS, PAD), vm((1, MODEL_WIDTH), f32), vm((2, ROWS, PAD), f32),
        vm((2, ROWS, PAD), f32), part(ROWS, MODEL_WIDTH), part(2, HALF, WIDTH),
        part(2, 2, 192, WIDTH), part(2, 2, 192, WIDTH), part(4, 2, 192, WIDTH),
        part(2, 192, WIDTH), part(4, 192, WIDTH), part(2, QUARTER, WIDTH), part(8, QUARTER, WIDTH),
        part(2, QUARTER, WIDTH), part(4, QUARTER, WIDTH), part(2, QUARTER, WIDTH),
        part(4, QUARTER, WIDTH),
    )
    ox.wait()

    def finish(n, _):
        @pl.when(crosses(n))
        def _():
            x_copy(n).wait_send()

        @pl.when(crosses(n) & (n % 2 == 1))
        def _():
            z4_copy(n).wait_send()

        c1_copy(n).wait()
        c2_copy(n).wait()
        y_copy(n).wait_send()
        return 0

    lax.fori_loop(0, CHUNKS, finish, 0)


def layer_call(*arrays):
    anyspace = pl.BlockSpec(memory_space=pl.ANY)
    dma = pltpu.SemaphoreType.DMA
    vmem = lambda *s: pltpu.VMEM(s, bf16)
    n = PARTS
    shapes = [(ROWS, MODEL_WIDTH)] * 3
    shapes += [(3, 8, HALF, FF), (HALF, BLOCKS * WIDTH), (2, 16, HALF), (ROWS, MODEL_WIDTH)]
    shapes += [(ROWS, WIDE)] * 2 + [(2, 3, MODEL_WIDTH, FF)] + [(CHUNKS, CHUNK, FF)] * 3
    shapes += [(BLOCKS, 2, HALF, WIDTH), (n, 2, 192, WIDTH), (n, 192, WIDTH)]
    shapes += [(n, QUARTER, WIDTH)] * 3 + [(5, 2, 16, HALF)]
    many, few = dma((CHUNKS,)), dma((n,))
    scratch = [
        vmem(4 * ROWS, WIDE), vmem(2, 3, MODEL_WIDTH, FF), vmem(4 * ROWS, PAD), vmem(ROWS, WIDE),
        vmem(ROWS, MODEL_WIDTH), vmem(2, CHUNK, FF), vmem(2, CHUNK, FF), vmem(4, CHUNK, FF),
        vmem(2, CHUNK, FF), vmem(4, CHUNK, FF), vmem(2, CHUNK, FF), vmem(4, CHUNK, FF),
        vmem(2, 16, HALF), vmem(2, 16, HALF),
        dma((9,)), dma((3,)), dma((3,)), dma((3,)), dma((3,)), dma((3,)), dma((3,)),
        dma((2,)), many, many, dma((2,)), dma((2,)),
        many, many, dma((2,)), many, many, dma((2,)),
        many, many, dma((4,)), many, many, many, many, many, many, many, many,
        dma((2, 3)), dma((2, 3)), dma((2,)), dma((2,)), dma((8,)), dma((8,)), dma((3,)),
        few, few, dma((2, 2)), few, few, dma((2,)), few, few, dma((2,)), few, few, dma((2,)),
        few, few, dma((2,)), few, few, dma((4,)), few, few, few, few, few, few,
        dma((5,)), dma((5,)), dma((2,)), dma((32,)),
    ]
    return pl.pallas_call(
        layer_kernel,
        out_shape=[jax.ShapeDtypeStruct(s, bf16) for s in shapes],
        in_specs=[anyspace] * len(arrays),
        out_specs=[anyspace] * len(shapes),
        scratch_shapes=scratch,
        compiler_params=pltpu.CompilerParams(
            collective_id=2, has_side_effects=True, vmem_limit_bytes=66 * 1000 * 1000
        ),
        name="layer",
    )(*arrays)[:7]


def attention_forward(hidden, segments, gain_one, w_q, w_k, w_v, w_o, gain_two):
    sequence_length = hidden.shape[0]
    group = QUERY_HEADS // KEY_VALUE_HEADS
    head_scale = HEAD_SIZE ** (-0.5)
    cosine, sine = tables(sequence_length, HEAD_SIZE)
    normed_f, scale_one = normalize(hidden, gain_one)
    h1 = normed_f.astype(bf16)
    qr = jnp.dot(h1, w_q, preferred_element_type=f32)
    kr = jnp.dot(h1, w_k, preferred_element_type=f32)
    values = jnp.dot(h1, w_v, preferred_element_type=f32).astype(bf16)
    values = values.reshape(sequence_length, KEY_VALUE_HEADS, HEAD_SIZE)
    qr = qr.reshape(sequence_length, QUERY_HEADS, HEAD_SIZE)
    kr = kr.reshape(sequence_length, KEY_VALUE_HEADS, HEAD_SIZE)
    queries = apply_rotary(qr, cosine, sine).astype(bf16)
    queries = queries.reshape(sequence_length, KEY_VALUE_HEADS, group, HEAD_SIZE)
    keys = apply_rotary(kr, cosine, sine).astype(bf16)
    position = jnp.arange(sequence_length)
    allowed = (position[None, :] <= position[:, None]) & (segments[:, None] == segments[None, :])
    scores = jnp.einsum("qkgd,skd->kgqs", queries, keys, preferred_element_type=f32) * head_scale
    scores = jnp.where(allowed, scores, -1e30)
    top_score = jnp.max(scores, axis=-1, keepdims=True)
    exp_scores = jnp.exp(scores - top_score)
    sum_exp = jnp.sum(exp_scores, axis=-1, keepdims=True)
    log_total = top_score + jnp.log(sum_exp)
    probs = (exp_scores / sum_exp).astype(bf16)
    mixed = jnp.einsum("kgqs,skd->qkgd", probs, values, preferred_element_type=f32)
    mixed = mixed.reshape(sequence_length, QUERY_HEADS * HEAD_SIZE).astype(bf16)
    middle = hidden + jnp.dot(mixed, w_o, preferred_element_type=f32)
    normed_two_f, scale_two = normalize(middle, gain_two)
    h2 = normed_two_f.astype(bf16)
    kept = (scale_one, h1, queries, keys, values, allowed, log_total, mixed, middle, scale_two)
    return h2, kept


def router_forward(h2, w_router, routes):
    logits = jnp.dot(h2, w_router, preferred_element_type=f32)
    probs = softmax_rows(logits)
    experts = w_router.shape[1]
    chosen = jnp.any(
        routes[:, :, None] == jnp.arange(experts, dtype=jnp.int32)[None, None, :], axis=1
    )
    picked = jnp.where(chosen, probs, 0.0)
    total = jnp.sum(picked, axis=-1, keepdims=True)
    return probs, chosen, total, picked / total


def router_backward(h2, w_router, probs, chosen, total, gates, gate_grads):
    gate_grads = jnp.where(chosen, gate_grads, 0.0)
    weighted = jnp.sum(gate_grads * gates, axis=-1, keepdims=True)
    prob_grad = jnp.where(chosen, (gate_grads - weighted) / total, 0.0)
    logit_grad = probs * (prob_grad - jnp.sum(prob_grad * probs, axis=-1, keepdims=True))
    logit_grad = logit_grad.astype(bf16)
    return contract(h2, logit_grad, 0, 0), contract(logit_grad, w_router, 1, 1)


def attention_backward(hidden, kept, gain_one, w_q, w_k, w_v, w_o, gain_two, upstream, dh2):
    scale_one, h1, queries, keys, values, allowed, log_total, mixed, middle, scale_two = kept
    sequence_length = hidden.shape[0]
    group = QUERY_HEADS // KEY_VALUE_HEADS
    head_scale = HEAD_SIZE ** (-0.5)
    cosine, sine = tables(sequence_length, HEAD_SIZE)
    middle_norm_grad, gain_two_grad = norm_back(middle, scale_two, gain_two, dh2)
    middle_grad = upstream + middle_norm_grad
    branch_grad = middle_grad.astype(bf16)
    out_proj_sum = contract(mixed, branch_grad, 0, 0)
    mixed_grad = contract(branch_grad, w_o, 1, 1).astype(bf16)
    mixed_grad = mixed_grad.reshape(sequence_length, KEY_VALUE_HEADS, group, HEAD_SIZE)
    probs = jnp.exp(
        jnp.einsum("qkgd,skd->kgqs", queries, keys, preferred_element_type=f32) * head_scale
        - log_total
    )
    probs = jnp.where(allowed, probs, 0.0)
    prob_back = jnp.einsum("qkgd,skd->kgqs", mixed_grad, values, preferred_element_type=f32)
    score_grad = probs * (prob_back - jnp.sum(prob_back * probs, axis=-1, keepdims=True))
    score_grad = score_grad.astype(bf16)
    dq = jnp.einsum("kgqs,skd->qkgd", score_grad, keys, preferred_element_type=f32) * head_scale
    dq = dq.reshape(sequence_length, QUERY_HEADS, HEAD_SIZE)
    dq = apply_rotary(dq, cosine, -sine).astype(bf16)
    dq = dq.reshape(sequence_length, QUERY_HEADS * HEAD_SIZE)
    dk = jnp.einsum("kgqs,qkgd->skd", score_grad, queries, preferred_element_type=f32) * head_scale
    dk = apply_rotary(dk, cosine, -sine).astype(bf16)
    dk = dk.reshape(sequence_length, KEY_VALUE_HEADS * HEAD_SIZE)
    dv = jnp.einsum("kgqs,qkgd->skd", probs.astype(bf16), mixed_grad, preferred_element_type=f32)
    dv = dv.astype(bf16).reshape(sequence_length, KEY_VALUE_HEADS * HEAD_SIZE)
    query_sum = contract(h1, dq, 0, 0)
    key_sum = contract(h1, dk, 0, 0)
    value_sum = contract(h1, dv, 0, 0)
    dh1 = contract(dq, w_q, 1, 1) + contract(dk, w_k, 1, 1) + contract(dv, w_v, 1, 1)
    hidden_norm_grad, gain_one_grad = norm_back(hidden, scale_one, gain_one, dh1)
    hidden_grad = (middle_grad + hidden_norm_grad).astype(bf16)
    return hidden_grad, (
        gain_one_grad,
        query_sum,
        key_sum,
        value_sum,
        out_proj_sum,
        gain_two_grad,
    )


def reduce_over_all(value, dimension):
    value = lax.psum_scatter(
        value.astype(bf16), "shard", scatter_dimension=dimension, tiled=True
    ).astype(f32)
    return lax.psum(value.astype(bf16), "rep").astype(f32)


def local(
    hidden_in,
    segment_ids,
    routes,
    out_grad,
    norm1_gain,
    w_query,
    key_weight,
    value_weight,
    w_out,
    norm2_gain,
    w_router,
    w_gate,
    w_up,
    w_down,
):
    small = jnp.concatenate(
        [norm1_gain[None], norm2_gain[None], w_router.T, jnp.zeros((6, HALF), bf16)], axis=0
    )
    w_q, w_k, w_v, w_o, small, g4, w0 = gather_call(
        w_query, key_weight, value_weight, w_out, small, out_grad, w_gate, w_up, w_down
    )
    whole = lambda w: w.reshape(MODEL_WIDTH, w.shape[-1])
    weights = (w_q, w_k, w_v, w_o)
    w_q, w_k, w_v, w_o = whole(w_q), whole(w_k), whole(w_v), whole(w_o)
    small = small.transpose(1, 0, 2).reshape(16, MODEL_WIDTH)
    gain_one, gain_two = small[0].astype(f32), small[1].astype(f32)
    router = small[2:10].T
    hidden = hidden_in.astype(f32)
    h2, kept = attention_forward(
        hidden, segment_ids[0], gain_one, w_q, w_k, w_v, w_o, gain_two
    )
    probs, chosen, total, gates = router_forward(h2, router, routes)
    high = gates.astype(bf16)
    low = (gates - high.astype(f32)).astype(bf16)
    hg = jnp.concatenate([h2, high, low, jnp.zeros((ROWS, PAD - 16), bf16)], axis=1)
    scale_one, h1, queries, keys, values, allowed, log_total, mixed, middle, scale_two = kept
    cosine, sine = tables(ROWS, HEAD_SIZE)
    lanes = lambda v: jnp.pad(v, ((0, 0), (0, PAD - v.shape[1])))
    segments = segment_ids[0]
    o_own, o_core, o_x, grads, d, sm, hidden_grad = layer_call(
        hg,
        g4.reshape(4 * ROWS, MODEL_WIDTH),
        w0,
        w_gate,
        w_up,
        w_down,
        middle,
        hidden_in,
        h1,
        queries.reshape(ROWS, MODEL_WIDTH),
        keys.reshape(ROWS, 256),
        values.reshape(ROWS, 256),
        mixed,
        lanes(log_total.reshape(QUERY_HEADS, ROWS).T),
        cosine[:, 0, :],
        turn_table(sine),
        jnp.pad(small[2:10], ((0, PAD - 8), (0, 0))),
        lanes(routes),
        gain_one[None],
        gain_two[None],
        jnp.broadcast_to(segments[:, None], (ROWS, PAD)),
        jnp.broadcast_to(segments[None, :], (8, ROWS)),
        *weights,
    )
    add = lambda a, b, c: a.astype(f32) + b.astype(f32) + c.astype(f32)
    hidden_out = (middle + add(o_own, o_core, o_x)).astype(bf16)
    sm = lax.dynamic_index_in_dim(sm, lax.axis_index("shard"), 0, keepdims=False).astype(f32)
    d = d.astype(f32)
    attn = (sm[0], d[:, 1536:3072], d[:, 3072:3328], d[:, 3328:], d[:, :1536], sm[1], sm[2:10].T)
    grads = [grads[m].astype(f32) for m in range(3)]
    return (hidden_out, hidden_grad, *attn, *grads)


def local_any(
    hidden_in,
    segment_ids,
    routes,
    out_grad,
    norm1_gain,
    w_query,
    key_weight,
    value_weight,
    w_out,
    norm2_gain,
    w_router,
    w_gate,
    w_up,
    w_down,
):
    wide = lambda w, axis: lax.all_gather(w, "shard", axis=axis, tiled=True)
    gain_one, gain_two = wide(norm1_gain, 0).astype(f32), wide(norm2_gain, 0).astype(f32)
    w_q, w_k, w_v, w_o = (wide(w, 0) for w in (w_query, key_weight, value_weight, w_out))
    router = wide(w_router, 0)
    hidden = hidden_in.astype(f32)
    h2, kept = attention_forward(
        hidden, segment_ids[0], gain_one, w_q, w_k, w_v, w_o, gain_two
    )
    probs, chosen, total, gates = router_forward(h2, router, routes)
    full = [wide(w, 1) for w in (w_gate, w_up, w_down)]

    def expert(carry, inputs):
        mixed, dh2 = carry
        gate_weight, up_weight, down_weight, gate = inputs
        gate = gate[:, None]
        ug = jnp.dot(h2, gate_weight, preferred_element_type=f32)
        uu = jnp.dot(h2, up_weight, preferred_element_type=f32)
        dh = jnp.dot(out_grad, down_weight, preferred_element_type=f32)
        sigma = jax.nn.sigmoid(ug)
        silu = ug * sigma
        hid = silu * uu
        gate_grad = jnp.sum(hid * dh, axis=1)
        hidden_rows = (hid * gate).astype(bf16)
        dug = (dh * gate * uu * sigma * (1.0 + ug * (1.0 - sigma))).astype(bf16)
        duu = (dh * gate * silu).astype(bf16)
        mixed = mixed + contract(hidden_rows, down_weight, 1, 1)
        dh2 = dh2 + contract(dug, gate_weight, 1, 1) + contract(duu, up_weight, 1, 1)
        sums = (contract(h2, dug, 0, 0), contract(h2, duu, 0, 0))
        sums = sums + (contract(out_grad, hidden_rows, 0, 0),)
        return (mixed, dh2), (gate_grad, *(s.astype(bf16) for s in sums))

    zeros = jnp.zeros(hidden.shape, f32)
    (mixed, dh2), (gate_grads, *sums) = lax.scan(expert, (zeros, zeros), (*full, gates.T))
    hidden_out = (kept[8] + mixed).astype(bf16)
    router_sum, routed = router_backward(h2, router, probs, chosen, total, gates, gate_grads.T)
    hidden_grad, attn = attention_backward(
        hidden, kept, gain_one, w_q, w_k, w_v, w_o, gain_two, out_grad.astype(f32), routed + dh2
    )
    attn = [reduce_over_all(value, 0) for value in attn + (router_sum,)]
    grads = [reduce_over_all(value, 1) for value in sums]
    return (hidden_out, hidden_grad, *attn, *grads)


def solution(mesh):
    rows, vector, matrix = P(("rep", "shard"), None), P("shard"), P("shard", None)
    stack = P(None, "shard", None)
    in_specs = (
        rows, rows, rows, rows, vector, matrix, matrix, matrix, matrix, vector, matrix,
        stack, stack, stack,
    )
    out_specs = (
        rows, rows, vector, matrix, matrix, matrix, matrix, vector, matrix, stack, stack, stack,
    )
    fits = dict(mesh.shape) == {"rep": 16, "shard": 2}
    body = local if fits else local_any
    return jax.shard_map(body, mesh=mesh, in_specs=in_specs, out_specs=out_specs, check_vma=False)
```

time: 1090 us -> 639 us (0.59)
  waiting for transfers between devices: 152 us -> 0 us
  Pallas kernels: 672 us -> 532 us
  blocking collectives: 66.6 us -> 0 us
  matrix products: 74.9 us -> 21 us
  other arithmetic: 77.1 us -> 45.5 us
  between operations: 15.9 us -> 1.32 us
  local copies, waits for them, and re-layouts: 22.4 us -> 36.5 us
    pallas_call x1, Pallas kernels: 327 us -> 88.2 us  [gather_call(): pl.pallas_call(gather_kernel, out_shape=[jax.ShapeDtypeStruct(s, bf16) fo...]
    reduce_scatter x5 -> x0, waiting for transfers between devices: 109 us -> none  [reduce_over_all(): lax.psum_scatter(value.astype(bf16), 'shard', scatter_dimension=dimension...]
    pallas_call x1, Pallas kernels: 345 us -> 443 us  [layer_call(): pl.pallas_call(layer_kernel, out_shape=[jax.ShapeDtypeStruct(s, bf16) for...]
    psum x1 -> x0, blocking collectives: 61.6 us -> none  [reduce_over_all(): return lax.psum(value.astype(bf16), 'rep').astype(f32)]
    dot_general x14 -> x0, matrix products: 54.9 us -> none  [the longest x10 31.7 us: contract(): lax.dot_general(left_side, right_side, (((left_dim,), (right_dim,)), ((),...]
    psum x1 -> x0, waiting for transfers between devices: 42.9 us -> none  [reduce_over_all(): return lax.psum(value.astype(bf16), 'rep').astype(f32)]
    convert_element_type x12 -> x3, other arithmetic: 28.5 us -> 2.44 us  [the longest x1 2 us: local(): hidden_out = (middle + add(o_own, o_core, o_x)).astype(bf16)]
  transfers between devices with their start and end apart: 6 -> 0, of which waited for: 3 -> 0; matrix products, arithmetic and copies ran while one was open for 8% -> 0% of each run, Pallas kernels for 0% -> 0%
where the time goes in v3:
time: 639 us; the launch traced here: 636 us
  Pallas kernels  532 us (83%)
  other arithmetic  45.5 us (7%)
  local copies, waits for them, and re-layouts  36.5 us (6%)
  matrix products  21 us (3%)
    pallas_call x1, Pallas kernels, layer_call(): pl.pallas_call(layer_kernel, out_shape=[jax.ShapeDtypeStruct(s, bf16) for...  443 us
    pallas_call x1, Pallas kernels, gather_call(): pl.pallas_call(gather_kernel, out_shape=[jax.ShapeDtypeStruct(s, bf16) fo...  88.2 us
    convert_element_type x1, other arithmetic, local(): grads = [grads[m].astype(f32) for m in range(3)]  28.9 us

profile of v3, /device:TPU:0, one launch (start us, length us, event | category | flops | bytes accessed | tf_op | source)
XLA Modules:
  0.0 635.8 jit_solution(16731845326490743967)
XLA Ops:
  2.1 1.4 maximum_maximum_fusion.sm
  3.5 88.2 %gather_weights.1 = (bf16[2,768,1536]{2,1,0:T(8,128)(2,1)}, bf16[2,768,256]{2,1,0:T(8,128)(2,1)}, bf16[2,768,256]{2,1,0:T(8,128)(2,1)}, bf16[2,768,1536]{2,1,0:T...) custom-call(bf16[768,1536]{1,0:T(8,128)(2,1)} %wq.1, ...), custom_call_target="tpu_custom_call" | custom-call | tf_op jit(solution)/shard_map/gather_weights/pallas_call | solution.py:198
  91.7 0.9 fusion.26
  93.5 2.0 copy.82
  96.0 0.8 slice_negate_fusion.1
  96.9 2.1 broadcast_multiply_fusion
  99.2 1.1 fusion.15
  100.4 6.6 %copy.85 = bf16[1536,1536]{1,0:T(8,128)(2,1)} copy(bf16[1536,1536]{0,1:T(8,128)(2,1)} %bitcast.77) | data formatting | bytes 9437184 | tf_op jit(solution)/shard_map/dot_general | solution.py:1172
  107.0 4.5 fusion.9
  112.0 0.9 fusion.7
  113.2 2.3 fusion.1
  115.5 2.6 fusion
  118.2 2.1 copy-done
  120.4 0.7 pad.12.lse
  121.9 7.2 %fusion.8 = bf16[2,128,6,512]{3,1,2,0:T(8,128)(2,1)S(1)} fusion(bf16[512,2,128,1]{0,2,3,1:T(8,128)(2,1)S(1)} %bitcast.90, f32[2,512,512,6]{2,1,3,0:T(8,128)} %copy-done, f32[2,6,512]{2,1,0:T(8,128)S(1)} %fusion, f32[2,6,512]{2,1,0:T(8,128)S(1)} %get-tuple-element.64, pred[512,512]{0,1:T(8,128)(4,1)S(1)} %fusion.13), kind=kOutput, calls=%fused_computation.21 | convolution fusion | flops 821821440 | bytes 14729216 | tf_op jit(solution)/shard_map/kgqs,skd->qkgd/dot_general | solution.py:1190
  129.1 5.3 multiply_reduce_fusion
  135.4 1.3 copy-done.5
  138.1 0.8 subtract_convert_fusion
  139.0 3.9 concatenate.28.hg
  142.9 1.6 copy.99.ob
  144.5 0.8 copy.108.k
  145.3 1.6 copy.98.q
  146.9 0.8 pad.13.rt
  147.7 1.4 slice_convert_fusion
  149.1 0.8 broadcast_in_dim.41.segc
  151.4 443.3 %layer.1 = (bf16[512,1536]{1,0:T(8,128)(2,1)}, bf16[512,1536]{1,0:T(8,128)(2,1)}, bf16[512,1536]{1,0:T(8,128)(2,1)}, bf16[3,8,768,768]{3,2,1,0:T(8,128)(2,1)}, b...) custom-call(bf16[512,1664]{1,0:T(8,128)(2,1)} %concatenate.28.hg, ...), custom_call_target="tpu_custom_call" | custom-call | tf_op jit(solution)/shard_map/layer/pallas_call | solution.py:1152
  594.7 28.9 %bitcast_convert_fusion = (f32[8,768,768]{2,1,0:T(8,128)}, f32[8,768,768]{2,1,0:T(8,128)}, f32[8,768,768]{2,1,0:T(8,128)}) fusion(bf16[3,8,768,768]{3,2,1,0:T(8,128)(2,1)} %get-tuple-element.39), kind=kLoop, calls=%fused_computation.5 | loop fusion | flops 14155776 | bytes 84934656 | tf_op jit(solution)/shard_map/convert_element_type | solution.py:1342
  623.7 5.1 fusion.28
  628.8 1.3 fusion.29
  630.0 1.2 copy-done.2
  631.2 2.0 add_convert_fusion
  634.5 1.1 copy.110
  (88 shorter events, 9.8 us)
Async XLA Ops:
  3.5 89.1 %copy-start.6 = (bf16[512,1536]{1,0:T(8,128)(2,1)S(1)}, bf16[512,1536]{1,0:T(8,128)(2,1)}, u32[]{:S(2)}) copy-start(bf16[512,1536]{1,0:T(8,128)(2,1)} %xin.1) | copy-start | bytes 4718596
  93.5 27.7 %copy-start.8 = (bf16[512,1536]{1,0:T(8,128)(2,1)}, bf16[512,1536]{1,0:T(8,128)(2,1)S(1)}, u32[]{:S(2)}) copy-start(bf16[512,1536]{1,0:T(8,128)(2,1)S(1)} %fusion.5.h1) | copy-start | bytes 4718596
  99.0 8.0 %copy-start.9 = (f32[512,128]{1,0:T(8,128)}, f32[512,128]{1,0:T(8,128)S(1)}, u32[]{:S(2)}) copy-start(f32[512,128]{1,0:T(8,128)S(1)} %get-tuple-element.61.cos) | copy-start | bytes 786436
  112.0 1.0 copy-start.21
  113.0 2.5 copy-start.3
  115.5 4.8 copy-start
  115.5 5.7 copy-start.17
  121.8 7.3 %copy-start.16 = (bf16[512,256]{1,0:T(8,128)(2,1)}, bf16[512,256]{1,0:T(8,128)(2,1)S(1)}, u32[]{:S(2)}) copy-start(bf16[512,256]{1,0:T(8,128)(2,1)S(1)} %convolution_convert_fusion.v) | copy-start | bytes 786436
  121.9 7.2 %copy-start.7 = (bf16[512,1536]{1,0:T(8,128)(2,1)S(1)}, bf16[512,1536]{1,0:T(8,128)(2,1)}, u32[]{:S(2)}) copy-start(bf16[512,1536]{1,0:T(8,128)(2,1)} %xin.1) | copy-start | bytes 4718596
  129.1 5.4 copy-start.14
  134.5 2.7 copy-start.1
  134.5 0.8 copy-start.20
  134.6 3.1 copy-start.22
  135.4 1.3 copy-start.5
  135.4 1.8 copy-start.18
  137.2 5.7 copy-start.15
  139.0 6.3 copy-start.4
  142.9 4.0 copy-start.19
  594.7 29.0 %slice-start = ((s8[5505024]{0:T(1024)(128)(4,1)}), s8[4194304]{0:T(1024)(128)(4,1)S(1)}, s32[]{:S(2)}) async-start(s8[5505024]{0:T(1024)(128)(4,1)} %bitcast.75), calls=%async_computation | async-start | bytes 8388608
  594.7 28.9 %slice-start.1 = ((s8[5505024]{0:T(1024)(128)(4,1)}), s8[1310720]{0:T(1024)(128)(4,1)S(1)}, s32[]{:S(2)}) async-start(s8[5505024]{0:T(1024)(128)(4,1)} %bitcast.75), calls=%async_computation.1 | async-start | bytes 2621440
  623.7 6.4 copy-start.10
  623.7 6.3 copy-start.11
  623.7 6.3 copy-start.12
  628.8 2.5 copy-start.2
  631.2 2.0 copy-start.23
  631.2 3.2 copy-start.13

commit v4 on v3

--- a/solution.py
+++ b/solution.py
@@ -94,123 +94,6 @@
     for device in partners:
         pl.semaphore_signal(barrier, inc=1, device_id=device, device_id_type=MESH)
     pl.semaphore_wait(barrier, len(partners))
-
-
-def gather_kernel(
-    wq, wk, wv, wo, sm, g, wg, wu, wd,
-    wqf, wkf, wvf, wof, smf, g4, w0,
-    bq, bk, bv, bo, bs, bg, loc, y_s, y_r, x_s, x_r, c_s, c_r, d_s, d_r, z_s, z_r,
-):
-    z, x, c, y = place()
-    ydev, xdev, cdev = at(z, x, c, 1 - y), at(z, 1 - x, c, y), at(z, x, 1 - c, y)
-    zdev = at(z + 1 - 2 * (z % 2), x, c, y)
-    greet((ydev, xdev, cdev, zdev))
-    parts, fulls, experts = (wq, wk, wv, wo), (wqf, wkf, wvf, wof), (wg, wu, wd)
-    piece = HALF // 4
-    mine = pl.ds((2 * x + c) * piece, piece)
-    theirs = pl.ds((2 * (1 - x) + c) * piece, piece)
-    expert = 2 * (2 * x + c)
-    h = z % 2
-    ys, xs, cs, ds, zs = [], [], [], [], []
-    for a in range(4):
-        ys.append(remote(parts[a].at[mine], fulls[a].at[y, mine], y_s.at[a], y_r.at[a], ydev))
-        ys[a].start()
-    ys.append(remote(sm, smf.at[y], y_s.at[4], y_r.at[4], ydev))
-    ys[4].start()
-    xs_g = remote(g, g4.at[2], x_s.at[4], x_r.at[4], xdev)
-    cs_g = remote(g, g4.at[1], c_s.at[4], c_r.at[4], cdev)
-    cs_g.start()
-    for m in range(3):
-        ys.append(
-            remote(
-                experts[m].at[expert, pl.ds(h * 384, 384)],
-                w0.at[m, pl.ds(h * 384, 384)],
-                y_s.at[5 + m],
-                y_r.at[5 + m],
-                ydev,
-            )
-        )
-        ys[5 + m].start()
-    pairs = [(parts[a], (bq, bk, bv, bo)[a], fulls[a].at[y]) for a in range(4)]
-    pairs += [(sm, bs, smf.at[y]), (g, bg, g4.at[0])]
-    loads = [pltpu.make_async_copy(p[0], p[1], loc.at[i]) for i, p in enumerate(pairs)]
-    locs = [pltpu.make_async_copy(p[1], p[2], loc.at[6 + i]) for i, p in enumerate(pairs)]
-    for copy in loads:
-        copy.start()
-    for i in range(6):
-        loads[i].wait()
-        locs[i].start()
-    for a in range(4):
-        ys[a].wait_recv()
-        xs.append(
-            remote(
-                fulls[a].at[1 - y, mine], fulls[a].at[1 - y, mine], x_s.at[a], x_r.at[a], xdev
-            )
-        )
-        cs.append(
-            remote(
-                fulls[a].at[1 - y, mine], fulls[a].at[1 - y, mine], c_s.at[a], c_r.at[a], cdev
-            )
-        )
-        xs[a].start()
-        cs[a].start()
-    xs_g.start()
-    for a in range(4):
-        xs[a].wait_recv()
-        ds.append(
-            remote(
-                fulls[a].at[1 - y, theirs], fulls[a].at[1 - y, theirs], d_s.at[a], d_r.at[a], cdev
-            )
-        )
-        ds[a].start()
-    for m in range(3):
-        ys[5 + m].wait_recv()
-        rows = pl.ds(h * 384, 384)
-        zs.append(remote(w0.at[m, rows], w0.at[m, rows], z_s.at[m], z_r.at[m], zdev))
-        zs[m].start()
-    xs_g.wait_recv()
-    ds_g = remote(g4.at[2], g4.at[3], d_s.at[4], d_r.at[4], cdev)
-    ds_g.start()
-    ys[4].wait_recv()
-    for copy in ys:
-        copy.wait_send()
-    for copy in xs + [xs_g]:
-        copy.wait_send()
-    xs_g = None
-    for copy in cs + [cs_g] + ds + [ds_g] + zs:
-        copy.wait()
-    for copy in locs:
-        copy.wait()
-
-
-def gather_call(wq, wk, wv, wo, sm, g, wg, wu, wd):
-    anyspace = pl.BlockSpec(memory_space=pl.ANY)
-    shapes = [
-        (2, HALF, MODEL_WIDTH),
-        (2, HALF, 256),
-        (2, HALF, 256),
-        (2, HALF, MODEL_WIDTH),
-        (2, 16, HALF),
-        (4, ROWS, MODEL_WIDTH),
-        (3, HALF, FF),
-    ]
-    dma = pltpu.SemaphoreType.DMA
-    return pl.pallas_call(
-        gather_kernel,
-        out_shape=[jax.ShapeDtypeStruct(s, bf16) for s in shapes],
-        in_specs=[anyspace] * 9,
-        out_specs=[anyspace] * 7,
-        scratch_shapes=[
-            pltpu.VMEM(s, bf16)
-            for s in (
-                (HALF, MODEL_WIDTH), (HALF, 256), (HALF, 256), (HALF, MODEL_WIDTH), (16, HALF),
-                (ROWS, MODEL_WIDTH),
-            )
-        ]
-        + [dma((12,)), dma((8,)), dma((8,))] + [dma((5,))] * 6 + [dma((3,))] * 2,
-        compiler_params=pltpu.CompilerParams(collective_id=1, has_side_effects=True),
-        name="gather_weights",
-    )(wq, wk, wv, wo, sm, g, wg, wu, wd)
 
 
 def nt_dot(a, b):
@@ -336,17 +219,22 @@
 PARTS = 2 * BLOCKS
 WIDTH = 512
 QUARTER = 96
-EXPERT_SLOTS = CHUNKS + 14
-PART_SLOTS = PARTS + 13
+SLACK = 3
+AT_ZL, AT_FL, AT_X = 1 + SLACK, 2 + 2 * SLACK, 3 + 3 * SLACK
+AT_CX, AT_CZ = AT_X + 16, AT_X + 20
+EXPERT_SLOTS = CHUNKS + AT_CZ + 1
+PART_SLOTS = PARTS + 25
 
 
 def layer_kernel(
-    hg, g4, w0, wg, wu, wd, y1, xin, h1, q, k, v, ob, lse, cos, sin, rt, routes, gain1, gain2,
-    segc, segr, wq, wk, wv, wo,
-    o_own, o_core, o_x, out, aout, smo, hgrad,
+    xin, g, wq, wk, wv, wo, sm, wg, wu, wd, cos, sin, routes, segc, segr,
+    o_own, o_core, o_x, out, aout, smo, hgrad, y1,
+    h1, q, k, v, ob, lse, wqo, wko, wvo, woo, smf, gl,
     r_core, r_x, gr, ya, za, zb, d, ca, yb, xb, zc, zd, sa,
-    H, W, DG, CR, CO, VA, VB, VS, VZ, VT, VF, FN, SM, SB,
-    loc, h_s, h_r, wy_s, wy_r, wz_s, wz_r, stg_sem, y_s, y_r, ld_a, ld_b,
+    H, W, DG, CR, CO, VA, VB, VS, VZ, VT, VF, FN, SM, SB, RT, G1, G2,
+    fl_s, wa_s, wa_r, wx_s, wx_r, wc_s, wc_r, wd_s, wd_r, wz_s, wz_r, hx_s, hx_r, hc_s, hc_r,
+    hd_s, hd_r, own_s, st_s,
+    loc, stg_sem, y_s, y_r, ld_a, ld_b,
     z1_s, z1_r, ld_z, z2_s, z2_r, ld_f, z3_s, z3_r, fo, x_s, x_r, c1_s, c1_r, c2_s, c2_r,
     z4_s, z4_r, rc_s, rc_r, rx_s, rx_r, rd_s, rd_r, ro,
     ac_s, ac_r, ald, ay_s, ay_r, aldy, ax_s, ax_r, aldx, az1_s, az1_r, aldz, az2_s, az2_r, aldf,
@@ -364,11 +252,212 @@
     other = 2 * (2 * (1 - x) + c)
     h = z % 2
     local_copy = pltpu.make_async_copy
-
-    hx = remote(hg, H.at[pl.ds(2 * ROWS, ROWS)], h_s.at[0], h_r.at[0], xdev)
-    hc = remote(hg, H.at[pl.ds(ROWS, ROWS)], h_s.at[1], h_r.at[1], cdev)
-    hx.start()
-    hc.start()
+    vm = pltpu.VMEM
+    part = lambda *shape: vm(shape, bf16)
+
+    kinds = ((wk, wko), (wv, wvo), (wq, wqo), (wo, woo))
+    piece = HALF // 4
+    mine = pl.ds((2 * x + c) * piece, piece)
+    theirs = pl.ds((2 * (1 - x) + c) * piece, piece)
+    wa = [remote(p[0].at[mine], p[1].at[mine], wa_s.at[n], wa_r.at[n], ydev) for n, p in enumerate(kinds)]
+    wa.append(remote(sm, smf, wa_s.at[4], wa_r.at[4], ydev))
+    wx = [remote(p[1].at[mine], p[1].at[mine], wx_s.at[n], wx_r.at[n], xdev) for n, p in enumerate(kinds)]
+    wc = [remote(p[1].at[mine], p[1].at[mine], wc_s.at[n], wc_r.at[n], cdev) for n, p in enumerate(kinds)]
+    wt = [
+        remote(p[1].at[theirs], p[1].at[theirs], wd_s.at[n], wd_r.at[n], cdev)
+        for n, p in enumerate(kinds)
+    ]
+    gx = remote(g, gl.at[1], wx_s.at[4], wx_r.at[4], xdev)
+    gc = remote(g, gl.at[0], wc_s.at[4], wc_r.at[4], cdev)
+    gt = remote(gl.at[1], gl.at[2], wd_s.at[4], wd_r.at[4], cdev)
+
+    def wy(n):
+        j, m = n // 3, n % 3
+        return remote(
+            shards[m].at[e0 + j, pl.ds(h * 384, 384)],
+            W.at[j, m, pl.ds(y * HALF + h * 384, 384)],
+            wa_s.at[5 + n],
+            wa_r.at[5 + n],
+            ydev,
+        )
+
+    def wz(n):
+        rows = pl.ds((1 - y) * HALF + h * 384, 384)
+        ref = W.at[n // 3, n % 3, rows]
+        return remote(ref, ref, wz_s.at[n], wz_r.at[n], zdev)
+
+    def own_half(n):
+        j, m = n // 3, n % 3
+        return local_copy(shards[m].at[e0 + j], W.at[j, m, pl.ds(y * HALF, HALF)], own_s.at[n])
+
+    def pass_on(n):
+        wy(n).wait_recv()
+        wz(n).start()
+
+    def hx(b):
+        src = H.at[pl.ds(b * 256, 256)]
+        return remote(src, H.at[pl.ds(2 * ROWS + b * 256, 256)], hx_s.at[b], hx_r.at[b], xdev)
+
+    def hc(b):
+        src = H.at[pl.ds(b * 256, 256)]
+        return remote(src, H.at[pl.ds(ROWS + b * 256, 256)], hc_s.at[b], hc_r.at[b], cdev)
+
+    def hd(b):
+        src = H.at[pl.ds(2 * ROWS + b * 256, 256)]
+        return remote(src, H.at[pl.ds(3 * ROWS + b * 256, 256)], hd_s.at[b], hd_r.at[b], cdev)
+
+    wa[4].start()
+    for n in range(4):
+        wa[n].start()
+    gc.start()
+    for n in range(6):
+        wy(n).start()
+
+    def front(X, H1, WQ, WKV, WO, Q, K, V, OB, BIAS, LSE, COS, SIN, RO, SC, SR, SF, Y1):
+        there = pl.ds(y * HALF, HALF)
+        away = pl.ds((1 - y) * HALF, HALF)
+        left, right = pl.ds(0, 256), pl.ds(256, 256)
+        pairs = [
+            (xin, X), (sm, SF.at[y]), (wk, WKV.at[there, left]), (wv, WKV.at[there, right]),
+            (wq, WQ.at[there]), (wo, WO.at[there]), (cos, COS), (sin, SIN), (routes, RO),
+            (segc, SC), (segr, SR),
+        ]
+        loads = [local_copy(p[0], p[1], fl_s.at[n]) for n, p in enumerate(pairs)]
+        for copy in loads:
+            copy.start()
+        for n in range(6):
+            own_half(n).start()
+        late = [
+            local_copy(wko, WKV.at[away, left], fl_s.at[11]),
+            local_copy(wvo, WKV.at[away, right], fl_s.at[12]),
+            local_copy(wqo, WQ.at[away], fl_s.at[13]),
+            local_copy(woo, WO.at[away], fl_s.at[14]),
+            local_copy(smf, SF.at[1 - y], fl_s.at[15]),
+        ]
+        wa[4].wait_recv()
+        late[4].start()
+        for n in (0, 1):
+            loads[n].wait()
+        late[4].wait()
+        row = lax.broadcasted_iota(jnp.int32, (16, HALF), 0)
+        RT[...] = jnp.zeros_like(RT)
+        for half in range(2):
+            columns = pl.ds(half * HALF, HALF)
+            small = SF[half].astype(f32)
+            RT[0:16, columns] = jnp.where(row < 8, small, 0.0).astype(bf16)
+            G1[:, columns] = jnp.sum(jnp.where(row == 8, small, 0.0), axis=0, keepdims=True)
+            G2[:, columns] = jnp.sum(jnp.where(row == 9, small, 0.0), axis=0, keepdims=True)
+
+        def norm_step(b, _):
+            rows = pl.ds(pl.multiple_of(b * 128, 128), 128)
+            value = X[rows, :].astype(f32)
+            r = lax.rsqrt(jnp.mean(value * value, axis=1, keepdims=True) + epsilon)
+            H1[rows, :] = (value * r * G1[...]).astype(bf16)
+            return 0
+
+        lax.fori_loop(0, ROWS // 128, norm_step, 0)
+        for n in range(2, 11):
+            loads[n].wait()
+        mask_bias(SC, SR, BIAS)
+        for n in range(4):
+            wa[n].wait_recv()
+            wx[n].start()
+            wc[n].start()
+        gx.start()
+        for n in range(3):
+            wx[n].wait_recv()
+            wt[n].start()
+        for n in range(3):
+            wc[n].wait_recv()
+            wt[n].wait_recv()
+            late[n].start()
+        for n in range(3):
+            late[n].wait()
+
+        def rotate(u):
+            return u * COS[...] + pltpu.roll(u, 64, 1) * SIN[...]
+
+        def query_step(t, _):
+            begin = pl.multiple_of(t * 512, 512)
+            tile = jnp.dot(H1[...], WQ[:, pl.ds(begin, 512)], preferred_element_type=f32)
+            for n in range(4):
+                u = tile[:, n * HEAD_SIZE : (n + 1) * HEAD_SIZE]
+                Q[:, pl.ds(begin + n * HEAD_SIZE, HEAD_SIZE)] = rotate(u).astype(bf16)
+            return 0
+
+        tile = jnp.dot(H1[...], WKV[...], preferred_element_type=f32)
+        for n in range(2):
+            columns = pl.ds(n * HEAD_SIZE, HEAD_SIZE)
+            u = tile[:, n * HEAD_SIZE : (n + 1) * HEAD_SIZE]
+            K[:, columns] = rotate(u).astype(bf16)
+        V[...] = tile[:, 256:].astype(bf16)
+        lax.fori_loop(0, 3, query_step, 0)
+        wx[3].wait_recv()
+        wt[3].start()
+        pass_on(0)
+        LSE[...] = jnp.zeros_like(LSE)
+        scale = HEAD_SIZE ** (-0.5)
+        for b in range(2):
+            rows, keys = pl.ds(b * 256, 256), pl.ds(0, 256 * (b + 1))
+
+            def head(n, _, rows=rows, keys=keys):
+                columns = pl.ds(pl.multiple_of(n * HEAD_SIZE, HEAD_SIZE), HEAD_SIZE)
+                shared = pl.ds(pl.multiple_of(n // 6 * HEAD_SIZE, HEAD_SIZE), HEAD_SIZE)
+                logits = nt_dot(Q[rows, columns], K[keys, shared]) * scale + BIAS[rows, keys]
+                top = jnp.max(logits, axis=1, keepdims=True)
+                p = jnp.exp(logits - top)
+                total = jnp.sum(p, axis=1, keepdims=True)
+                lane = lax.broadcasted_iota(jnp.int32, (256, PAD), 1)
+                LSE[rows, :] = jnp.where(lane == n, top + jnp.log(total), LSE[rows, :])
+                p = (p * (1.0 / total)).astype(bf16)
+                mixed = jnp.dot(p, V[keys, shared], preferred_element_type=f32)
+                OB[rows, columns] = mixed.astype(bf16)
+                return 0
+
+            lax.fori_loop(0, QUERY_HEADS, head, 0)
+            if b == 0:
+                wc[3].wait_recv()
+                wt[3].wait_recv()
+                late[3].start()
+                pass_on(1)
+                late[3].wait()
+            for t in range(3):
+                ns = pl.ds(t * 512, 512)
+                Y1[rows, ns] = X[rows, ns].astype(f32) + jnp.dot(
+                    OB[rows, :], WO[:, ns], preferred_element_type=f32
+                )
+            for n in range(2):
+                block = pl.ds(b * 256 + n * 128, 128)
+                value = Y1[block, :]
+                r = lax.rsqrt(jnp.mean(value * value, axis=1, keepdims=True) + epsilon)
+                h2 = (value * r * G2[...]).astype(bf16)
+                H[block, :MODEL_WIDTH] = h2
+                gates = router_rows(h2, RT[...], RO[block, :])[3]
+                high = gates.astype(bf16).astype(f32)
+                H[block, MODEL_WIDTH:] = (high + pltpu.roll(gates - high, 8, 1)).astype(bf16)
+            hx(b).start()
+            hc(b).start()
+        stores = [
+            local_copy(p[0], p[1], st_s.at[n])
+            for n, p in enumerate(
+                ((Y1, y1), (H1, h1), (Q, q), (K, k), (V, v), (OB, ob), (LSE, lse))
+            )
+        ]
+        for copy in stores:
+            copy.start()
+        pass_on(2)
+        for copy in stores:
+            copy.wait()
+
+    pl.run_scoped(
+        front,
+        part(ROWS, MODEL_WIDTH), part(ROWS, MODEL_WIDTH), part(MODEL_WIDTH, MODEL_WIDTH),
+        part(MODEL_WIDTH, 512), part(MODEL_WIDTH, MODEL_WIDTH), part(ROWS, MODEL_WIDTH),
+        part(ROWS, 256), part(ROWS, 256), part(ROWS, MODEL_WIDTH), vm((ROWS, ROWS), f32),
+        vm((ROWS, PAD), f32), vm((ROWS, PAD), f32), vm((ROWS, PAD), f32),
+        vm((ROWS, PAD), jnp.int32), vm((ROWS, PAD), jnp.int32), vm((8, ROWS), jnp.int32),
+        part(2, 16, HALF), vm((ROWS, MODEL_WIDTH), f32),
+    )
 
     def parts_of(n):
         return n // (3 * PER), (n // PER) % 3, n % PER
@@ -420,6 +509,9 @@
     def c2_copy(n):
         return remote(spot(n, other), spot(n, other), c2_s.at[n], c2_r.at[n], cdev)
 
+    def handed(n):
+        return n % 2 == 1
+
     def crosses(n):
         return (n % 2 == 0) | ((n % 4 == 1) & mid) | ((n % 4 == 3) & end)
 
@@ -428,79 +520,93 @@
         return pl.when(ok if cond is None else ok & cond)
 
     def slot(s):
-        @when(s - 13, jnp.logical_not(crosses(s - 13 + 4 * CHUNKS)))
-        def _():
-            z4_copy(s - 13).wait_recv()
-            c2_copy(s - 13).start()
-
-        crossed = crosses(s - 11 + 4 * CHUNKS)
-
-        @when(s - 11, crossed)
-        def _():
-            x_copy(s - 11).wait_recv()
-            c2_copy(s - 11).start()
-
-        @when(s - 11, crossed & ((s + 1) % 2 == 1))
-        def _():
-            z4_copy(s - 11).start()
-
-        @when(s - 9, mid)
-        def _():
-            store_f(s - 9).wait()
-            z3_copy(s - 9).wait_send()
-
-        @when(s - 9, end)
-        def _():
-            z3_copy(s - 9).wait_recv()
-
-        @when(s - 9, crosses(s - 9 + 4 * CHUNKS))
-        def _():
-            x_copy(s - 9).start()
-
-        @when(s - 9)
-        def _():
-            c1_copy(s - 9).start()
-
-        @when(s - 7, mid)
-        def _():
-            n = s - 7
+        n = s - AT_CZ
+
+        @when(n, jnp.logical_not(crosses(n + 4 * CHUNKS)))
+        def _(n=n):
+            z4_copy(n).wait_recv()
+            c2_copy(n).start()
+
+        n = s - AT_CX
+        crossed = crosses(n + 4 * CHUNKS)
+
+        @when(n, crossed)
+        def _(n=n):
+            x_copy(n).wait_recv()
+            c2_copy(n).start()
+
+        @when(n, crossed & handed(n + 4 * CHUNKS))
+        def _(n=n):
+            z4_copy(n).start()
+
+        n = s - AT_X
+
+        @when(n, mid)
+        def _(n=n):
+            store_f(n).wait()
+            z3_copy(n).wait_send()
+
+        @when(n, end)
+        def _(n=n):
+            z3_copy(n).wait_recv()
+
+        @when(n, crosses(n + 4 * CHUNKS))
+        def _(n=n):
+            x_copy(n).start()
+
+        @when(n)
+        def _(n=n):
+            c1_copy(n).start()
+
+        n = s - AT_FL - 1
+
+        @when(n, mid)
+        def _(n=n):
             load_f(n).wait()
             z2_copy(n).wait_send()
             FN[n % 4] = (VT[n % 4].astype(f32) + VF[n % 2].astype(f32)).astype(bf16)
             z3_copy(n).start()
             store_f(n).start()
 
-        @when(s - 6, mid)
-        def _():
-            z2_copy(s - 6).wait_recv()
-            load_f(s - 6).start()
-
-        @when(s - 4, mid)
-        def _():
-            n = s - 4
+        n = s - AT_FL
+
+        @when(n, mid)
+        def _(n=n):
+            z2_copy(n).wait_recv()
+            load_f(n).start()
+
+        n = s - AT_ZL - 1
+
+        @when(n, mid)
+        def _(n=n):
             load_z(n).wait()
             VT[n % 4] = (VS[n % 4].astype(f32) + VZ[n % 2].astype(f32)).astype(bf16)
             z2_copy(n).start()
 
-        @when(s - 3, mid)
-        def _():
-            z1_copy(s - 3).wait_recv()
-            load_z(s - 3).start()
-
-        @when(s - 5, end)
-        def _():
-            z1_copy(s - 5).wait_send()
-
-        @when(s - 1)
-        def _():
-            n = s - 1
+        n = s - AT_ZL
+
+        @when(n, mid)
+        def _(n=n):
+            z1_copy(n).wait_recv()
+            load_z(n).start()
+
+        n = s - 5
+
+        @when(n, end)
+        def _(n=n):
+            z1_copy(n).wait_send()
+
+        n = s - 1
+
+        @when(n)
+        def _(n=n):
             load_a(n).wait()
             load_b(n).wait()
             VS[n % 4] = (VA[n % 2].astype(f32) + VB[n % 2].astype(f32)).astype(bf16)
 
-        @when(s - 1, end)
-        def _():
-            z1_copy(s - 1).start()
+        @when(n, end)
+        def _(n=n):
+            z1_copy(n).start()
 
         @when(s)
         def _():
@@ -519,33 +625,13 @@
     first, zeroth = pl.ds(ROWS, ROWS), pl.ds(0, ROWS)
 
     def experts(G, ACT, STG, RS, OS):
-        own = [
-            local_copy(hg, H.at[pl.ds(0, ROWS)], loc.at[0]),
-            local_copy(g4, G, loc.at[1]),
-            local_copy(w0, W.at[0, :, pl.ds((1 - y) * HALF, HALF)], loc.at[2]),
+        gain_rows = [
+            local_copy(src, G.at[pl.ds(n * ROWS, ROWS)], loc.at[n])
+            for n, src in enumerate((g, gl.at[0], gl.at[1], gl.at[2]))
         ]
-        for m in range(3):
-            own.append(
-                local_copy(shards[m].at[e0 + 1], W.at[1, m, pl.ds(y * HALF, HALF)], loc.at[3 + m])
-            )
-        for m in range(3):
-            own.append(
-                local_copy(shards[m].at[e0], W.at[0, m, pl.ds(y * HALF, HALF)], loc.at[6 + m])
-            )
-        wys = []
-        for m in range(3):
-            wys.append(
-                remote(
-                    shards[m].at[e0 + 1, pl.ds(h * 384, 384)],
-                    W.at[1, m, pl.ds(y * HALF + h * 384, 384)],
-                    wy_s.at[m],
-                    wy_r.at[m],
-                    ydev,
-                )
-            )
-            wys[m].start()
-        for copy in own:
-            copy.start()
+        gain_rows[0].start()
+        gc.wait_recv()
+        gain_rows[1].start()
 
         def gate_of(j, rows):
             lane = lax.broadcasted_iota(jnp.int32, (2 * ROWS, PAD), 1)
@@ -597,13 +683,15 @@
             e = e + nt_dot(ACT[1, 2, rows, :], W[1, 1, ns, :])
             return o, e
 
+        def store_tile(j, m, half, i, place_in):
+            rows = pl.ds(half * HALF + i * 384, 384)
+            return local_copy(STG.at[place_in], gr.at[j, m, rows], stg_sem.at[place_in])
+
         def weight_tile(j, m, left, half, i, place_in):
             begin = half * HALF + i * 384
             lhs = left[:, pl.ds(pl.multiple_of(begin, 128), 384)]
             STG[place_in] = tn_dot(lhs, ACT[j, (m + 1) % 3]).astype(bf16)
-            copy = local_copy(
-                STG.at[place_in], gr.at[j, m, pl.ds(begin, 384)], stg_sem.at[place_in]
-            )
+            copy = store_tile(j, m, half, i, place_in)
             copy.start()
             return copy
 
@@ -614,18 +702,23 @@
                 def step(n, _, left=left, m0=m0, done=done):
                     m, i = m0 + n // 2, n % 2
                     away = weight_tile(j, m, left, 1 - y, i, 0)
-                    here = weight_tile(j, m, left, y, i, 1)
+
+                    @pl.when(n + done > 0)
+                    def _():
+                        store_tile(j, m, y, i, 1).wait()
+
+                    weight_tile(j, m, left, y, i, 1)
                     away.wait()
                     begin = (j * 3 + m) * PER + i * (384 // CHUNK)
                     for p in range(384 // CHUNK):
                         y_copy(begin + p).start()
                     if base is not None:
                         slot(base + done + n)
-                    here.wait()
                     return 0
 
                 lax.fori_loop(0, steps, step, 0)
                 done += steps
+            store_tile(j, 2, y, 1, 1).wait()
 
         def rc_copy(t, which):
             ns = pl.ds(pl.multiple_of(t * 512, 512), 512)
@@ -646,30 +739,35 @@
             ns = pl.ds(pl.multiple_of(t * 512, 512), 512)
             return local_copy(OS.at[t % 2], o_own.at[:, ns], ro.at[t])
 
-        own[1].wait()
-        own[2].wait()
-        own[0].wait()
-        for m in range(3):
-            own[6 + m].wait()
-        hc.wait_recv()
+        for n in range(3):
+            wz(n).wait_recv()
+            own_half(n).wait()
+        gain_rows[0].wait()
+        gain_rows[1].wait()
+        for b in range(2):
+            hc(b).wait_recv()
+        pass_on(3)
         forward(0, 0)
-        hx.wait_recv()
-        hd = remote(H.at[second], H.at[third], h_s.at[2], h_r.at[2], cdev)
-        hd.start()
-        wzs = []
-        for m in range(3):
-            wys[m].wait_recv()
-            rows = pl.ds((1 - y) * HALF + h * 384, 384)
-            wzs.append(remote(W.at[1, m, rows], W.at[1, m, rows], wz_s.at[m], wz_r.at[m], zdev))
-            wzs[m].start()
-        hd.wait_recv()
+        gx.wait_recv()
+        gt.start()
+        gain_rows[2].start()
+        pass_on(4)
+        for b in range(2):
+            hx(b).wait_recv()
+            hd(b).start()
+        pass_on(5)
+        gt.wait_recv()
+        gain_rows[3].start()
+        for b in range(2):
+            hd(b).wait_recv()
+        gain_rows[2].wait()
+        gain_rows[3].wait()
         forward(0, 2 * ROWS)
         weight_grads(0)
-        for m in range(3):
-            wzs[m].wait_recv()
-            own[3 + m].wait()
-        forward(1, 0, 0)
-        forward(1, 2 * ROWS, 3)
+        for n in range(3, 6):
+            wz(n).wait_recv()
+            own_half(n).wait()
+        forward(1, 2 * ROWS, 0)
 
         def third_step(t, _):
             ns = pl.ds(pl.multiple_of(t * 512, 512), 512)
@@ -684,7 +782,7 @@
             OS[t % 2] = o.astype(bf16)
             rc_copy(t, 0).start()
             rc_copy(t, 1).start()
-            slot(6 + t)
+            slot(3 + t)
             return 0
 
         lax.fori_loop(0, 3, third_step, 0)
@@ -700,13 +798,14 @@
             rc_copy(t, 1).wait_recv()
             CR[:, ns] = (CR[:, ns].astype(f32) + e).astype(bf16)
             CO[:, ns] = (CO[:, ns].astype(f32) + o).astype(bf16)
-            slot(9 + t)
+            slot(6 + t)
             return 0
 
         lax.fori_loop(0, 3, second_step, 0)
         dg_copy.wait_recv()
         CR[:, MODEL_WIDTH:] = CR[:, MODEL_WIDTH:] + DG[second, :]
         rx.start()
+        forward(1, 0, 9)
         weight_grads(1, 12)
         for which in range(2):
             for t in (1, 2):
@@ -756,12 +855,21 @@
             rb_copy(t, 1).wait_recv()
         for t in (1, 2):
             ro_copy(t).wait()
-        for m in range(3):
-            wys[m].wait_send()
-            wzs[m].wait_send()
-        hx.wait_send()
-        hc.wait_send()
-        hd.wait_send()
+        for n in range(6):
+            wy(n).wait_send()
+            wz(n).wait_send()
+        for n in range(4):
+            wa[n].wait_send()
+            wx[n].wait_send()
+            wc[n].wait_send()
+            wt[n].wait_send()
+        wa[4].wait_send()
+        for copy in (gx, gc, gt):
+            copy.wait_send()
+        for b in range(2):
+            hx(b).wait_send()
+            hc(b).wait_send()
+            hd(b).wait_send()
         rx.wait_send()
 
     rx = remote(CR, r_x, rx_s.at[0], rx_r.at[0], xdev)
@@ -769,7 +877,6 @@
     tail_b = remote(
         DG.at[first], r_core.at[:, pl.ds(MODEL_WIDTH, PAD)], rd_s.at[7], rd_r.at[7], cdev
     )
-    vm = pltpu.VMEM
     pl.run_scoped(
         experts,
         vm((4 * ROWS, MODEL_WIDTH), bf16),
@@ -782,31 +889,35 @@
     tail_b.wait()
 
     def attention(
-        Y1, DY, GB, XB, H1, OB, QB, KB, VV, DA, DOB, DQKV, BIAS, LSE, COS, SIN, RT, RO, G1, G2,
-        SC, SR, DL, GS, DK, DV, HG, STG,
+        Y1, DY, GB, XB, H1, OB, QB, KB, VV, DA, DOB, DQKV, BIAS, LSE, COS, SIN, RO,
+        SC, SR, DL, GS, DK, DV, STG,
         AA, AB, PP, VY, QQ, VX, AS, AZ, AT, AF, AN,
     ):
         pairs = [
-            (y1, Y1), (g4.at[pl.ds(0, ROWS)], GB), (xin, XB), (h1, H1), (ob, OB), (q, QB), (k, KB),
-            (v, VV), (lse, LSE), (cos, COS), (sin, SIN), (rt, RT), (routes, RO), (gain1, G1),
-            (gain2, G2), (segc, SC), (segr, SR), (r_core, H.at[second]),
+            (segc, SC), (segr, SR), (y1, Y1), (g, GB), (routes, RO), (r_core, H.at[second]),
+            (ob, OB), (q, QB), (k, KB), (v, VV), (lse, LSE), (cos, COS), (sin, SIN), (h1, H1),
+            (xin, XB),
         ]
-        for half in range(2):
-            rows = pl.ds(half * HALF, HALF)
-            for n, w in ((0, wq), (1, wo)):
-                for part in range(2):
-                    columns = pl.ds(part * HALF, HALF)
-                    pairs.append((w.at[half, :, columns], W.at[n, part, rows]))
-            pairs.append((wk.at[half], W.at[0, 2, rows, pl.ds(0, 256)]))
-            pairs.append((wv.at[half], W.at[0, 2, rows, pl.ds(256, 256)]))
+        for n, ws in ((1, (wo, woo)), (0, (wq, wqo))):
+            for w, rows in zip(ws, (pl.ds(y * HALF, HALF), pl.ds((1 - y) * HALF, HALF))):
+                for side in range(2):
+                    pairs.append((w.at[:, pl.ds(side * HALF, HALF)], W.at[n, side, rows]))
+        for ws, columns in (((wk, wko), pl.ds(0, 256)), ((wv, wvo), pl.ds(256, 256))):
+            for w, rows in zip(ws, (pl.ds(y * HALF, HALF), pl.ds((1 - y) * HALF, HALF))):
+                pairs.append((w, W.at[0, 2, rows, columns]))
         loads = [local_copy(p[0], p[1], att.at[n]) for n, p in enumerate(pairs)]
         for copy in loads:
             copy.start()
+
+        def need(first, last):
+            for copy in loads[first:last]:
+                copy.wait()
+
         slots(24, 26)
-        for copy in loads:
-            copy.wait()
+        need(0, 2)
         mask_bias(SC, SR, BIAS)
         slots(26, 28)
+        need(2, 6)
         rx.wait_recv()
         last = local_copy(r_x, H.at[third], att.at[len(pairs)])
         last.start()
@@ -878,81 +989,84 @@
             return pl.when(ok if cond is None else ok & cond)
 
         def aslot(s):
-            @awhen(s - 13)
-            def _():
-                axg_copy(s - 13).wait_recv()
-                ac2_copy(s - 13).start()
-
-            @awhen(s - 12, mid)
-            def _():
-                astore(s - 12).wait()
-                az3_copy(s - 12).wait_send()
-
-            @awhen(s - 12, end)
-            def _():
-                az3_copy(s - 12).wait_recv()
-                az1_copy(s - 12).wait_send()
-
-            @awhen(s - 12)
-            def _():
-                axg_copy(s - 12).start()
-                ac1_copy(s - 12).start()
-
-            @awhen(s - 10, mid)
-            def _():
-                n = s - 10
+            @awhen(s - 24)
+            def _():
+                axg_copy(s - 24).wait_recv()
+                ac2_copy(s - 24).start()
+
+            @awhen(s - 20, mid)
+            def _():
+                astore(s - 20).wait()
+                az3_copy(s - 20).wait_send()
+
+            @awhen(s - 20, end)
+            def _():
+                az3_copy(s - 20).wait_recv()
+
+            @awhen(s - 20)
+            def _():
+                axg_copy(s - 20).start()
+                ac1_copy(s - 20).start()
+
+            @awhen(s - 17, mid)
+            def _():
+                n = s - 17
                 aload_f(n).wait()
                 az2_copy(n).wait_send()
                 AN[n % 4] = (AT[n % 4].astype(f32) + AF[n % 2].astype(f32)).astype(bf16)
                 az3_copy(n).start()
                 astore(n).start()
 
-            @awhen(s - 9, mid)
-            def _():
-                az2_copy(s - 9).wait_recv()
-                aload_f(s - 9).start()
-
-            @awhen(s - 8, mid)
-            def _():
-                n = s - 8
+            @awhen(s - 16, mid)
+            def _():
+                az2_copy(s - 16).wait_recv()
+                aload_f(s - 16).start()
+
+            @awhen(s - 13, mid)
+            def _():
+                n = s - 13
                 aload_z(n).wait()
                 AT[n % 4] = (AS[n % 8].astype(f32) + AZ[n % 2].astype(f32)).astype(bf16)
                 az2_copy(n).start()
 
-            @awhen(s - 7, mid)
-            def _():
-                az1_copy(s - 7).wait_recv()
-                aload_z(s - 7).start()
-
-            @awhen(s - 6)
-            def _():
-                n = s - 6
+            @awhen(s - 13, end)
+            def _():
+                az1_copy(s - 13).wait_send()
+
+            @awhen(s - 12, mid)
+            def _():
+                az1_copy(s - 12).wait_recv()
+                aload_z(s - 12).start()
+
+            @awhen(s - 9)
+            def _():
+                n = s - 9
                 aload_x(n).wait()
                 ax_copy(n).wait_send()
                 mine = pl.ds(pl.multiple_of(x * QUARTER, 16), QUARTER)
                 AS[n % 8] = (QQ[n % 4, mine, :].astype(f32) + VX[n % 2].astype(f32)).astype(bf16)
 
-            @awhen(s - 6, end)
-            def _():
-                az1_copy(s - 6).start()
+            @awhen(s - 9, end)
+            def _():
+                az1_copy(s - 9).start()
+
+            @awhen(s - 8)
+            def _():
+                ax_copy(s - 8).wait_recv()
+                aload_x(s - 8).start()
 
             @awhen(s - 5)
             def _():
-                ax_copy(s - 5).wait_recv()
-                aload_x(s - 5).start()
-
-            @awhen(s - 4)
-            def _():
-                n = s - 4
+                n = s - 5
                 aload_y(n).wait()
                 ay_copy(n).wait_send()
                 QQ[n % 4] = (PP[n % 4, y].astype(f32) + VY[n % 2].astype(f32)).astype(bf16)
                 ax_copy(n).start()
 
-            @awhen(s - 3)
-            def _():
-                ay_copy(s - 3).wait_recv()
-                aload_y(s - 3).start()
+            @awhen(s - 4)
+            def _():
+                ay_copy(s - 4).wait_recv()
+                aload_y(s - 4).start()
 
             @awhen(s - 1)
             def _():
@@ -991,9 +1105,9 @@
         )
         for half in range(2):
             columns = pl.ds(half * HALF, HALF)
-            SM[half, 1:2, :] = GS[:, columns].astype(bf16)
+            SM[half, 9:10, :] = GS[:, columns].astype(bf16)
             router = tn_dot(DL[...], H[zeroth, columns])
-            SM[half, 2:10, :] = router[0:8].astype(bf16)
+            SM[half, 0:8, :] = router[0:8].astype(bf16)
             SM[half, 10:16, :] = jnp.zeros((6, HALF), bf16)
 
         def out_block(b, _):
@@ -1001,7 +1115,9 @@
             slot(28 + b)
             return 0
 
+        need(6, 7)
         lax.fori_loop(0, 3, out_block, 0)
+        need(15, 19)
 
         def dob_tile(t, _):
             ns = pl.ds(pl.multiple_of(t * 512, 512), 512)
@@ -1011,6 +1127,7 @@
             return 0
 
         lax.fori_loop(0, 3, dob_tile, 0)
+        need(7, 13)
         state = [34, 0]
 
         def tick():
@@ -1034,7 +1151,10 @@
             slot(done + b)
             return 0
 
+        need(13, 14)
         lax.fori_loop(0, 4, qkv_block, 0)
+        need(14, 15)
+        need(19, 27)
         done += 4
 
         def dh1_tile(t, _):
@@ -1048,10 +1168,10 @@
 
         lax.fori_loop(0, 3, dh1_tile, 0)
         done, parts_done = done + 3, parts_done + 3
-        first_backward(Y1, XB, DY, G1, HG, GS)
+        first_backward(Y1, XB, DY, G1, GB, GS)
         for half in range(2):
-            SM[half, 0:1, :] = GS[:, pl.ds(half * HALF, HALF)].astype(bf16)
-        result = local_copy(HG, hgrad, att.at[len(pairs) + 1])
+            SM[half, 8:9, :] = GS[:, pl.ds(half * HALF, HALF)].astype(bf16)
+        result = local_copy(GB, hgrad, att.at[len(pairs) + 1])
         result.start()
 
         for i, device in enumerate((cdev, xdev, ydev, zdev, mdev)):
@@ -1088,7 +1208,6 @@
 
         lax.fori_loop(0, PARTS, finish_part, 0)
 
-    part = lambda *shape: vm(shape, bf16)
     pl.run_scoped(
         attention,
         vm((ROWS, MODEL_WIDTH), f32), vm((ROWS, MODEL_WIDTH), f32),
@@ -1096,10 +1215,9 @@
         part(ROWS, MODEL_WIDTH), part(ROWS, MODEL_WIDTH), part(ROWS, 256), part(ROWS, 256),
         part(ROWS, MODEL_WIDTH), part(ROWS, MODEL_WIDTH), part(ROWS, 2048),
         vm((ROWS, ROWS), f32), vm((ROWS, PAD), f32), vm((ROWS, PAD), f32), vm((ROWS, PAD), f32),
-        part(PAD, MODEL_WIDTH), vm((ROWS, PAD), jnp.int32), vm((1, MODEL_WIDTH), f32),
-        vm((1, MODEL_WIDTH), f32), vm((ROWS, PAD), jnp.int32), vm((8, ROWS), jnp.int32),
+        vm((ROWS, PAD), jnp.int32), vm((ROWS, PAD), jnp.int32), vm((8, ROWS), jnp.int32),
         part(ROWS, PAD), vm((1, MODEL_WIDTH), f32), vm((2, ROWS, PAD), f32),
-        vm((2, ROWS, PAD), f32), part(ROWS, MODEL_WIDTH), part(2, HALF, WIDTH),
+        vm((2, ROWS, PAD), f32), part(2, HALF, WIDTH),
         part(2, 2, 192, WIDTH), part(2, 2, 192, WIDTH), part(4, 2, 192, WIDTH),
         part(2, 192, WIDTH), part(4, 192, WIDTH), part(2, QUARTER, WIDTH), part(8, QUARTER, WIDTH),
         part(2, QUARTER, WIDTH), part(4, QUARTER, WIDTH), part(2, QUARTER, WIDTH),
@@ -1112,7 +1230,7 @@
         def _():
             x_copy(n).wait_send()
 
-        @pl.when(crosses(n) & (n % 2 == 1))
+        @pl.when(crosses(n) & handed(n))
         def _():
             z4_copy(n).wait_send()
 
@@ -1129,19 +1247,30 @@
     dma = pltpu.SemaphoreType.DMA
     vmem = lambda *s: pltpu.VMEM(s, bf16)
     n = PARTS
-    shapes = [(ROWS, MODEL_WIDTH)] * 3
-    shapes += [(3, 8, HALF, FF), (HALF, BLOCKS * WIDTH), (2, 16, HALF), (ROWS, MODEL_WIDTH)]
+    wide, narrow = (ROWS, MODEL_WIDTH), (ROWS, 256)
+    shapes = [wide] * 3
+    shapes += [(3, 8, HALF, FF), (HALF, BLOCKS * WIDTH), (2, 16, HALF), wide]
+    shapes += [(*wide, f32), wide, wide, narrow, narrow, wide, (ROWS, PAD, f32)]
+    shapes += [(HALF, MODEL_WIDTH), (HALF, 256), (HALF, 256), (HALF, MODEL_WIDTH), (16, HALF)]
+    shapes += [(3, ROWS, MODEL_WIDTH)]
     shapes += [(ROWS, WIDE)] * 2 + [(2, 3, MODEL_WIDTH, FF)] + [(CHUNKS, CHUNK, FF)] * 3
     shapes += [(BLOCKS, 2, HALF, WIDTH), (n, 2, 192, WIDTH), (n, 192, WIDTH)]
     shapes += [(n, QUARTER, WIDTH)] * 3 + [(5, 2, 16, HALF)]
+    outputs = [
+        jax.ShapeDtypeStruct(s[:-1], f32) if s[-1] is f32 else jax.ShapeDtypeStruct(s, bf16)
+        for s in shapes
+    ]
     many, few = dma((CHUNKS,)), dma((n,))
     scratch = [
         vmem(4 * ROWS, WIDE), vmem(2, 3, MODEL_WIDTH, FF), vmem(4 * ROWS, PAD), vmem(ROWS, WIDE),
         vmem(ROWS, MODEL_WIDTH), vmem(2, CHUNK, FF), vmem(2, CHUNK, FF), vmem(4, CHUNK, FF),
         vmem(2, CHUNK, FF), vmem(4, CHUNK, FF), vmem(2, CHUNK, FF), vmem(4, CHUNK, FF),
-        vmem(2, 16, HALF), vmem(2, 16, HALF),
-        dma((9,)), dma((3,)), dma((3,)), dma((3,)), dma((3,)), dma((3,)), dma((3,)),
-        dma((2,)), many, many, dma((2,)), dma((2,)),
+        vmem(2, 16, HALF), vmem(2, 16, HALF), vmem(PAD, MODEL_WIDTH),
+        pltpu.VMEM((1, MODEL_WIDTH), f32), pltpu.VMEM((1, MODEL_WIDTH), f32),
+        dma((16,)), dma((11,)), dma((11,)), dma((5,)), dma((5,)), dma((5,)), dma((5,)), dma((5,)),
+        dma((5,)), dma((6,)), dma((6,)), dma((2,)), dma((2,)), dma((2,)), dma((2,)), dma((2,)),
+        dma((2,)), dma((6,)), dma((7,)),
+        dma((4,)), dma((2,)), many, many, dma((2,)), dma((2,)),
         many, many, dma((2,)), many, many, dma((2,)),
         many, many, dma((4,)), many, many, many, many, many, many, many, many,
         dma((2, 3)), dma((2, 3)), dma((2,)), dma((2,)), dma((8,)), dma((8,)), dma((3,)),
@@ -1151,15 +1280,15 @@
     ]
     return pl.pallas_call(
         layer_kernel,
-        out_shape=[jax.ShapeDtypeStruct(s, bf16) for s in shapes],
+        out_shape=outputs,
         in_specs=[anyspace] * len(arrays),
         out_specs=[anyspace] * len(shapes),
         scratch_shapes=scratch,
         compiler_params=pltpu.CompilerParams(
-            collective_id=2, has_side_effects=True, vmem_limit_bytes=66 * 1000 * 1000
+            collective_id=2, has_side_effects=True, vmem_limit_bytes=67 * 1000 * 1000
         ),
         name="layer",
-    )(*arrays)[:7]
+    )(*arrays)[:8]
 
 
 def attention_forward(hidden, segments, gain_one, w_q, w_k, w_v, w_o, gain_two):
@@ -1286,59 +1415,32 @@
     w_down,
 ):
     small = jnp.concatenate(
-        [norm1_gain[None], norm2_gain[None], w_router.T, jnp.zeros((6, HALF), bf16)], axis=0
+        [w_router.T, norm1_gain[None], norm2_gain[None], jnp.zeros((6, HALF), bf16)], axis=0
     )
-    w_q, w_k, w_v, w_o, small, g4, w0 = gather_call(
-        w_query, key_weight, value_weight, w_out, small, out_grad, w_gate, w_up, w_down
-    )
-    whole = lambda w: w.reshape(MODEL_WIDTH, w.shape[-1])
-    weights = (w_q, w_k, w_v, w_o)
-    w_q, w_k, w_v, w_o = whole(w_q), whole(w_k), whole(w_v), whole(w_o)
-    small = small.transpose(1, 0, 2).reshape(16, MODEL_WIDTH)
-    gain_one, gain_two = small[0].astype(f32), small[1].astype(f32)
-    router = small[2:10].T
-    hidden = hidden_in.astype(f32)
-    h2, kept = attention_forward(
-        hidden, segment_ids[0], gain_one, w_q, w_k, w_v, w_o, gain_two
-    )
-    probs, chosen, total, gates = router_forward(h2, router, routes)
-    high = gates.astype(bf16)
-    low = (gates - high.astype(f32)).astype(bf16)
-    hg = jnp.concatenate([h2, high, low, jnp.zeros((ROWS, PAD - 16), bf16)], axis=1)
-    scale_one, h1, queries, keys, values, allowed, log_total, mixed, middle, scale_two = kept
     cosine, sine = tables(ROWS, HEAD_SIZE)
-    lanes = lambda v: jnp.pad(v, ((0, 0), (0, PAD - v.shape[1])))
     segments = segment_ids[0]
-    o_own, o_core, o_x, grads, d, sm, hidden_grad = layer_call(
-        hg,
-        g4.reshape(4 * ROWS, MODEL_WIDTH),
-        w0,
+    o_own, o_core, o_x, grads, d, sm, hidden_grad, middle = layer_call(
+        hidden_in,
+        out_grad,
+        w_query,
+        key_weight,
+        value_weight,
+        w_out,
+        small,
         w_gate,
         w_up,
         w_down,
-        middle,
-        hidden_in,
-        h1,
-        queries.reshape(ROWS, MODEL_WIDTH),
-        keys.reshape(ROWS, 256),
-        values.reshape(ROWS, 256),
-        mixed,
-        lanes(log_total.reshape(QUERY_HEADS, ROWS).T),
         cosine[:, 0, :],
         turn_table(sine),
-        jnp.pad(small[2:10], ((0, PAD - 8), (0, 0))),
-        lanes(routes),
-        gain_one[None],
-        gain_two[None],
+        jnp.pad(routes, ((0, 0), (0, PAD - TOPK))),
         jnp.broadcast_to(segments[:, None], (ROWS, PAD)),
         jnp.broadcast_to(segments[None, :], (8, ROWS)),
-        *weights,
     )
     add = lambda a, b, c: a.astype(f32) + b.astype(f32) + c.astype(f32)
     hidden_out = (middle + add(o_own, o_core, o_x)).astype(bf16)
     sm = lax.dynamic_index_in_dim(sm, lax.axis_index("shard"), 0, keepdims=False).astype(f32)
     d = d.astype(f32)
-    attn = (sm[0], d[:, 1536:3072], d[:, 3072:3328], d[:, 3328:], d[:, :1536], sm[1], sm[2:10].T)
+    attn = (sm[8], d[:, 1536:3072], d[:, 3072:3328], d[:, 3328:], d[:, :1536], sm[9], sm[:8].T)
     grads = [grads[m].astype(f32) for m in range(3)]
     return (hidden_out, hidden_grad, *attn, *grads)
 

time: 639 us -> 509 us (0.80)
  Pallas kernels: 532 us -> 446 us
  local copies, waits for them, and re-layouts: 36.5 us -> 15.2 us
  matrix products: 21 us -> 0 us
  other arithmetic: 45.5 us -> 37.3 us
    pallas_call x2 -> x1, Pallas kernels: 532 us -> 446 us  [layer_call(): pl.pallas_call(layer_kernel, out_shape=outputs, in_specs=[anyspace] * len...]
    dot_general x7 -> x0, matrix products: 21 us -> none  [the longest x1 7.16 us: attention_forward(): jnp.einsum('kgqs,skd->qkgd', probs, values, preferred_element_type=f32)]
    dot_general x3 -> x0, local copies, waits for them, and re-layouts: 8.71 us -> none  [the longest x1 6.62 us: attention_forward(): qr = jnp.dot(h1, w_q, preferred_element_type=f32)]
where the time goes in v4:
time: 509 us; the launch traced here: 500 us
  Pallas kernels  446 us (88%)
  other arithmetic  37.3 us (7%)
  local copies, waits for them, and re-layouts  15.2 us (3%)
    pallas_call x1, Pallas kernels, layer_call(): pl.pallas_call(layer_kernel, out_shape=outputs, in_specs=[anyspace] * len...  446 us
    convert_element_type x1, other arithmetic, local(): grads = [grads[m].astype(f32) for m in range(3)]  28.7 us

profile of v4, /device:TPU:0, one launch (start us, length us, event | category | flops | bytes accessed | tf_op | source)
XLA Modules:
  0.0 499.7 jit_solution(18159722639626515068)
XLA Ops:
  0.7 0.1 iota_multiply_fusion
  0.7 1.8 sine_multiply_fusion
  2.6 1.5 broadcast_in_dim.38.segc
  4.1 1.3 broadcast_in_dim.39.segr
  5.4 0.8 copy.26
  6.2 0.7 pad.4.routes
  7.0 0.7 broadcast_in_dim.32
  7.6 0.7 broadcast_in_dim.33
  8.3 0.1 pad.10.clone
  8.4 1.4 maximum_maximum_fusion.sm
  9.8 446.0 %layer.1 = (bf16[512,1536]{1,0:T(8,128)(2,1)}, bf16[512,1536]{1,0:T(8,128)(2,1)}, bf16[512,1536]{1,0:T(8,128)(2,1)}, bf16[3,8,768,768]{3,2,1,0:T(8,128)(2,1)}, b...) custom-call(bf16[512,1536]{1,0:T(8,128)(2,1)} %xin.1, ...), custom_call_target="tpu_custom_call" | custom-call | tf_op jit(solution)/shard_map/layer/pallas_call | solution.py:1281
  455.8 0.0 copy-start.1
  455.8 5.3 %add_convert_fusion = bf16[512,1536]{1,0:T(8,128)(2,1)} fusion(f32[512,1536]{1,0:T(8,128)} %get-tuple-element.20, bf16[512,1536]{1,0:T(8,128)(2,1)} %get-tuple-element.23, bf16[512,1536]{1,0:T(8,128)(2,1)} %get-tuple-element.22, bf16[512,1536]{1,0:T(8,128)(2,1)} %get-tuple-element.21), kind=kLoop, calls=%fused_computation.3 | loop fusion | flops 5505024 | bytes 9437184 | tf_op jit(solution)/shard_map/convert_element_type | solution.py:1440
  461.1 0.0 copy-done.1
  461.1 0.6 slice_reduce_fusion
  461.7 0.6 slice_bitcast_fusion
  462.3 0.0 slice-start
  462.3 0.0 slice-start.1
  462.3 28.7 %bitcast_convert_fusion = (f32[8,768,768]{2,1,0:T(8,128)}, f32[8,768,768]{2,1,0:T(8,128)}, f32[8,768,768]{2,1,0:T(8,128)}) fusion(bf16[3,8,768,768]{3,2,1,0:T(8,128)(2,1)} %get-tuple-element.27), kind=kLoop, calls=%fused_computation | loop fusion | flops 14155776 | bytes 84934656 | tf_op jit(solution)/shard_map/convert_element_type | solution.py:1444
  491.0 0.0 slice-done
  491.0 0.0 slice-done.1
  491.1 5.1 %fusion.1 = (f32[768,1536]{1,0:T(8,128)}, f32[768,1536]{1,0:T(8,128)}) fusion(bf16[768,3584]{1,0:T(8,128)(2,1)S(1)} %bitcast.16), kind=kLoop, calls=%fused_computation.15 | loop fusion | bytes 18874368 | tf_op jit(solution)/shard_map/slice | solution.py:1443
  496.1 0.0 copy-start
  496.1 1.3 fusion.2
  497.4 0.7 copy-done
  498.1 1.1 copy.28
  (5 shorter events, 0.0 us)
Async XLA Ops:
  455.8 5.3 %copy-start.1 = (bf16[2,16,768]{2,1,0:T(8,128)(2,1)S(1)}, bf16[2,16,768]{2,1,0:T(8,128)(2,1)}, u32[]{:S(2)}) copy-start(bf16[2,16,768]{2,1,0:T(8,128)(2,1)} %get-tuple-element.25) | copy-start | bytes 147460
  462.3 28.7 %slice-start = ((s8[5505024]{0:T(1024)(128)(4,1)}), s8[4194304]{0:T(1024)(128)(4,1)S(1)}, s32[]{:S(2)}) async-start(s8[5505024]{0:T(1024)(128)(4,1)} %bitcast.15), calls=%async_computation | async-start | bytes 8388608
  462.3 28.7 %slice-start.1 = ((s8[5505024]{0:T(1024)(128)(4,1)}), s8[1310720]{0:T(1024)(128)(4,1)S(1)}, s32[]{:S(2)}) async-start(s8[5505024]{0:T(1024)(128)(4,1)} %bitcast.15), calls=%async_computation.1 | async-start | bytes 2621440
  496.1 2.0 copy-start

commit v5 on v4

--- a/solution.py
+++ b/solution.py
@@ -2,6 +2,7 @@
 
 import jax
 import jax.numpy as jnp
+import numpy as np
 from jax import lax
 from jax.experimental import pallas as pl
 from jax.experimental.pallas import tpu as pltpu
@@ -104,9 +105,15 @@
     return lax.dot_general(a, b, (((0,), (0,)), ((), ())), preferred_element_type=f32)
 
 
-def turn_table(sine):
-    sign = jnp.where(jnp.arange(HEAD_SIZE) < HEAD_SIZE // 2, -1.0, 1.0)
-    return sine[:, 0, :] * sign[None, :]
+def turn_tables(length):
+    half = HEAD_SIZE // 2
+    exponent = np.float32(-2.0) * np.arange(half, dtype=np.float32) / np.float32(HEAD_SIZE)
+    frequency = np.float32(rope_base) ** exponent
+    angles = np.arange(length, dtype=np.float32)[:, None] * frequency[None, :]
+    cosine, sine = np.cos(angles), np.sin(angles)
+    cosine = np.concatenate([cosine, cosine], axis=1)
+    sine = np.concatenate([-sine, sine], axis=1)
+    return jnp.asarray(cosine, f32), jnp.asarray(sine, f32)
 
 
 def router_rows(h2, router_rows_t, routes):
@@ -184,7 +191,7 @@
 
         for n in range(0, 6, 3):
             lax.fori_loop(n, n + 3, head, 0)
-            tick()
+            tick(group * 6 + n + 3)
         dk = DK[group] * scale
         dk = dk * COS[...] - pltpu.roll(dk, 64, 1) * SIN[...]
         DQKV[:, pl.ds(1536 + group * HEAD_SIZE, HEAD_SIZE)] = dk.astype(bf16)
@@ -208,10 +215,11 @@
     lax.fori_loop(0, ROWS // 128, step, 0)
 
 
-def mask_bias(seg_column, seg_row, BIAS):
+def mask_bias(seg_row, BIAS):
     row = lax.broadcasted_iota(jnp.int32, (ROWS, ROWS), 0)
     column = lax.broadcasted_iota(jnp.int32, (ROWS, ROWS), 1)
-    same = seg_column[:, 0:1] == seg_row[0:1, :]
+    ids = seg_row[0:1, :].astype(f32)
+    same = jnp.transpose(jnp.broadcast_to(ids, (PAD, ROWS)))[:, 0:1] == ids
     BIAS[...] = jnp.where((column <= row) & same, 0.0, -1e30)
 
 
@@ -221,15 +229,15 @@
 QUARTER = 96
 SLACK = 3
 AT_ZL, AT_FL, AT_X = 1 + SLACK, 2 + 2 * SLACK, 3 + 3 * SLACK
-AT_CX, AT_CZ = AT_X + 16, AT_X + 20
+AT_CX, AT_CZ = AT_X + 8, AT_X + 12
 EXPERT_SLOTS = CHUNKS + AT_CZ + 1
-PART_SLOTS = PARTS + 25
+PART_SLOTS = PARTS + 18
 
 
 def layer_kernel(
-    xin, g, wq, wk, wv, wo, sm, wg, wu, wd, cos, sin, routes, segc, segr,
-    o_own, o_core, o_x, out, aout, smo, hgrad, y1,
-    h1, q, k, v, ob, lse, wqo, wko, wvo, woo, smf, gl,
+    xin, g, wq, wk, wv, wo, sm, wg, wu, wd, cos, sin, routes, segr,
+    hout, out, aout, smo, hgrad,
+    o_own, o_core, o_x, y1, h1, q, k, v, ob, lse, wqo, wko, wvo, woo, smf, gl,
     r_core, r_x, gr, ya, za, zb, d, ca, yb, xb, zc, zd, sa,
     H, W, DG, CR, CO, VA, VB, VS, VZ, VT, VF, FN, SM, SB, RT, G1, G2,
     fl_s, wa_s, wa_r, wx_s, wx_r, wc_s, wc_r, wd_s, wd_r, wz_s, wz_r, hx_s, hx_r, hc_s, hc_r,
@@ -255,29 +263,35 @@
     vm = pltpu.VMEM
     part = lambda *shape: vm(shape, bf16)
 
-    kinds = ((wk, wko), (wv, wvo), (wq, wqo), (wo, woo))
     piece = HALF // 4
-    mine = pl.ds((2 * x + c) * piece, piece)
-    theirs = pl.ds((2 * (1 - x) + c) * piece, piece)
-    wa = [remote(p[0].at[mine], p[1].at[mine], wa_s.at[n], wa_r.at[n], ydev) for n, p in enumerate(kinds)]
-    wa.append(remote(sm, smf, wa_s.at[4], wa_r.at[4], ydev))
-    wx = [remote(p[1].at[mine], p[1].at[mine], wx_s.at[n], wx_r.at[n], xdev) for n, p in enumerate(kinds)]
-    wc = [remote(p[1].at[mine], p[1].at[mine], wc_s.at[n], wc_r.at[n], cdev) for n, p in enumerate(kinds)]
-    wt = [
-        remote(p[1].at[theirs], p[1].at[theirs], wd_s.at[n], wd_r.at[n], cdev)
-        for n, p in enumerate(kinds)
-    ]
-    gx = remote(g, gl.at[1], wx_s.at[4], wx_r.at[4], xdev)
-    gc = remote(g, gl.at[0], wc_s.at[4], wc_r.at[4], cdev)
-    gt = remote(gl.at[1], gl.at[2], wd_s.at[4], wd_r.at[4], cdev)
+    own_piece, x_piece = (2 * x + c) * piece, (2 * (1 - x) + c) * piece
+    kinds = [(wk, wko, 0, piece), (wv, wvo, 0, piece)]
+    kinds += [(wq, wqo, n * 64, 64) for n in range(3)] + [(wo, woo, n * 64, 64) for n in range(3)]
+
+    def copies(from_input, begin, send, receive, device):
+        made = []
+        for n, (whole, landed, shift, count) in enumerate(kinds):
+            rows = pl.ds(pl.multiple_of(begin + shift, 64), count)
+            src = whole if from_input else landed
+            made.append(remote(src.at[rows], landed.at[rows], send.at[n], receive.at[n], device))
+        return made
+
+    wa = copies(True, own_piece, wa_s, wa_r, ydev)
+    wa.append(remote(sm, smf, wa_s.at[8], wa_r.at[8], ydev))
+    wx = copies(False, own_piece, wx_s, wx_r, xdev)
+    wc = copies(False, own_piece, wc_s, wc_r, cdev)
+    wt = copies(False, x_piece, wd_s, wd_r, cdev)
+    gx = remote(g, gl.at[1], wx_s.at[8], wx_r.at[8], xdev)
+    gc = remote(g, gl.at[0], wc_s.at[8], wc_r.at[8], cdev)
+    gt = remote(gl.at[1], gl.at[2], wd_s.at[8], wd_r.at[8], cdev)
 
     def wy(n):
         j, m = n // 3, n % 3
         return remote(
             shards[m].at[e0 + j, pl.ds(h * 384, 384)],
             W.at[j, m, pl.ds(y * HALF + h * 384, 384)],
-            wa_s.at[5 + n],
-            wa_r.at[5 + n],
+            wa_s.at[9 + n],
+            wa_r.at[9 + n],
             ydev,
         )
 
@@ -306,21 +320,21 @@
         src = H.at[pl.ds(2 * ROWS + b * 256, 256)]
         return remote(src, H.at[pl.ds(3 * ROWS + b * 256, 256)], hd_s.at[b], hd_r.at[b], cdev)
 
-    wa[4].start()
-    for n in range(4):
+    wa[8].start()
+    for n in range(8):
         wa[n].start()
     gc.start()
     for n in range(6):
         wy(n).start()
 
-    def front(X, H1, WQ, WKV, WO, Q, K, V, OB, BIAS, LSE, COS, SIN, RO, SC, SR, SF, Y1):
+    def front(X, H1, WQ, WKV, WO, Q, K, V, OB, BIAS, LSE, COS, SIN, RO, SR, SF, Y1):
         there = pl.ds(y * HALF, HALF)
         away = pl.ds((1 - y) * HALF, HALF)
         left, right = pl.ds(0, 256), pl.ds(256, 256)
         pairs = [
             (xin, X), (sm, SF.at[y]), (wk, WKV.at[there, left]), (wv, WKV.at[there, right]),
             (wq, WQ.at[there]), (wo, WO.at[there]), (cos, COS), (sin, SIN), (routes, RO),
-            (segc, SC), (segr, SR),
+            (segr, SR),
         ]
         loads = [local_copy(p[0], p[1], fl_s.at[n]) for n, p in enumerate(pairs)]
         for copy in loads:
@@ -334,7 +348,7 @@
             local_copy(woo, WO.at[away], fl_s.at[14]),
             local_copy(smf, SF.at[1 - y], fl_s.at[15]),
         ]
-        wa[4].wait_recv()
+        wa[8].wait_recv()
         late[4].start()
         for n in (0, 1):
             loads[n].wait()
@@ -356,20 +370,31 @@
             return 0
 
         lax.fori_loop(0, ROWS // 128, norm_step, 0)
-        for n in range(2, 11):
+        for n in range(2, 10):
             loads[n].wait()
-        mask_bias(SC, SR, BIAS)
-        for n in range(4):
+        mask_bias(SR, BIAS)
+        def onward(n):
             wa[n].wait_recv()
             wx[n].start()
             wc[n].start()
-        gx.start()
-        for n in range(3):
+
+        def across(n):
             wx[n].wait_recv()
             wt[n].start()
+
         for n in range(3):
+            onward(n)
+        for n in range(3):
+            across(n)
+            onward(n + 3)
+        for n in (3, 4):
+            across(n)
+            onward(n + 3)
+        gx.start()
+        for n in range(5):
             wc[n].wait_recv()
             wt[n].wait_recv()
+        for n in range(3):
             late[n].start()
         for n in range(3):
             late[n].wait()
@@ -392,8 +417,8 @@
             K[:, columns] = rotate(u).astype(bf16)
         V[...] = tile[:, 256:].astype(bf16)
         lax.fori_loop(0, 3, query_step, 0)
-        wx[3].wait_recv()
-        wt[3].start()
+        for n in (5, 6, 7):
+            across(n)
         pass_on(0)
         LSE[...] = jnp.zeros_like(LSE)
         scale = HEAD_SIZE ** (-0.5)
@@ -416,8 +441,9 @@
 
             lax.fori_loop(0, QUERY_HEADS, head, 0)
             if b == 0:
-                wc[3].wait_recv()
-                wt[3].wait_recv()
+                for n in (5, 6, 7):
+                    wc[n].wait_recv()
+                    wt[n].wait_recv()
                 late[3].start()
                 pass_on(1)
                 late[3].wait()
@@ -455,7 +481,7 @@
         part(MODEL_WIDTH, 512), part(MODEL_WIDTH, MODEL_WIDTH), part(ROWS, MODEL_WIDTH),
         part(ROWS, 256), part(ROWS, 256), part(ROWS, MODEL_WIDTH), vm((ROWS, ROWS), f32),
         vm((ROWS, PAD), f32), vm((ROWS, PAD), f32), vm((ROWS, PAD), f32),
-        vm((ROWS, PAD), jnp.int32), vm((ROWS, PAD), jnp.int32), vm((8, ROWS), jnp.int32),
+        vm((ROWS, TOPK), jnp.int32), vm((1, ROWS), jnp.int32),
         part(2, 16, HALF), vm((ROWS, MODEL_WIDTH), f32),
     )
 
@@ -564,7 +590,7 @@
         def _(n=n):
             load_f(n).wait()
             z2_copy(n).wait_send()
-            FN[n % 4] = (VT[n % 4].astype(f32) + VF[n % 2].astype(f32)).astype(bf16)
+            FN[n % 4] = VT[n % 4] + VF[n % 2]
             z3_copy(n).start()
             store_f(n).start()
 
@@ -580,7 +606,7 @@
         @when(n, mid)
         def _(n=n):
             load_z(n).wait()
-            VT[n % 4] = (VS[n % 4].astype(f32) + VZ[n % 2].astype(f32)).astype(bf16)
+            VT[n % 4] = VS[n % 4] + VZ[n % 2]
             z2_copy(n).start()
 
         n = s - AT_ZL
@@ -602,7 +628,7 @@
         def _(n=n):
             load_a(n).wait()
             load_b(n).wait()
-            VS[n % 4] = (VA[n % 2].astype(f32) + VB[n % 2].astype(f32)).astype(bf16)
+            VS[n % 4] = VA[n % 2] + VB[n % 2]
 
         @when(n, end)
         def _(n=n):
@@ -755,7 +781,6 @@
         for b in range(2):
             hx(b).wait_recv()
             hd(b).start()
-        pass_on(5)
         gt.wait_recv()
         gain_rows[3].start()
         for b in range(2):
@@ -763,6 +788,7 @@
         gain_rows[2].wait()
         gain_rows[3].wait()
         forward(0, 2 * ROWS)
+        pass_on(5)
         weight_grads(0)
         for n in range(3, 6):
             wz(n).wait_recv()
@@ -858,12 +884,12 @@
         for n in range(6):
             wy(n).wait_send()
             wz(n).wait_send()
-        for n in range(4):
+        for n in range(8):
             wa[n].wait_send()
             wx[n].wait_send()
             wc[n].wait_send()
             wt[n].wait_send()
-        wa[4].wait_send()
+        wa[8].wait_send()
         for copy in (gx, gc, gt):
             copy.wait_send()
         for b in range(2):
@@ -890,11 +916,11 @@
 
     def attention(
         Y1, DY, GB, XB, H1, OB, QB, KB, VV, DA, DOB, DQKV, BIAS, LSE, COS, SIN, RO,
-        SC, SR, DL, GS, DK, DV, STG,
+        SR, DL, GS, DK, DV, STG,
         AA, AB, PP, VY, QQ, VX, AS, AZ, AT, AF, AN,
     ):
         pairs = [
-            (segc, SC), (segr, SR), (y1, Y1), (g, GB), (routes, RO), (r_core, H.at[second]),
+            (segr, SR), (y1, Y1), (g, GB), (routes, RO), (r_core, H.at[second]),
             (ob, OB), (q, QB), (k, KB), (v, VV), (lse, LSE), (cos, COS), (sin, SIN), (h1, H1),
             (xin, XB),
         ]
@@ -914,10 +940,10 @@
                 copy.wait()
 
         slots(24, 26)
-        need(0, 2)
-        mask_bias(SC, SR, BIAS)
+        need(0, 1)
+        mask_bias(SR, BIAS)
         slots(26, 28)
-        need(2, 6)
+        need(1, 5)
         rx.wait_recv()
         last = local_copy(r_x, H.at[third], att.at[len(pairs)])
         last.start()
@@ -989,91 +1015,91 @@
             return pl.when(ok if cond is None else ok & cond)
 
         def aslot(s):
-            @awhen(s - 24)
-            def _():
-                axg_copy(s - 24).wait_recv()
-                ac2_copy(s - 24).start()
-
-            @awhen(s - 20, mid)
-            def _():
-                astore(s - 20).wait()
-                az3_copy(s - 20).wait_send()
-
-            @awhen(s - 20, end)
-            def _():
-                az3_copy(s - 20).wait_recv()
-
-            @awhen(s - 20)
-            def _():
-                axg_copy(s - 20).start()
-                ac1_copy(s - 20).start()
-
-            @awhen(s - 17, mid)
-            def _():
-                n = s - 17
+            @awhen(s - 17)
+            def _():
+                axg_copy(s - 17).wait_recv()
+                ac2_copy(s - 17).start()
+
+            @awhen(s - 15, mid)
+            def _():
+                astore(s - 15).wait()
+                az3_copy(s - 15).wait_send()
+
+            @awhen(s - 15, end)
+            def _():
+                az3_copy(s - 15).wait_recv()
+
+            @awhen(s - 15)
+            def _():
+                axg_copy(s - 15).start()
+                ac1_copy(s - 15).start()
+
+            @awhen(s - 13, mid)
+            def _():
+                n = s - 13
                 aload_f(n).wait()
                 az2_copy(n).wait_send()
-                AN[n % 4] = (AT[n % 4].astype(f32) + AF[n % 2].astype(f32)).astype(bf16)
+                AN[n % 4] = AT[n % 4] + AF[n % 2]
                 az3_copy(n).start()
                 astore(n).start()
 
-            @awhen(s - 16, mid)
-            def _():
-                az2_copy(s - 16).wait_recv()
-                aload_f(s - 16).start()
-
-            @awhen(s - 13, mid)
-            def _():
-                n = s - 13
+            @awhen(s - 12, mid)
+            def _():
+                az2_copy(s - 12).wait_recv()
+                aload_f(s - 12).start()
+
+            @awhen(s - 10, mid)
+            def _():
+                n = s - 10
                 aload_z(n).wait()
-                AT[n % 4] = (AS[n % 8].astype(f32) + AZ[n % 2].astype(f32)).astype(bf16)
+                AT[n % 4] = AS[n % 8] + AZ[n % 2]
                 az2_copy(n).start()
 
-            @awhen(s - 13, end)
-            def _():
-                az1_copy(s - 13).wait_send()
-
-            @awhen(s - 12, mid)
-            def _():
-                az1_copy(s - 12).wait_recv()
-                aload_z(s - 12).start()
-
-            @awhen(s - 9)
-            def _():
-                n = s - 9
+            @awhen(s - 10, end)
+            def _():
+                az1_copy(s - 10).wait_send()
+
+            @awhen(s - 9, mid)
+            def _():
+                az1_copy(s - 9).wait_recv()
+                aload_z(s - 9).start()
+
+            @awhen(s - 7)
+            def _():
+                n = s - 7
                 aload_x(n).wait()
                 ax_copy(n).wait_send()
                 mine = pl.ds(pl.multiple_of(x * QUARTER, 16), QUARTER)
-                AS[n % 8] = (QQ[n % 4, mine, :].astype(f32) + VX[n % 2].astype(f32)).astype(bf16)
-
-            @awhen(s - 9, end)
-            def _():
-                az1_copy(s - 9).start()
-
-            @awhen(s - 8)
-            def _():
-                ax_copy(s - 8).wait_recv()
-                aload_x(s - 8).start()
-
-            @awhen(s - 5)
-            def _():
-                n = s - 5
+                AS[n % 8] = QQ[n % 4, mine, :] + VX[n % 2]
+
+            @awhen(s - 7, end)
+            def _():
+                az1_copy(s - 7).start()
+
+            @awhen(s - 6)
+            def _():
+                ax_copy(s - 6).wait_recv()
+                aload_x(s - 6).start()
+
+            @awhen(s - 4)
+            def _():
+                n = s - 4
                 aload_y(n).wait()
                 ay_copy(n).wait_send()
-                QQ[n % 4] = (PP[n % 4, y].astype(f32) + VY[n % 2].astype(f32)).astype(bf16)
+                QQ[n % 4] = PP[n % 4, y] + VY[n % 2]
                 ax_copy(n).start()
 
-            @awhen(s - 4)
-            def _():
-                ay_copy(s - 4).wait_recv()
-                aload_y(s - 4).start()
+            @awhen(s - 3)
+            def _():
+                ay_copy(s - 3).wait_recv()
+                aload_y(s - 3).start()
 
             @awhen(s - 1)
             def _():
                 n = s - 1
                 aload_a(n).wait()
                 aload_b(n).wait()
-                PP[n % 4] = (AA[n % 2].astype(f32) + AB[n % 2].astype(f32)).astype(bf16)
+                PP[n % 4] = AA[n % 2] + AB[n % 2]
                 ay_copy(n).start()
 
             @awhen(s)
@@ -1115,9 +1141,9 @@
             slot(28 + b)
             return 0
 
-        need(6, 7)
+        need(5, 6)
         lax.fori_loop(0, 3, out_block, 0)
-        need(15, 19)
+        need(14, 18)
 
         def dob_tile(t, _):
             ns = pl.ds(pl.multiple_of(t * 512, 512), 512)
@@ -1127,35 +1153,43 @@
             return 0
 
         lax.fori_loop(0, 3, dob_tile, 0)
-        need(7, 13)
+        need(6, 12)
         state = [34, 0]
 
-        def tick():
+        def run(slots_now, parts_now):
             first_slot, first_part = state
 
-            def step(n, _):
+            def slot_step(n, _):
                 slot(first_slot + n)
                 return 0
 
-            lax.fori_loop(0, 2, step, 0)
-            if first_part < 6:
-                lax.fori_loop(0, 2, lambda n, _: (aslot(first_part + n), 0)[1], 0)
-            state[0] += 2
-            state[1] = min(state[1] + 2, 6)
+            def part_step(n, _):
+                aslot(first_part + n)
+                return 0
+
+            lax.fori_loop(0, slots_now, slot_step, 0)
+            lax.fori_loop(0, parts_now, part_step, 0)
+            state[0] += slots_now
+            state[1] += parts_now
+
+        def emit_query(b):
+            emit(3 + b, H1, DQKV[:, pl.ds(b * WIDTH, WIDTH)])
+
+        def tick(heads):
+            if heads == 6:
+                need(12, 13)
+                emit_query(0)
+            if heads == 9:
+                emit_query(1)
+            run(2, 2)
 
         heads_backward(QB, KB, VV, DOB, BIAS, LSE, COS, SIN, DQKV, DK, DV, tick)
+        for b in (2, 3):
+            emit_query(b)
+            run(2, 2)
+        need(13, 14)
+        need(18, 26)
         done, parts_done = state
-
-        def qkv_block(b, _):
-            emit(3 + b, H1, DQKV[:, pl.ds(pl.multiple_of(b * WIDTH, WIDTH), WIDTH)])
-            slot(done + b)
-            return 0
-
-        need(13, 14)
-        lax.fori_loop(0, 4, qkv_block, 0)
-        need(14, 15)
-        need(19, 27)
-        done += 4
 
         def dh1_tile(t, _):
             ns = pl.ds(pl.multiple_of(t * 512, 512), 512)
@@ -1188,16 +1222,45 @@
         small = local_copy(SM, smo, sl.at[1])
         small.start()
 
-        last_slot = max(EXPERT_SLOTS - done, PART_SLOTS - parts_done)
-
-        def drain(n, _):
+        sums = [
+            local_copy(p[0], p[1], att.at[n])
+            for n, p in enumerate(((y1, Y1), (o_own, OB), (o_core, QB), (o_x, H1)))
+        ]
+        for copy in sums[:3]:
+            copy.start()
+
+        def first_drain(n, _):
             slot(done + n)
             aslot(parts_done + n)
             return 0
 
+        lax.fori_loop(0, 8, first_drain, 0)
+        done_now, parts_now = done + 8, parts_done + 8
+        ox.wait()
+        sums[3].start()
+        for copy in sums:
+            copy.wait()
+
+        def sum_step(b, _):
+            rows = pl.ds(pl.multiple_of(b * 128, 128), 128)
+            total = OB[rows, :].astype(f32) + QB[rows, :].astype(f32) + H1[rows, :].astype(f32)
+            DOB[rows, :] = (Y1[rows, :] + total).astype(bf16)
+            return 0
+
+        lax.fori_loop(0, ROWS // 128, sum_step, 0)
+        forward_out = local_copy(DOB, hout, att.at[4])
+        forward_out.start()
+        last_slot = max(EXPERT_SLOTS - done_now, PART_SLOTS - parts_now)
+
+        def drain(n, _):
+            slot(done_now + n)
+            aslot(parts_now + n)
+            return 0
+
         lax.fori_loop(0, last_slot, drain, 0)
         small.wait()
         result.wait()
+        forward_out.wait()
 
         def finish_part(n, _):
             ac_copy(n).wait_send()
@@ -1215,7 +1278,7 @@
         part(ROWS, MODEL_WIDTH), part(ROWS, MODEL_WIDTH), part(ROWS, 256), part(ROWS, 256),
         part(ROWS, MODEL_WIDTH), part(ROWS, MODEL_WIDTH), part(ROWS, 2048),
         vm((ROWS, ROWS), f32), vm((ROWS, PAD), f32), vm((ROWS, PAD), f32), vm((ROWS, PAD), f32),
-        vm((ROWS, PAD), jnp.int32), vm((ROWS, PAD), jnp.int32), vm((8, ROWS), jnp.int32),
+        vm((ROWS, TOPK), jnp.int32), vm((1, ROWS), jnp.int32),
         part(ROWS, PAD), vm((1, MODEL_WIDTH), f32), vm((2, ROWS, PAD), f32),
         vm((2, ROWS, PAD), f32), part(2, HALF, WIDTH),
         part(2, 2, 192, WIDTH), part(2, 2, 192, WIDTH), part(4, 2, 192, WIDTH),
@@ -1223,7 +1286,6 @@
         part(2, QUARTER, WIDTH), part(4, QUARTER, WIDTH), part(2, QUARTER, WIDTH),
         part(4, QUARTER, WIDTH),
     )
-    ox.wait()
 
     def finish(n, _):
         @pl.when(crosses(n))
@@ -1248,9 +1310,8 @@
     vmem = lambda *s: pltpu.VMEM(s, bf16)
     n = PARTS
     wide, narrow = (ROWS, MODEL_WIDTH), (ROWS, 256)
-    shapes = [wide] * 3
-    shapes += [(3, 8, HALF, FF), (HALF, BLOCKS * WIDTH), (2, 16, HALF), wide]
-    shapes += [(*wide, f32), wide, wide, narrow, narrow, wide, (ROWS, PAD, f32)]
+    shapes = [wide, (3, 8, HALF, FF), (HALF, BLOCKS * WIDTH), (2, 16, HALF), wide]
+    shapes += [wide] * 3 + [(*wide, f32), wide, wide, narrow, narrow, wide, (ROWS, PAD, f32)]
     shapes += [(HALF, MODEL_WIDTH), (HALF, 256), (HALF, 256), (HALF, MODEL_WIDTH), (16, HALF)]
     shapes += [(3, ROWS, MODEL_WIDTH)]
     shapes += [(ROWS, WIDE)] * 2 + [(2, 3, MODEL_WIDTH, FF)] + [(CHUNKS, CHUNK, FF)] * 3
@@ -1267,8 +1328,8 @@
         vmem(2, CHUNK, FF), vmem(4, CHUNK, FF), vmem(2, CHUNK, FF), vmem(4, CHUNK, FF),
         vmem(2, 16, HALF), vmem(2, 16, HALF), vmem(PAD, MODEL_WIDTH),
         pltpu.VMEM((1, MODEL_WIDTH), f32), pltpu.VMEM((1, MODEL_WIDTH), f32),
-        dma((16,)), dma((11,)), dma((11,)), dma((5,)), dma((5,)), dma((5,)), dma((5,)), dma((5,)),
-        dma((5,)), dma((6,)), dma((6,)), dma((2,)), dma((2,)), dma((2,)), dma((2,)), dma((2,)),
+        dma((16,)), dma((15,)), dma((15,)), dma((9,)), dma((9,)), dma((9,)), dma((9,)), dma((9,)),
+        dma((9,)), dma((6,)), dma((6,)), dma((2,)), dma((2,)), dma((2,)), dma((2,)), dma((2,)),
         dma((2,)), dma((6,)), dma((7,)),
         dma((4,)), dma((2,)), many, many, dma((2,)), dma((2,)),
         many, many, dma((2,)), many, many, dma((2,)),
@@ -1288,7 +1349,7 @@
             collective_id=2, has_side_effects=True, vmem_limit_bytes=67 * 1000 * 1000
         ),
         name="layer",
-    )(*arrays)[:8]
+    )(*arrays)[:5]
 
 
 def attention_forward(hidden, segments, gain_one, w_q, w_k, w_v, w_o, gain_two):
@@ -1417,9 +1478,8 @@
     small = jnp.concatenate(
         [w_router.T, norm1_gain[None], norm2_gain[None], jnp.zeros((6, HALF), bf16)], axis=0
     )
-    cosine, sine = tables(ROWS, HEAD_SIZE)
-    segments = segment_ids[0]
-    o_own, o_core, o_x, grads, d, sm, hidden_grad, middle = layer_call(
+    cosine, sine = turn_tables(ROWS)
+    hidden_out, grads, d, sm, hidden_grad = layer_call(
         hidden_in,
         out_grad,
         w_query,
@@ -1430,14 +1490,11 @@
         w_gate,
         w_up,
         w_down,
-        cosine[:, 0, :],
-        turn_table(sine),
-        jnp.pad(routes, ((0, 0), (0, PAD - TOPK))),
-        jnp.broadcast_to(segments[:, None], (ROWS, PAD)),
-        jnp.broadcast_to(segments[None, :], (8, ROWS)),
+        cosine,
+        sine,
+        routes,
+        segment_ids,
     )
-    add = lambda a, b, c: a.astype(f32) + b.astype(f32) + c.astype(f32)
-    hidden_out = (middle + add(o_own, o_core, o_x)).astype(bf16)
     sm = lax.dynamic_index_in_dim(sm, lax.axis_index("shard"), 0, keepdims=False).astype(f32)
     d = d.astype(f32)
     attn = (sm[8], d[:, 1536:3072], d[:, 3072:3328], d[:, 3328:], d[:, :1536], sm[9], sm[:8].T)

time: 509 us -> 499 us (0.980)
  other arithmetic: 37.3 us -> 30.5 us
    convert_element_type x1 -> x0, other arithmetic: 5.26 us -> none  [local(): hidden_out = (middle + add(o_own, o_core, o_x)).astype(bf16)]
where the time goes in v5:
time: 499 us; the launch traced here: 491 us
  Pallas kernels  443 us (89%)
  other arithmetic  30.5 us (6%)
  local copies, waits for them, and re-layouts  16.3 us (3%)
    pallas_call x1, Pallas kernels, layer_call(): pl.pallas_call(layer_kernel, out_shape=outputs, in_specs=[anyspace] * len...  443 us
    convert_element_type x1, other arithmetic, local(): grads = [grads[m].astype(f32) for m in range(3)]  28.4 us

profile of v5, /device:TPU:0, one launch (start us, length us, event | category | flops | bytes accessed | tf_op | source)
XLA Modules:
  0.0 490.8 jit_solution(1182915700581239311)
XLA Ops:
  0.6 0.7 broadcast_in_dim.10
  1.3 0.7 broadcast_in_dim.9
  2.0 0.1 pad.3.clone
  2.1 1.4 maximum_maximum_fusion.sm
  3.5 1.5 copy.28.routes
  5.0 442.8 %layer.1 = (bf16[512,1536]{1,0:T(8,128)(2,1)}, bf16[3,8,768,768]{3,2,1,0:T(8,128)(2,1)}, bf16[768,3584]{1,0:T(8,128)(2,1)}, bf16[2,16,768]{2,1,0:T(8,128)(2,1)},...) custom-call(bf16[512,1536]{1,0:T(8,128)(2,1)} %xin.1, ...), custom_call_target="tpu_custom_call" | custom-call | tf_op jit(solution)/shard_map/layer/pallas_call | solution.py:1342
  447.9 0.7 dynamic-slice_convert_fusion
  448.6 0.6 slice_reduce_fusion
  449.2 7.5 %fusion = (f32[768,1536]{1,0:T(8,128)}, f32[768,1536]{1,0:T(8,128)}) fusion(bf16[768,3584]{1,0:T(8,128)(2,1)} %get-tuple-element.20), kind=kLoop, calls=%fused_computation.8 | loop fusion | bytes 18874368 | tf_op jit(solution)/shard_map/slice | solution.py:1500
  456.7 2.4 fusion.1
  459.1 0.6 slice_bitcast_fusion
  459.7 0.0 copy-start.1
  459.7 0.0 copy-start
  459.7 28.4 %bitcast_convert_fusion = (f32[8,768,768]{2,1,0:T(8,128)}, f32[8,768,768]{2,1,0:T(8,128)}, f32[8,768,768]{2,1,0:T(8,128)}) fusion(bf16[3,8,768,768]{3,2,1,0:T(8,128)(2,1)} %get-tuple-element.21), kind=kLoop, calls=%fused_computation | loop fusion | flops 14155776 | bytes 84934656 | tf_op jit(solution)/shard_map/convert_element_type | solution.py:1501
  488.1 0.0 copy-done.1
  488.1 1.1 copy.31
  489.2 0.0 copy-done
  489.2 1.1 copy.32
  (1 shorter events, 0.0 us)
Async XLA Ops:
  459.7 28.4 %copy-start.1 = (bf16[512,1536]{1,0:T(8,128)(2,1)S(1)}, bf16[512,1536]{1,0:T(8,128)(2,1)}, u32[]{:S(2)}) copy-start(bf16[512,1536]{1,0:T(8,128)(2,1)} %get-tuple-element.43) | copy-start | bytes 4718596
  459.7 29.6 %copy-start = (bf16[512,1536]{1,0:T(8,128)(2,1)S(1)}, bf16[512,1536]{1,0:T(8,128)(2,1)}, u32[]{:S(2)}) copy-start(bf16[512,1536]{1,0:T(8,128)(2,1)} %get-tuple-element.44) | copy-start | bytes 4718596

commit v6 on v5

--- a/solution.py
+++ b/solution.py
@@ -227,7 +227,7 @@
 PARTS = 2 * BLOCKS
 WIDTH = 512
 QUARTER = 96
-SLACK = 3
+SLACK = 2
 AT_ZL, AT_FL, AT_X = 1 + SLACK, 2 + 2 * SLACK, 3 + 3 * SLACK
 AT_CX, AT_CZ = AT_X + 8, AT_X + 12
 EXPERT_SLOTS = CHUNKS + AT_CZ + 1

time: 499 us -> 500 us (level)
  no operation moved by 1% of the time
where the time goes in v6:
time: 500 us; the launch traced here: 491 us
  Pallas kernels  443 us (89%)
  other arithmetic  30.5 us (6%)
  local copies, waits for them, and re-layouts  16.3 us (3%)
    pallas_call x1, Pallas kernels, layer_call(): pl.pallas_call(layer_kernel, out_shape=outputs, in_specs=[anyspace] * len...  443 us
    convert_element_type x1, other arithmetic, local(): grads = [grads[m].astype(f32) for m in range(3)]  28.4 us

profile of v6, /device:TPU:0, one launch (start us, length us, event | category | flops | bytes accessed | tf_op | source)
XLA Modules:
  0.0 491.5 jit_solution(5853644596087346551)
XLA Ops:
  0.6 0.7 broadcast_in_dim.10
  1.3 0.7 broadcast_in_dim.9
  2.0 0.1 pad.3.clone
  2.1 1.4 maximum_maximum_fusion.sm
  3.5 1.5 copy.28.routes
  5.0 443.5 %layer.1 = (bf16[512,1536]{1,0:T(8,128)(2,1)}, bf16[3,8,768,768]{3,2,1,0:T(8,128)(2,1)}, bf16[768,3584]{1,0:T(8,128)(2,1)}, bf16[2,16,768]{2,1,0:T(8,128)(2,1)},...) custom-call(bf16[512,1536]{1,0:T(8,128)(2,1)} %xin.1, ...), custom_call_target="tpu_custom_call" | custom-call | tf_op jit(solution)/shard_map/layer/pallas_call | solution.py:1342
  448.5 0.7 dynamic-slice_convert_fusion
  449.3 0.6 slice_reduce_fusion
  449.9 7.5 %fusion = (f32[768,1536]{1,0:T(8,128)}, f32[768,1536]{1,0:T(8,128)}) fusion(bf16[768,3584]{1,0:T(8,128)(2,1)} %get-tuple-element.20), kind=kLoop, calls=%fused_computation.8 | loop fusion | bytes 18874368 | tf_op jit(solution)/shard_map/slice | solution.py:1500
  457.4 2.4 fusion.1
  459.7 0.6 slice_bitcast_fusion
  460.3 0.0 copy-start.1
  460.3 0.0 copy-start
  460.3 28.4 %bitcast_convert_fusion = (f32[8,768,768]{2,1,0:T(8,128)}, f32[8,768,768]{2,1,0:T(8,128)}, f32[8,768,768]{2,1,0:T(8,128)}) fusion(bf16[3,8,768,768]{3,2,1,0:T(8,128)(2,1)} %get-tuple-element.21), kind=kLoop, calls=%fused_computation | loop fusion | flops 14155776 | bytes 84934656 | tf_op jit(solution)/shard_map/convert_element_type | solution.py:1501
  488.8 0.0 copy-done.1
  488.8 1.1 copy.31
  489.9 0.0 copy-done
  489.9 1.1 copy.32
  (1 shorter events, 0.0 us)
Async XLA Ops:
  460.3 28.4 %copy-start.1 = (bf16[512,1536]{1,0:T(8,128)(2,1)S(1)}, bf16[512,1536]{1,0:T(8,128)(2,1)}, u32[]{:S(2)}) copy-start(bf16[512,1536]{1,0:T(8,128)(2,1)} %get-tuple-element.43) | copy-start | bytes 4718596
  460.3 29.6 %copy-start = (bf16[512,1536]{1,0:T(8,128)(2,1)S(1)}, bf16[512,1536]{1,0:T(8,128)(2,1)}, u32[]{:S(2)}) copy-start(bf16[512,1536]{1,0:T(8,128)(2,1)} %get-tuple-element.44) | copy-start | bytes 4718596
